TPU v7x, 512 devices: a whole 4x8x8 slice. The times are simulated.
512 devices in a mesh: rep: 16 (over z, core), fsdp: 32 (over y, x).
Axes of the slice: x: 4, y: 8, z: 8, core: 2. Of those that a mesh axis runs over, the one named last changes fastest.
Arguments:
- grad: bfloat16 [16, 4096, 3072], P('rep', 'fsdp'), may hold values from -50 to 50
- momentum: bfloat16 [16, 4096, 3072], P('rep', 'fsdp'), may hold values from -6 to 6
- kept_index: int32 [16, 64, 1536], P('rep', 'fsdp'), may hold values from 0 to 4095, as said below
- weights: bfloat16 [4096, 3072], P('fsdp'), may hold values from -3 to 3
Outputs:
- new_momentum: bfloat16 [16, 4096, 3072], P('rep', 'fsdp')
- new_weights: bfloat16 [4096, 3072], P('fsdp')
Inputs may be any that keep to these rules, and one draw needn't show every extreme that they name: `kept_index`: the 32 positions of a group are distinct: the j-th lies among positions j * 128 to (j + 1) * 128 - 1.
All inputs are finite; a program needn't handle non-finite values.
Results may differ from a plain program's by a relative error of at most 0.001.
Values sent between devices are 32-bit elements; how exact they have to be, the bound alone decides.
No kernel may reach another device: no remote copies, remote signals or barrier semaphores. Data moves between devices by JAX's collectives and lax.ppermute only.
A program may use at most 64 MiB of HBM per device.

v0:
```python
import jax
import jax.numpy as jnp
from jax import lax
from jax.sharding import PartitionSpec as P

clip_rms = 0.5
momentum_decay = 0.9
step_rate = 0.5


def dct_table():
    frequency = jnp.arange(64, dtype=jnp.float32)[:, None]
    position = jnp.arange(64, dtype=jnp.float32)[None, :]
    weight = jnp.where(frequency == 0, jnp.sqrt(1.0 / 64.0), jnp.sqrt(2.0 / 64.0))
    return weight * jnp.cos(jnp.pi * (2.0 * position + 1.0) * frequency / 128.0)


def lists_to_tiles(kept_values, kept_where, dct_rows):
    high = lax.Precision.HIGHEST
    levels = jnp.arange(64, dtype=jnp.int32)
    high_hot = ((kept_where // 64)[..., None] == levels).astype(jnp.float32)
    low_hot = ((kept_where % 64)[..., None] == levels).astype(jnp.float32) * kept_values[..., None]
    sparse_sum = jnp.einsum("cnu,cnv->cuv", high_hot, low_hot, precision=high)
    row_pass = jnp.einsum("ux,cuv->cxv", dct_rows, sparse_sum, precision=high)
    tile_sum = jnp.einsum("cxv,vy->xcy", row_pass, dct_rows, precision=high)
    return tile_sum.reshape(64, -1)


def body(grad, momentum, kept_index, weights):
    dct_rows = dct_table()
    high = lax.Precision.HIGHEST
    row_count = grad.shape[1]
    col_count = grad.shape[2]
    block_rows = row_count // 64
    block_cols = col_count // 64
    per_group = kept_index.shape[2] // block_cols
    gradient = grad[0].astype(jnp.float32)
    square_sum = lax.psum(jnp.sum(gradient * gradient), "fsdp")
    mean_square = square_sum / (row_count * lax.axis_size("fsdp") * col_count)
    factor = jnp.minimum(1.0, clip_rms / jnp.sqrt(mean_square + 1e-06))
    blended = momentum_decay * momentum[0].astype(jnp.float32) + factor * gradient
    pair_table = jnp.kron(jnp.eye(2, dtype=jnp.float32), dct_rows)
    row_pass = jnp.einsum(
        "ux,rxc->ruc", dct_rows, blended.reshape(block_rows, 64, col_count), precision=high
    )
    coeffs = jnp.einsum(
        "ruhy,vy->ruhv",
        row_pass.reshape(block_rows, 64, col_count // 128, 128),
        pair_table,
        precision=high,
    )
    coeffs = (
        coeffs.reshape(block_rows, 64, block_cols, 64)
        .transpose(0, 2, 1, 3)
        .reshape(block_rows, block_cols, 4096)
    )
    kept_where = kept_index[0].reshape(block_rows, block_cols, per_group)
    kept_values = jnp.take_along_axis(coeffs, kept_where, axis=2)

    def decode_block(packed):
        return lists_to_tiles(packed[0], packed[1], dct_rows)

    own_terms = lax.map(decode_block, (kept_values, kept_where)).reshape(row_count, col_count)
    new_momentum = (blended - own_terms).astype(jnp.bfloat16)[None]
    all_values, all_where = (
        lax.all_gather(
            kept_values.reshape(1, block_rows, block_cols * per_group), "rep", axis=0, tiled=True
        ),
        lax.all_gather(kept_index, "rep", axis=0, tiled=True),
    )
    replicas = all_values.shape[0]

    def arrange(listing):
        listing = listing.reshape(replicas, block_rows, block_cols, per_group).transpose(1, 2, 0, 3)
        return listing.reshape(block_rows, block_cols, replicas * per_group)

    summed = lax.map(decode_block, (arrange(all_values), arrange(all_where))).reshape(
        row_count, col_count
    )
    new_weights = (weights.astype(jnp.float32) - step_rate * summed).astype(jnp.bfloat16)
    return (new_momentum, new_weights)


def solution(mesh):
    in_specs = (
        P("rep", "fsdp", None),
        P("rep", "fsdp", None),
        P("rep", "fsdp", None),
        P("fsdp", None),
    )
    out_specs = (P("rep", "fsdp", None), P("fsdp", None))
    return jax.shard_map(body, mesh=mesh, in_specs=in_specs, out_specs=out_specs, check_vma=False)
```

profile of v0, /device:TPU:1, one launch (start us, length us, event | category | flops | bytes accessed | tf_op | source)
XLA Modules:
  0.0 215.2 jit_solution(13129487410980900815)
XLA Ops:
  0.6 2.1 fusion.56
  2.8 62.5 %psum.7 = f32[]{:T(128)} all-reduce(f32[]{:T(128)} %fusion.56), channel_id=1, replica_groups=mesh['rep'=16,'fsdp'=32] {'fsdp'}, use_global_device_ids=true, to_apply=%region_1.2 | all-reduce | flops 1 | bytes 8 | tf_op jit(solution)/shard_map/psum | solution.py:38
  66.0 1.6 fusion.57
  67.7 1.6 fusion.66
  69.3 0.3 copy.31
  70.0 2.6 %fusion.58 = f32[2,64,24,128]{3,2,1,0:T(8,128)} fusion(f32[128,128,1,1]{1,0,2,3:T(8,128)S(1)} %reshape.280, f32[2,64,24,128]{3,2,1,0:T(8,128)S(1)} %bitcast.157), kind=kOutput, calls=%fused_computation.80 | convolution fusion | flops 603979776 | bytes 3211264 | tf_op jit(solution)/shard_map/ruhy,vy->ruhv/dot_general | solution.py:46
  72.6 2.4 %reshape.263 = f32[2,64,48,64]{3,2,1,0:T(8,128)S(1)} reshape(f32[2,64,24,128]{3,2,1,0:T(8,128)} %fusion.58) | data formatting | bytes 3145728 | tf_op jit(solution)/shard_map/reshape | solution.py:53
  75.0 2.6 %copy.33 = f32[2,64,48,64]{3,1,2,0:T(8,128)} copy(f32[2,64,48,64]{3,2,1,0:T(8,128)S(1)} %reshape.263) | data formatting | bytes 3145728 | tf_op jit(solution)/shard_map/reshape | solution.py:53
  77.6 2.4 %reshape.264 = f32[2,48,4096]{2,1,0:T(8,128)S(1)} reshape(f32[2,48,64,64]{3,2,1,0:T(8,128)} %bitcast.156) | data formatting | bytes 3145728 | tf_op jit(solution)/shard_map/reshape | solution.py:55
  80.2 30.6 %gather_fusion = f32[3072]{0:T(1024)S(1)} fusion(f32[2,48,4096]{2,1,0:T(8,128)S(1)} %reshape.264, s32[3072]{0:T(1024)S(1)} %reshape.270), kind=kCustom, calls=%fused_computation | custom fusion | bytes 61440 | tf_op jit(solution)/shard_map/jit(take_along_axis)/gather | solution.py:58
  111.0 1.3 broadcast.289.clone
  112.4 18.7 %while.28 = (s32[]{:T(128)}, f32[2,64,3072]{2,1,0:T(8,128)}, s32[2,48,32]{2,1,0:T(8,128)S(1)}, f32[2,48,32]{2,1,0:T(8,128)S(1)}, f32[64]{0:T(128)S(1)}, /*index=5*/f32[64]{0:T(128)S(1)}, s32[]{:T(128)}) while((s32[]{:T(128)}, f32[2,64,3072]{2,1,0:T(8,128)}, s32[2,48,32]{2,1,0:T(8,128)S(1)}, f32[2,48,32]{2,1,0:T(8,128)S(1)}, ...), condition=%wide.region_3.4_spmd.clone.clone, body=%wide.region_2.3_spmd.clone.clone.sunk | while | flops 377845248 | bytes 8710745 | solution.py:63
  112.4 2.8 %fusion.93 = f32[48,64,64]{1,2,0:T(8,128)S(1)} fusion(f32[48,32]{1,0:T(8,128)S(1)} %dynamic-slice_bitcast_fusion.4, s32[48,32]{1,0:T(8,128)S(1)} %add_select_fusion.9, s32[48,32]{1,0:T(8,128)S(1)} %get-tuple-element.309), kind=kOutput, calls=%fused_computation.6.clone.1 | convolution fusion | flops 75792384 | bytes 804864 | tf_op jit(solution)/shard_map/while/body/eval_jaxpr/cnu,cnv->cuv/dot_general | solution.py:23
  115.2 1.5 fusion.94
  116.7 2.6 %fusion.95 = f32[64,48,64]{2,0,1:T(8,128)S(1)} fusion(f32[48,64,64]{2,1,0:T(8,128)S(1)} %fusion.94, f32[64]{0:T(128)S(1)} %get-tuple-element.336, f32[64]{0:T(128)S(1)} %get-tuple-element.337), kind=kOutput, calls=%fused_computation.5.clone.1 | convolution fusion | flops 151007232 | bytes 1573376 | tf_op jit(solution)/shard_map/while/body/eval_jaxpr/cxv,vy->xcy/dot_general | solution.py:25
  119.4 0.9 copy.36
  120.3 0.4 broadcast_in_dim.58
  120.7 1.0 constant_dynamic-update-slice_fusion.4
  121.7 2.8 %fusion.93 = f32[48,64,64]{1,2,0:T(8,128)S(1)} fusion(f32[48,32]{1,0:T(8,128)S(1)} %dynamic-slice_bitcast_fusion.4, s32[48,32]{1,0:T(8,128)S(1)} %add_select_fusion.9, s32[48,32]{1,0:T(8,128)S(1)} %get-tuple-element.309), kind=kOutput, calls=%fused_computation.6.clone.1 | convolution fusion | flops 75792384 | bytes 804864 | tf_op jit(solution)/shard_map/while/body/eval_jaxpr/cnu,cnv->cuv/dot_general | solution.py:23
  124.5 1.5 fusion.94
  126.0 2.6 %fusion.95 = f32[64,48,64]{2,0,1:T(8,128)S(1)} fusion(f32[48,64,64]{2,1,0:T(8,128)S(1)} %fusion.94, f32[64]{0:T(128)S(1)} %get-tuple-element.336, f32[64]{0:T(128)S(1)} %get-tuple-element.337), kind=kOutput, calls=%fused_computation.5.clone.1 | convolution fusion | flops 151007232 | bytes 1573376 | tf_op jit(solution)/shard_map/while/body/eval_jaxpr/cxv,vy->xcy/dot_general | solution.py:25
  128.7 0.9 copy.36
  129.6 0.4 broadcast_in_dim.58
  130.0 1.0 constant_dynamic-update-slice_fusion.4
  131.0 2.9 %fusion.61 = bf16[1,128,3072]{2,1,0:T(8,128)(2,1)} fusion(f32[1,128,3072]{2,1,0:T(8,128)} %copy-done, f32[1,128,3072]{2,1,0:T(8,128)} %bitcast.159), kind=kLoop, calls=%fused_computation.85 | loop fusion | flops 786432 | bytes 3932160 | tf_op jit(solution)/shard_map/convert_element_type | solution.py:64
  134.0 38.4 %all_gather.7 = f32[16,2,1536]{2,1,0:T(2,128)S(1)} all-gather(f32[1,2,1536]{2,1,0:T(2,128)S(1)} %and_select_fusion.1), channel_id=1, replica_groups=mesh['rep'=16,'fsdp'=32] {'rep'}, dimensions={0}, use_global_device_ids=true | all-gather | bytes 208896 | tf_op jit(solution)/shard_map/all_gather | solution.py:66
  172.4 0.2 reshape.268
  172.7 0.2 copy.25
  172.9 0.3 reshape.269
  173.2 15.0 %all_gather.6 = s32[16,2,1536]{2,1,0:T(2,128)S(1)} all-gather(s32[1,2,1536]{2,1,0:T(2,128)S(1)} %copy-done.2), channel_id=1, replica_groups=mesh['rep'=16,'fsdp'=32] {'rep'}, dimensions={0}, use_global_device_ids=true | all-gather | bytes 208896 | tf_op jit(solution)/shard_map/all_gather | solution.py:69
  188.5 0.2 copy.23
  188.7 0.3 reshape.267
  189.1 1.3 broadcast.289.clone.1
  190.4 22.2 %while.29 = (s32[]{:T(128)}, f32[2,64,3072]{2,1,0:T(8,128)}, s32[2,48,512]{2,1,0:T(8,128)S(1)}, f32[2,48,512]{2,1,0:T(8,128)S(1)}, f32[64]{0:T(128)S(1)}, /*index=5*/f32[64]{0:T(128)S(1)}, s32[]{:T(128)}) while((s32[]{:T(128)}, f32[2,64,3072]{2,1,0:T(8,128)}, s32[2,48,512]{2,1,0:T(8,128)S(1)}, ...), condition=%wide.region_5.6_spmd.clone.clone, body=%wide.region_4.5_spmd.clone.clone.sunk | while | flops 1515307008 | bytes 9586265 | solution.py:77
  190.6 4.4 %fusion.101 = f32[48,64,64]{1,2,0:T(8,128)S(1)} fusion(f32[48,512]{1,0:T(8,128)S(1)} %dynamic-slice_bitcast_fusion.5, s32[48,512]{1,0:T(8,128)S(1)} %add_select_fusion.11, s32[48,512]{1,0:T(8,128)S(1)} %get-tuple-element.317), kind=kOutput, calls=%fused_computation.39.clone.1 | convolution fusion | flops 1212678144 | bytes 1081344 | tf_op jit(solution)/shard_map/while/body/eval_jaxpr/cnu,cnv->cuv/dot_general | solution.py:23
  195.0 1.5 fusion.102
  196.5 2.6 %fusion.103 = f32[64,48,64]{2,0,1:T(8,128)S(1)} fusion(f32[48,64,64]{2,1,0:T(8,128)S(1)} %fusion.102, f32[64]{0:T(128)S(1)} %get-tuple-element.357, f32[64]{0:T(128)S(1)} %get-tuple-element.358), kind=kOutput, calls=%fused_computation.49.clone.1 | convolution fusion | flops 151007232 | bytes 1573376 | tf_op jit(solution)/shard_map/while/body/eval_jaxpr/cxv,vy->xcy/dot_general | solution.py:25
  199.2 0.9 copy.37
  200.1 0.4 broadcast_in_dim.59
  200.5 1.0 constant_dynamic-update-slice_fusion.5
  201.6 4.4 %fusion.101 = f32[48,64,64]{1,2,0:T(8,128)S(1)} fusion(f32[48,512]{1,0:T(8,128)S(1)} %dynamic-slice_bitcast_fusion.5, s32[48,512]{1,0:T(8,128)S(1)} %add_select_fusion.11, s32[48,512]{1,0:T(8,128)S(1)} %get-tuple-element.317), kind=kOutput, calls=%fused_computation.39.clone.1 | convolution fusion | flops 1212678144 | bytes 1081344 | tf_op jit(solution)/shard_map/while/body/eval_jaxpr/cnu,cnv->cuv/dot_general | solution.py:23
  206.1 1.5 fusion.102
  207.6 2.6 %fusion.103 = f32[64,48,64]{2,0,1:T(8,128)S(1)} fusion(f32[48,64,64]{2,1,0:T(8,128)S(1)} %fusion.102, f32[64]{0:T(128)S(1)} %get-tuple-element.357, f32[64]{0:T(128)S(1)} %get-tuple-element.358), kind=kOutput, calls=%fused_computation.49.clone.1 | convolution fusion | flops 151007232 | bytes 1573376 | tf_op jit(solution)/shard_map/while/body/eval_jaxpr/cxv,vy->xcy/dot_general | solution.py:25
  210.2 0.9 copy.37
  211.2 0.4 broadcast_in_dim.59
  211.6 1.0 constant_dynamic-update-slice_fusion.5
  212.6 1.6 broadcast_multiply_fusion
  214.2 1.0 fusion.60
  (34 shorter events, 1.5 us)
Async XLA Ops:
  67.7 1.7 copy-start
  77.6 2.5 %copy-start.2 = (s32[1,2,1536]{2,1,0:T(2,128)S(1)}, s32[1,2,1536]{2,1,0:T(2,128)}, u32[]{:S(2)}) copy-start(s32[1,2,1536]{2,1,0:T(2,128)} %param.10) | copy-start | bytes 36868
  212.6 1.6 copy-start.1
where the time goes:
time: 216 us; the launch traced here: 215 us
  blocking collectives  116 us (54%)
  local copies, waits for them, and re-layouts  52.4 us (24%)
  matrix products  35.2 us (16%)
  other arithmetic  9.98 us (5%)
    psum x1, blocking collectives, body(): square_sum = lax.psum(jnp.sum(gradient * gradient), 'fsdp')  62.5 us
    all_gather x1, blocking collectives, body(): lax.all_gather(kept_values.reshape(1, block_rows, block_cols * per_group)...  38.4 us
    gather x4, local copies, waits for them, and re-layouts, body(): kept_values = jnp.take_along_axis(coeffs, kept_where, axis=2)  30.8 us
    all_gather x1, blocking collectives, body(): lax.all_gather(kept_index, 'rep', axis=0, tiled=True)  15 us
    dot_general x4, matrix products, lists_to_tiles(): sparse_sum = jnp.einsum('cnu,cnv->cuv', high_hot, low_hot, precision=high)  14.4 us
    dot_general x4, matrix products, lists_to_tiles(): tile_sum = jnp.einsum('cxv,vy->xcy', row_pass, dct_rows, precision=high)  10.6 us
    dot_general x4, matrix products, lists_to_tiles(): row_pass = jnp.einsum('ux,cuv->cxv', dct_rows, sparse_sum, precision=high)  6 us
    reshape x2, local copies, waits for them, and re-layouts, body(): coeffs.reshape(block_rows, 64, block_cols, 64).transpose(0, 2, 1, 3)  5 us

commit v1 on v0

v1 whole, which is shorter than its diff:
```python
import functools

import jax
import jax.numpy as jnp
import ml_dtypes
import numpy as np
from jax import lax
from jax.experimental import pallas as pl
from jax.experimental.pallas import tpu as pltpu
from jax.sharding import PartitionSpec as P

clip_rms = 0.5
momentum_decay = 0.9
step_rate = 0.5
VMEM = pltpu.VMEM
NN = (((1,), (0,)), ((), ()))
NT = (((1,), (1,)), ((), ()))


def split_table(table):
    high = table.astype(ml_dtypes.bfloat16)
    low = (table - high.astype(np.float64)).astype(ml_dtypes.bfloat16)
    return high, low


def tables():
    u = np.arange(64, dtype=np.float64)[:, None]
    x = np.arange(64, dtype=np.float64)[None, :]
    weight = np.where(u == 0, np.sqrt(1.0 / 64.0), np.sqrt(2.0 / 64.0))
    dct = weight * np.cos(np.pi * (2.0 * x + 1.0) * u / 128.0)
    pair = np.kron(np.eye(2), dct)
    rows = np.zeros((2, 64, 2, 2, 32))
    by_parity = dct.reshape(32, 2, 64)
    for i in range(2):
        rows[i, :, :, i, :] = by_parity.transpose(2, 1, 0)
    return pair, rows.reshape(128, 128)


def split(value):
    high = value.astype(jnp.bfloat16)
    low = (value - high.astype(jnp.float32)).astype(jnp.bfloat16)
    return high, low


def dot(left, right, dims):
    return lax.dot_general(left, right, dims, preferred_element_type=jnp.float32)


def duplicate(packed):
    lane = lax.broadcasted_iota(jnp.int32, packed.shape, 1)
    other = pltpu.roll(packed, 64, 1)
    return jnp.where(lane < 64, packed, other), jnp.where(lane < 64, other, packed)


def rows_of(offset):
    lane = lax.broadcasted_iota(jnp.int32, offset.shape, 1)
    return jnp.where((offset >> 6) == (lane >> 6), offset & 63, -1)


def square_kernel(grad_ref, out_ref):
    def step(k, total):
        at = pl.ds(pl.multiple_of(k * 256, 256), 256)
        value = grad_ref[:, at].astype(jnp.float32)
        value = value * value
        value = value[:, :128] + value[:, 128:]
        return total + jnp.sum(value.reshape(-1, 8, 128), axis=0)

    total = lax.fori_loop(
        0, grad_ref.shape[1] // 256, step, jnp.zeros((8, 128), jnp.float32), unroll=4
    )
    out_ref[...] = jnp.broadcast_to(
        jnp.sum(total, axis=0, keepdims=True)[None], out_ref.shape
    )


def pick_kernel(
    grad_ref, moment_ref, where_ref, forth_ref, pair_high_ref, pair_low_ref, out_ref, at_ref, kept_ref
):
    for h, offset in enumerate(duplicate(where_ref[...] & 127)):
        at_ref[h] = rows_of(offset)
    level = lax.broadcasted_iota(jnp.int32, (64, 128), 0)
    forth = forth_ref[...]
    pair_high, pair_low = pair_high_ref[...], pair_low_ref[...]

    def step(k, carry):
        at = pl.ds(pl.multiple_of(k * 128, 128), 128)
        both = jnp.concatenate([grad_ref[:, at], moment_ref[:, at]], axis=1)
        first = dot(forth, both, NN)
        first = first[:128] + first[128:]
        for n in range(2):
            high, low = split(first[:, n * 128 : (n + 1) * 128])
            coeffs = dot(pair_high, high, NT) + (dot(pair_high, low, NT) + dot(pair_low, high, NT))
            for h in range(2):
                hit = level == at_ref[h, pl.ds(k, 1), :]
                kept_ref[n, h, pl.ds(k, 1), :] = jnp.sum(
                    jnp.where(hit, coeffs[h * 64 : (h + 1) * 64], 0.0), axis=0, keepdims=True
                )
        return carry

    lax.fori_loop(0, grad_ref.shape[1] // 128, step, 0, unroll=2)
    lane = lax.broadcasted_iota(jnp.int32, out_ref.shape[1:], 1)
    for n in range(2):
        front, back = kept_ref[n, 0], kept_ref[n, 1]
        front = front + pltpu.roll(front, 64, 1)
        back = back + pltpu.roll(back, 64, 1)
        out_ref[n] = jnp.where(lane < 64, front, back)


def scale_kernel(count, squares_ref, picked_ref, where_ref, factor_ref, out_ref):
    total = jnp.sum(jnp.sum(squares_ref[...], axis=0), axis=1, keepdims=True)
    mean_square = jnp.broadcast_to(total, (1, 128)) / count
    factor = jnp.minimum(1.0, clip_rms / jnp.sqrt(mean_square + 1e-06))
    factor_ref[...] = factor
    groups = where_ref.shape[0]
    out_ref[:groups] = momentum_decay * picked_ref[1] + factor * picked_ref[0]
    out_ref[groups:] = (where_ref[...] & 127).astype(jnp.float32)


def decode(sparse, back_high_ref, back_low_ref, pair_high_ref, pair_low_ref):
    high, low = split(sparse)
    back_high, back_low = back_high_ref[...], back_low_ref[...]
    first = dot(back_high, high, NT) + (dot(back_high, low, NT) + dot(back_low, high, NT))
    high, low = split(first)
    pair_high, pair_low = pair_high_ref[...], pair_low_ref[...]
    return dot(high, pair_high, NN) + (dot(low, pair_high, NN) + dot(high, pair_low, NN))


def finish_kernel(
    own_ref,
    all_ref,
    factor_ref,
    grad_ref,
    moment_ref,
    weight_ref,
    back_high_ref,
    back_low_ref,
    pair_high_ref,
    pair_low_ref,
    new_moment_ref,
    new_weight_ref,
    at_ref,
    value_ref,
):
    replicas = all_ref.shape[0]
    groups = all_ref.shape[1] // 2
    table_refs = (back_high_ref, back_low_ref, pair_high_ref, pair_low_ref)
    for r in range(replicas + 1):
        listing = own_ref[...] if r == replicas else all_ref[r]
        values = duplicate(listing[:groups])
        offsets = duplicate(listing[groups:].astype(jnp.int32))
        for h in range(2):
            value_ref[r, h] = values[h]
            at_ref[r, h] = rows_of(offsets[h])
    level = lax.broadcasted_iota(jnp.int32, (64, 128), 0)
    factor = factor_ref[...]

    def term(r, h, k):
        hit = level == at_ref[r, h, pl.ds(k, 1), :]
        return jnp.where(hit, value_ref[r, h, pl.ds(k, 1), :], 0.0)

    def step(k, carry):
        at = pl.ds(pl.multiple_of(k * 128, 128), 128)
        own = jnp.concatenate([term(replicas, h, k) for h in range(2)], axis=0)
        blended = momentum_decay * moment_ref[:, at].astype(jnp.float32) + factor * grad_ref[
            :, at
        ].astype(jnp.float32)
        new_moment_ref[:, at] = (blended - decode(own, *table_refs)).astype(jnp.bfloat16)
        parts = []
        for h in range(2):
            total = term(0, h, k)
            for r in range(1, replicas):
                total = total + term(r, h, k)
            parts.append(total)
        update = decode(jnp.concatenate(parts, axis=0), *table_refs)
        new_weight_ref[:, at] = (
            weight_ref[:, at].astype(jnp.float32) - step_rate * update
        ).astype(jnp.bfloat16)
        return carry

    lax.fori_loop(0, groups, step, 0, unroll=2)


def body(grad, momentum, kept_index, weights):
    grad, momentum = grad[0], momentum[0]
    rows, cols = grad.shape
    ring = lax.axis_size("fsdp")
    replicas = lax.axis_size("rep")
    groups = cols // 128
    pair, back = tables()
    pair_high, pair_low = (jnp.asarray(t) for t in split_table(pair))
    back_high, back_low = (jnp.asarray(t) for t in split_table(back))
    forth = jnp.asarray(np.concatenate(split_table(back.T), axis=0))
    whole = pl.BlockSpec(memory_space=VMEM)
    params = pltpu.CompilerParams(vmem_limit_bytes=48 * 1024 * 1024)

    squares = pl.pallas_call(
        square_kernel,
        out_shape=jax.ShapeDtypeStruct((ring, 1, 128), jnp.float32),
        in_specs=[whole],
        out_specs=whole,
        compiler_params=params,
        name="squares",
    )(grad)
    squares = lax.all_to_all(squares, "fsdp", 0, 0, tiled=True)

    where = kept_index[0].reshape(2, groups, 2, 32).transpose(1, 2, 0, 3).reshape(groups, 128)
    picked = pl.pallas_call(
        pick_kernel,
        out_shape=jax.ShapeDtypeStruct((2, groups, 128), jnp.float32),
        in_specs=[whole] * 6,
        out_specs=whole,
        scratch_shapes=[
            VMEM((2, groups, 128), jnp.int32),
            VMEM((2, 2, groups, 128), jnp.float32),
        ],
        compiler_params=params,
        cost_estimate=pl.CostEstimate(
            flops=2 * 2 * 5 * 128 * 128 * cols, bytes_accessed=4 * rows * cols, transcendentals=0
        ),
        name="pick",
    )(grad, momentum, where, forth, pair_high, pair_low)

    factor, own = pl.pallas_call(
        functools.partial(scale_kernel, float(rows * ring * cols)),
        out_shape=(
            jax.ShapeDtypeStruct((1, 128), jnp.float32),
            jax.ShapeDtypeStruct((2 * groups, 128), jnp.float32),
        ),
        in_specs=[whole] * 3,
        out_specs=(whole, whole),
        compiler_params=params,
        name="scale",
    )(squares, picked, where)

    every = lax.all_gather(own, "rep", axis=0, tiled=False)

    new_momentum, new_weights = pl.pallas_call(
        finish_kernel,
        out_shape=(
            jax.ShapeDtypeStruct((rows, cols), jnp.bfloat16),
            jax.ShapeDtypeStruct((rows, cols), jnp.bfloat16),
        ),
        in_specs=[whole] * 10,
        out_specs=(whole, whole),
        scratch_shapes=[
            VMEM((replicas + 1, 2, groups, 128), jnp.int32),
            VMEM((replicas + 1, 2, groups, 128), jnp.float32),
        ],
        compiler_params=params,
        name="finish",
    )(own, every, factor, grad, momentum, weights, back_high, back_low, pair_high, pair_low)
    return (new_momentum[None], new_weights)


def solution(mesh):
    in_specs = (
        P("rep", "fsdp", None),
        P("rep", "fsdp", None),
        P("rep", "fsdp", None),
        P("fsdp", None),
    )
    out_specs = (P("rep", "fsdp", None), P("fsdp", None))
    return jax.shard_map(body, mesh=mesh, in_specs=in_specs, out_specs=out_specs, check_vma=False)
```

time: 216 us -> 65.5 us (0.30)
  blocking collectives: 116 us -> 25.2 us
  local copies, waits for them, and re-layouts: 52.4 us -> 3.22 us
  matrix products: 35.2 us -> 0 us
  Pallas kernels: 0 us -> 25.4 us
  starting transfers between devices: 0 us -> 10.6 us
  other arithmetic: 9.98 us -> 0 us
    psum x1 -> x0, blocking collectives: 62.5 us -> none  [body(): square_sum = lax.psum(jnp.sum(gradient * gradient), 'fsdp')]
    dot_general x14 -> x0, matrix products: 35.2 us -> none  [the longest x4 14.4 us: lists_to_tiles(): sparse_sum = jnp.einsum('cnu,cnv->cuv', high_hot, low_hot, precision=high)]
    gather x4 -> x0, local copies, waits for them, and re-layouts: 30.8 us -> none  [body(): kept_values = jnp.take_along_axis(coeffs, kept_where, axis=2)]
    all_gather x2 -> x1, blocking collectives: 53.4 us -> 25.2 us  [body(): every = lax.all_gather(own, 'rep', axis=0, tiled=False)]
    pallas_call x0 -> x4, Pallas kernels: none -> 25.4 us  [the longest x1 15.4 us: body(): pl.pallas_call(finish_kernel, out_shape=(jax.ShapeDtypeStruct((rows, cols...]
    all_to_all x0 -> x1, starting transfers between devices: none -> 10.6 us  [body(): squares = lax.all_to_all(squares, 'fsdp', 0, 0, tiled=True)]
    reshape x7 -> x1, local copies, waits for them, and re-layouts: 8.54 us -> 0.1 us  [body(): kept_index[0].reshape(2, groups, 2, 32).transpose(1, 2, 0, 3)]
    transpose x6 -> x0, local copies, waits for them, and re-layouts: 4.14 us -> none  [the longest x4 3.66 us: lists_to_tiles(): tile_sum = jnp.einsum('cxv,vy->xcy', row_pass, dct_rows, precision=high)]
  transfers between devices with their start and end apart: 0 -> 1, of which waited for: 0 -> 0; matrix products, arithmetic and copies ran while one was open for 0% -> 0% of each run, Pallas kernels for 0% -> 14%
where the time goes in v1:
time: 65.5 us; the launch traced here: 65.2 us
  Pallas kernels  25.4 us (39%)
  blocking collectives  25.2 us (38%)
  starting transfers between devices  10.6 us (16%)
  local copies, waits for them, and re-layouts  3.22 us (5%)
  between operations  0.73 us (1%)
    all_gather x1, blocking collectives, body(): every = lax.all_gather(own, 'rep', axis=0, tiled=False)  25.2 us
    pallas_call x1, Pallas kernels, body(): pl.pallas_call(finish_kernel, out_shape=(jax.ShapeDtypeStruct((rows, cols...  15.4 us
    all_to_all x1, starting transfers between devices, body(): squares = lax.all_to_all(squares, 'fsdp', 0, 0, tiled=True)  10.6 us
    pallas_call x1, Pallas kernels, body(): pl.pallas_call(pick_kernel, out_shape=jax.ShapeDtypeStruct((2, groups, 12...  9.06 us
    unnamed x22, local copies, waits for them, and re-layouts  2.98 us
  transfers between devices with their start and end apart: 1, of which 0 were waited for; matrix products, arithmetic and copies ran while one was open for 0% of the time, Pallas kernels for 14%

profile of v1, /device:TPU:1, one launch (start us, length us, event | category | flops | bytes accessed | tf_op | source)
XLA Modules:
  0.0 65.2 jit_solution(10040871791018646509)
XLA Ops:
  0.6 0.0 copy-start
  0.6 1.1 %copy-done = bf16[1,128,3072]{2,1,0:T(8,128)(2,1)S(1)} copy-done((bf16[1,128,3072]{2,1,0:T(8,128)(2,1)S(1)}, bf16[1,128,3072]{2,1,0:T(8,128)(2,1)}, u32[]{:S(2)}) %copy-start) | copy-done | bytes 786456
  1.8 0.0 copy-start.1
  1.8 0.8 %squares.1 = f32[32,1,128]{2,1,0:T(1,128)} custom-call(bf16[128,3072]{1,0:T(8,128)(2,1)S(1)} %bitcast.7), custom_call_target="tpu_custom_call" | custom-call | tf_op jit(solution)/shard_map/squares/pallas_call | solution.py:196
  2.6 0.0 copy-start.10
  2.6 10.6 %all-to-all-start = ((f32[32,1,128]{2,1,0:T(1,128)}), f32[32,1,128]{2,1,0:T(1,128)S(1)}, u32[]{:S(2)}, u32[]{:S(2)}) async-start(f32[32,1,128]{2,1,0:T(1,128)} %squares.1), calls=%async_computation | async-start | bytes 32768 | tf_op jit(solution)/shard_map/all_to_all | solution.py:204
  13.2 0.0 copy-done.10
  13.2 0.1 reshape_squeeze.3
  13.3 0.0 copy-start.6
  13.3 0.0 copy-start.9
  13.4 0.0 copy-start.5
  13.4 0.1 reshape.7.where_ref
  13.5 0.0 copy-done.1
  13.5 0.6 copy-done.6
  14.1 0.1 copy-done.9
  14.2 0.0 copy-done.5
  14.2 0.0 copy-start.2
  14.2 1.1 %copy-done.2 = bf16[1,128,3072]{2,1,0:T(8,128)(2,1)S(1)} copy-done((bf16[1,128,3072]{2,1,0:T(8,128)(2,1)S(1)}, bf16[1,128,3072]{2,1,0:T(8,128)(2,1)}, u32[]{:S(2)}) %copy-start.2) | copy-done | bytes 786456
  15.3 0.0 copy-start.3
  15.3 0.0 copy-start.4
  15.3 9.1 %pick.1.picked_ref = f32[2,24,128]{2,1,0:T(8,128)S(1)} custom-call(bf16[128,3072]{1,0:T(8,128)(2,1)S(1)} %bitcast.8, bf16[128,3072]{1,0:T(8,128)(2,1)S(1)} %bitcast.11, s32[24,128]{1,0:T(8,128)S(1)} %reshape.7.where_ref, bf16[256,128]{1,0:T(8,128)(2,1)S(1)} %copy-done.9, bf16[128,128]{1,0:T(8,128)(2,1)S(1)} %copy-done.6, bf16[128,128]{1,0:T(8,128)(2,1)S(1)} %copy-done.5), custom_call_target="tpu_custom_call" | custom-call | flops 1006632960 | bytes 1572864 | tf_op jit(solution)/shard_map/pick/pallas_call | solution.py:207
  24.4 0.0 all-to-all-done.squares_ref
  24.4 0.1 scale.1
  24.5 0.0 copy-start.7
  24.5 0.0 copy-start.8
  24.5 25.2 %all-gather = f32[768,128]{1,0:T(8,128)S(1)} all-gather(f32[48,128]{1,0:T(8,128)S(1)} %get-tuple-element.6.own_ref), channel_id=2, replica_groups=mesh['rep'=16,'fsdp'=32] {'rep'}, dimensions={0}, use_global_device_ids=true | all-gather | bytes 417792 | tf_op jit(solution)/shard_map/all_gather | solution.py:235
  49.7 0.0 copy-done.3
  49.7 0.0 copy-done.4
  49.7 0.0 copy-done.7
  49.7 0.0 copy-done.8
  49.7 15.4 %finish.1 = (bf16[128,3072]{1,0:T(8,128)(2,1)}, bf16[128,3072]{1,0:T(8,128)(2,1)}) custom-call(f32[48,128]{1,0:T(8,128)S(1)} %get-tuple-element.6.own_ref, f32[16,48,128]{2,1,0:T(8,128)S(1)} %bitcast.10, f32[1,128]{1,0:T(1,128)S(1)} %get-tuple-element.7.factor_ref, bf16[128,3072]{1,0:T(8,128)(2,1)S(1)} %bitcast.9, bf16[128,3072]{1,0:T(8,128)(2,1)S(1)} %bitcast.12, ...), custom_call_target="tpu_custom_call" | custom-call | tf_op jit(solution)/shard_map/finish/pallas_call | solution.py:237
  (1 shorter events, 0.0 us)
Async XLA Ops:
  0.6 1.1 %copy-start = (bf16[1,128,3072]{2,1,0:T(8,128)(2,1)S(1)}, bf16[1,128,3072]{2,1,0:T(8,128)(2,1)}, u32[]{:S(2)}) copy-start(bf16[1,128,3072]{2,1,0:T(8,128)(2,1)} %param.9) | copy-start | bytes 2359300
  1.8 11.7 %copy-start.1 = (bf16[1,128,3072]{2,1,0:T(8,128)(2,1)S(1)}, bf16[1,128,3072]{2,1,0:T(8,128)(2,1)}, u32[]{:S(2)}) copy-start(bf16[1,128,3072]{2,1,0:T(8,128)(2,1)} %param.9) | copy-start | bytes 2359300
  2.6 10.6 %copy-start.10 = (s32[1,2,1536]{2,1,0:T(2,128)S(1)}, s32[1,2,1536]{2,1,0:T(2,128)}, u32[]{:S(2)}) copy-start(s32[1,2,1536]{2,1,0:T(2,128)} %param.11) | copy-start | bytes 36868
  2.6 21.8 %all-to-all-start = ((f32[32,1,128]{2,1,0:T(1,128)}), f32[32,1,128]{2,1,0:T(1,128)S(1)}, u32[]{:S(2)}, u32[]{:S(2)}) async-start(f32[32,1,128]{2,1,0:T(1,128)} %squares.1), calls=%async_computation | async-start | bytes 32768 | tf_op jit(solution)/shard_map/all_to_all | solution.py:204
  13.3 0.8 %copy-start.6 = (bf16[128,128]{1,0:T(8,128)(2,1)S(1)}, bf16[128,128]{1,0:T(8,128)(2,1)}, u32[]{:S(2)}) copy-start(bf16[128,128]{1,0:T(8,128)(2,1)} %constant.10.clone.pair_high_ref) | copy-start | bytes 98308
  13.3 0.8 %copy-start.9 = (bf16[256,128]{1,0:T(8,128)(2,1)S(1)}, bf16[256,128]{1,0:T(8,128)(2,1)}, u32[]{:S(2)}) copy-start(bf16[256,128]{1,0:T(8,128)(2,1)} %constant.14.clone.forth_ref) | copy-start | bytes 196612
  13.4 0.8 %copy-start.5 = (bf16[128,128]{1,0:T(8,128)(2,1)S(1)}, bf16[128,128]{1,0:T(8,128)(2,1)}, u32[]{:S(2)}) copy-start(bf16[128,128]{1,0:T(8,128)(2,1)} %constant.11.clone.pair_low_ref) | copy-start | bytes 98308
  14.2 1.1 %copy-start.2 = (bf16[1,128,3072]{2,1,0:T(8,128)(2,1)S(1)}, bf16[1,128,3072]{2,1,0:T(8,128)(2,1)}, u32[]{:S(2)}) copy-start(bf16[1,128,3072]{2,1,0:T(8,128)(2,1)} %param.10) | copy-start | bytes 2359300
  15.3 34.4 %copy-start.3 = (bf16[1,128,3072]{2,1,0:T(8,128)(2,1)S(1)}, bf16[1,128,3072]{2,1,0:T(8,128)(2,1)}, u32[]{:S(2)}) copy-start(bf16[1,128,3072]{2,1,0:T(8,128)(2,1)} %param.10) | copy-start | bytes 2359300
  15.3 34.4 %copy-start.4 = (bf16[128,3072]{1,0:T(8,128)(2,1)S(1)}, bf16[128,3072]{1,0:T(8,128)(2,1)}, u32[]{:S(2)}) copy-start(bf16[128,3072]{1,0:T(8,128)(2,1)} %weight_ref.1) | copy-start | bytes 2359300
  24.5 25.2 %copy-start.7 = (bf16[128,128]{1,0:T(8,128)(2,1)S(1)}, bf16[128,128]{1,0:T(8,128)(2,1)}, u32[]{:S(2)}) copy-start(bf16[128,128]{1,0:T(8,128)(2,1)} %constant.13.clone.back_low_ref) | copy-start | bytes 98308
  24.5 25.2 %copy-start.8 = (bf16[128,128]{1,0:T(8,128)(2,1)S(1)}, bf16[128,128]{1,0:T(8,128)(2,1)}, u32[]{:S(2)}) copy-start(bf16[128,128]{1,0:T(8,128)(2,1)} %constant.12.clone.back_high_ref) | copy-start | bytes 98308

commit v2 on v1

v2 whole, which is shorter than its diff:
```python
import functools

import jax
import jax.numpy as jnp
import ml_dtypes
import numpy as np
from jax import lax
from jax.experimental import pallas as pl
from jax.experimental.pallas import tpu as pltpu
from jax.sharding import PartitionSpec as P

clip_rms = 0.5
momentum_decay = 0.9
step_rate = 0.5
VMEM = pltpu.VMEM
UNROLL = 24
NN = (((1,), (0,)), ((), ()))
NT = (((1,), (1,)), ((), ()))


def split_table(table):
    high = table.astype(ml_dtypes.bfloat16)
    low = (table - high.astype(np.float64)).astype(ml_dtypes.bfloat16)
    return high, low


def tables():
    u = np.arange(64, dtype=np.float64)[:, None]
    x = np.arange(64, dtype=np.float64)[None, :]
    weight = np.where(u == 0, np.sqrt(1.0 / 64.0), np.sqrt(2.0 / 64.0))
    dct = weight * np.cos(np.pi * (2.0 * x + 1.0) * u / 128.0)
    pair = np.kron(np.eye(2), dct)
    rows = np.zeros((2, 64, 2, 2, 32))
    by_parity = dct.reshape(32, 2, 64)
    for i in range(2):
        rows[i, :, :, i, :] = by_parity.transpose(2, 1, 0)
    return pair, rows.reshape(128, 128)


def widen(table):
    high, low = split_table(table)
    return np.block([[high, high], [low, low]])


def split(value):
    high = value.astype(jnp.bfloat16)
    low = (value - high.astype(jnp.float32)).astype(jnp.bfloat16)
    return high, low


def dot(left, right, dims):
    return lax.dot_general(left, right, dims, preferred_element_type=jnp.float32)


def duplicate(packed):
    lane = lax.broadcasted_iota(jnp.int32, packed.shape, 1)
    other = pltpu.roll(packed, 64, 1)
    return jnp.where(lane < 64, packed, other), jnp.where(lane < 64, other, packed)


def rows_of(offset):
    lane = lax.broadcasted_iota(jnp.int32, offset.shape, 1)
    return jnp.where((offset >> 6) == (lane >> 6), offset & 63, -1)


def stages(count, unroll, *steps):
    for step in steps:
        if unroll >= count:
            for k in range(count):
                step(k)
        else:
            lax.fori_loop(0, count, lambda k, carry, step=step: (step(k), carry)[1], 0, unroll=unroll)


def block(k):
    return pl.ds(k * 128 if isinstance(k, int) else pl.multiple_of(k * 128, 128), 128)


def row(k):
    return pl.ds(k, 1)


def square_kernel(grad_ref, out_ref):
    def step(k, total):
        value = grad_ref[:, block(k)].astype(jnp.float32)
        return total + jnp.sum((value * value).reshape(-1, 8, 128), axis=0)

    total = lax.fori_loop(
        0, grad_ref.shape[1] // 128, step, jnp.zeros((8, 128), jnp.float32), unroll=8
    )
    out_ref[...] = jnp.broadcast_to(
        jnp.sum(total, axis=0, keepdims=True)[None], out_ref.shape
    )


def pick_kernel(
    grad_ref, moment_ref, where_ref, forth_ref, pair_ref, out_ref, at_ref, first_ref, kept_ref
):
    groups = where_ref.shape[0]
    for h, offset in enumerate(duplicate(where_ref[...] & 127)):
        at_ref[h] = rows_of(offset)
    level = lax.broadcasted_iota(jnp.int32, (64, 128), 0)

    def over_rows(k):
        both = jnp.concatenate([grad_ref[:, block(k)], moment_ref[:, block(k)]], axis=1)
        first = dot(forth_ref[...], both, NN)
        high, low = split(first[:128] + first[128:])
        for n in range(2):
            first_ref[k, n * 128 : (n + 1) * 128, :128] = high[:, n * 128 : (n + 1) * 128]
            first_ref[k, n * 128 : (n + 1) * 128, 128:] = low[:, n * 128 : (n + 1) * 128]

    def over_columns(k):
        coeffs = dot(pair_ref[...], first_ref[k], NT)
        coeffs = coeffs[:128] + coeffs[128:]
        for h in range(2):
            hit = level == at_ref[h, row(k), :]
            for n in range(2):
                part = coeffs[h * 64 : (h + 1) * 64, n * 128 : (n + 1) * 128]
                kept_ref[n, h, row(k), :] = jnp.sum(
                    jnp.where(hit, part, 0.0), axis=0, keepdims=True
                )

    stages(groups, UNROLL, over_rows, over_columns)
    lane = lax.broadcasted_iota(jnp.int32, out_ref.shape[1:], 1)
    for n in range(2):
        front, back = kept_ref[n, 0], kept_ref[n, 1]
        front = front + pltpu.roll(front, 64, 1)
        back = back + pltpu.roll(back, 64, 1)
        out_ref[n] = jnp.where(lane < 64, front, back)


def scale_kernel(count, squares_ref, picked_ref, where_ref, factor_ref, out_ref):
    total = jnp.sum(jnp.sum(squares_ref[...], axis=0), axis=1, keepdims=True)
    mean_square = jnp.broadcast_to(total, (1, 128)) / count
    factor = jnp.minimum(1.0, clip_rms / jnp.sqrt(mean_square + 1e-06))
    factor_ref[...] = factor
    groups = where_ref.shape[0]
    out_ref[:groups] = momentum_decay * picked_ref[1] + factor * picked_ref[0]
    out_ref[groups:] = (where_ref[...] & 127).astype(jnp.float32)


def finish_kernel(
    own_ref,
    all_ref,
    factor_ref,
    grad_ref,
    moment_ref,
    weight_ref,
    back_ref,
    pair_ref,
    new_moment_ref,
    new_weight_ref,
    at_ref,
    value_ref,
    sparse_ref,
    first_ref,
):
    replicas = all_ref.shape[0]
    groups = all_ref.shape[1] // 2
    for r in range(replicas + 1):
        listing = own_ref[...] if r == replicas else all_ref[r]
        values = duplicate(listing[:groups])
        offsets = duplicate(listing[groups:].astype(jnp.int32))
        for h in range(2):
            value_ref[r, h] = values[h]
            at_ref[r, h] = rows_of(offsets[h])
    level = lax.broadcasted_iota(jnp.int32, (64, 128), 0)
    factor = factor_ref[...]

    def term(r, h, k):
        hit = level == at_ref[r, h, row(k), :]
        return jnp.where(hit, value_ref[r, h, row(k), :], 0.0)

    def scatter(k):
        for h in range(2):
            total = term(0, h, k)
            for r in range(1, replicas):
                total = total + term(r, h, k)
            for n, part in enumerate((term(replicas, h, k), total)):
                high, low = split(part)
                at = slice(n * 128 + h * 64, n * 128 + h * 64 + 64)
                sparse_ref[k, at, :128] = high
                sparse_ref[k, at, 128:] = low

    def over_rows(k):
        first = dot(back_ref[...], sparse_ref[k], NT)
        high, low = split(first[:128] + first[128:])
        for n in range(2):
            first_ref[k, n * 128 : (n + 1) * 128, :128] = high[:, n * 128 : (n + 1) * 128]
            first_ref[k, n * 128 : (n + 1) * 128, 128:] = low[:, n * 128 : (n + 1) * 128]

    def over_columns(k):
        decoded = dot(first_ref[k], pair_ref[...], NN)
        decoded = decoded[:, :128] + decoded[:, 128:]
        blended = momentum_decay * moment_ref[:, block(k)].astype(jnp.float32)
        blended = blended + factor * grad_ref[:, block(k)].astype(jnp.float32)
        new_moment_ref[:, block(k)] = (blended - decoded[:128]).astype(jnp.bfloat16)
        new_weight_ref[:, block(k)] = (
            weight_ref[:, block(k)].astype(jnp.float32) - step_rate * decoded[128:]
        ).astype(jnp.bfloat16)

    stages(groups, UNROLL, scatter, over_rows, over_columns)


def body(grad, momentum, kept_index, weights):
    grad, momentum = grad[0], momentum[0]
    rows, cols = grad.shape
    ring = lax.axis_size("fsdp")
    replicas = lax.axis_size("rep")
    groups = cols // 128
    pair, back = tables()
    forth = jnp.asarray(np.concatenate(split_table(back.T), axis=0))
    back_wide = jnp.asarray(widen(back))
    pair_wide = jnp.asarray(widen(pair))
    pair_tall = jnp.asarray(np.ascontiguousarray(widen(pair.T).T))
    whole = pl.BlockSpec(memory_space=VMEM)
    params = pltpu.CompilerParams(vmem_limit_bytes=48 * 1024 * 1024)

    squares = pl.pallas_call(
        square_kernel,
        out_shape=jax.ShapeDtypeStruct((ring, 1, 128), jnp.float32),
        in_specs=[whole],
        out_specs=whole,
        compiler_params=params,
        name="squares",
    )(grad)
    squares = lax.all_to_all(squares, "fsdp", 0, 0, tiled=True)

    where = kept_index[0].reshape(2, groups, 2, 32).transpose(1, 2, 0, 3).reshape(groups, 128)
    picked = pl.pallas_call(
        pick_kernel,
        out_shape=jax.ShapeDtypeStruct((2, groups, 128), jnp.float32),
        in_specs=[whole] * 5,
        out_specs=whole,
        scratch_shapes=[
            VMEM((2, groups, 128), jnp.int32),
            VMEM((groups, 256, 256), jnp.bfloat16),
            VMEM((2, 2, groups, 128), jnp.float32),
        ],
        compiler_params=params,
        cost_estimate=pl.CostEstimate(
            flops=2 * 2 * 5 * 128 * 128 * cols, bytes_accessed=4 * rows * cols, transcendentals=0
        ),
        name="pick",
    )(grad, momentum, where, forth, pair_wide)

    factor, own = pl.pallas_call(
        functools.partial(scale_kernel, float(rows * ring * cols)),
        out_shape=(
            jax.ShapeDtypeStruct((1, 128), jnp.float32),
            jax.ShapeDtypeStruct((2 * groups, 128), jnp.float32),
        ),
        in_specs=[whole] * 3,
        out_specs=(whole, whole),
        compiler_params=params,
        name="scale",
    )(squares, picked, where)

    every = lax.all_gather(own, "rep", axis=0, tiled=False)

    new_momentum, new_weights = pl.pallas_call(
        finish_kernel,
        out_shape=(
            jax.ShapeDtypeStruct((rows, cols), jnp.bfloat16),
            jax.ShapeDtypeStruct((rows, cols), jnp.bfloat16),
        ),
        in_specs=[whole] * 8,
        out_specs=(whole, whole),
        scratch_shapes=[
            VMEM((replicas + 1, 2, groups, 128), jnp.int32),
            VMEM((replicas + 1, 2, groups, 128), jnp.float32),
            VMEM((groups, 256, 256), jnp.bfloat16),
            VMEM((groups, 256, 256), jnp.bfloat16),
        ],
        compiler_params=params,
        name="finish",
    )(own, every, factor, grad, momentum, weights, back_wide, pair_tall)
    return (new_momentum[None], new_weights)


def solution(mesh):
    in_specs = (
        P("rep", "fsdp", None),
        P("rep", "fsdp", None),
        P("rep", "fsdp", None),
        P("fsdp", None),
    )
    out_specs = (P("rep", "fsdp", None), P("fsdp", None))
    return jax.shard_map(body, mesh=mesh, in_specs=in_specs, out_specs=out_specs, check_vma=False)
```

time: 65.5 us -> 55.6 us (0.85)
  Pallas kernels: 25.4 us -> 9.99 us
  waiting for transfers between devices: 0.01 us -> 4.49 us
  blocking collectives: 25.2 us -> 26.3 us
    pallas_call x1, Pallas kernels: 15.4 us -> 7.12 us  [body(): pl.pallas_call(finish_kernel, out_shape=(jax.ShapeDtypeStruct((rows, cols...]
    pallas_call x1, Pallas kernels: 9.06 us -> 1.91 us  [body(): pl.pallas_call(pick_kernel, out_shape=jax.ShapeDtypeStruct((2, groups, 12...]
    all_to_all x1, waiting for transfers between devices: 0.01 us -> 4.49 us  [body(): squares = lax.all_to_all(squares, 'fsdp', 0, 0, tiled=True)]
    all_gather x1, blocking collectives: 25.2 us -> 26.3 us  [body(): every = lax.all_gather(own, 'rep', axis=0, tiled=False)]
    unnamed x22 -> x20, local copies, waits for them, and re-layouts: 2.98 us -> 2.98 us
  transfers between devices with their start and end apart: 1 -> 1, of which waited for: 0 -> 1; matrix products, arithmetic and copies ran while one was open for 0% -> 0% of each run, Pallas kernels for 14% -> 3%
where the time goes in v2:
time: 55.6 us; the launch traced here: 55.3 us
  blocking collectives  26.3 us (47%)
  starting transfers between devices  10.6 us (19%)
  Pallas kernels  9.99 us (18%)
  waiting for transfers between devices  4.49 us (8%)
  local copies, waits for them, and re-layouts  3.22 us (6%)
  between operations  0.71 us (1%)
    all_gather x1, blocking collectives, body(): every = lax.all_gather(own, 'rep', axis=0, tiled=False)  26.3 us
    all_to_all x1, starting transfers between devices, body(): squares = lax.all_to_all(squares, 'fsdp', 0, 0, tiled=True)  10.6 us
    pallas_call x1, Pallas kernels, body(): pl.pallas_call(finish_kernel, out_shape=(jax.ShapeDtypeStruct((rows, cols...  7.12 us
    all_to_all x1, waiting for transfers between devices, body(): squares = lax.all_to_all(squares, 'fsdp', 0, 0, tiled=True)  4.49 us
    unnamed x20, local copies, waits for them, and re-layouts  2.98 us
    pallas_call x1, Pallas kernels, body(): pl.pallas_call(pick_kernel, out_shape=jax.ShapeDtypeStruct((2, groups, 12...  1.91 us
  transfers between devices with their start and end apart: 1, of which 1 were waited for; matrix products, arithmetic and copies ran while one was open for 0% of the time, Pallas kernels for 3%

profile of v2, /device:TPU:1, one launch (start us, length us, event | category | flops | bytes accessed | tf_op | source)
XLA Modules:
  0.0 55.3 jit_solution(12152815186720943944)
XLA Ops:
  0.6 0.0 copy-start
  0.6 1.1 %copy-done = bf16[1,128,3072]{2,1,0:T(8,128)(2,1)S(1)} copy-done((bf16[1,128,3072]{2,1,0:T(8,128)(2,1)S(1)}, bf16[1,128,3072]{2,1,0:T(8,128)(2,1)}, u32[]{:S(2)}) %copy-start) | copy-done | bytes 786456
  1.8 0.0 copy-start.9
  1.8 0.0 copy-start.1
  1.8 0.8 %squares.1 = f32[32,1,128]{2,1,0:T(1,128)} custom-call(bf16[128,3072]{1,0:T(8,128)(2,1)S(1)} %bitcast.7), custom_call_target="tpu_custom_call" | custom-call | tf_op jit(solution)/shard_map/squares/pallas_call | solution.py:219
  2.6 0.0 copy-start.7
  2.6 10.6 %all-to-all-start = ((f32[32,1,128]{2,1,0:T(1,128)}), f32[32,1,128]{2,1,0:T(1,128)S(1)}, u32[]{:S(2)}, u32[]{:S(2)}) async-start(f32[32,1,128]{2,1,0:T(1,128)} %squares.1), calls=%async_computation | async-start | bytes 32768 | tf_op jit(solution)/shard_map/all_to_all | solution.py:227
  13.2 0.0 copy-done.9
  13.3 0.1 reshape_squeeze.3
  13.4 0.0 copy-start.8
  13.4 0.1 reshape.7.where_ref
  13.5 0.0 copy-done.1
  13.5 0.0 copy-done.7
  13.5 0.7 %copy-done.8 = bf16[256,128]{1,0:T(8,128)(2,1)S(1)} copy-done((bf16[256,128]{1,0:T(8,128)(2,1)S(1)}, bf16[256,128]{1,0:T(8,128)(2,1)}, u32[]{:S(2)}) %copy-start.8) | copy-done | bytes 65560
  14.2 0.0 copy-start.2
  14.2 1.1 %copy-done.2 = bf16[1,128,3072]{2,1,0:T(8,128)(2,1)S(1)} copy-done((bf16[1,128,3072]{2,1,0:T(8,128)(2,1)S(1)}, bf16[1,128,3072]{2,1,0:T(8,128)(2,1)}, u32[]{:S(2)}) %copy-start.2) | copy-done | bytes 786456
  15.3 0.0 copy-start.3
  15.4 0.0 copy-start.4
  15.4 1.9 %pick.1.picked_ref = f32[2,24,128]{2,1,0:T(8,128)S(1)} custom-call(bf16[128,3072]{1,0:T(8,128)(2,1)S(1)} %bitcast.8, bf16[128,3072]{1,0:T(8,128)(2,1)S(1)} %bitcast.11, s32[24,128]{1,0:T(8,128)S(1)} %reshape.7.where_ref, bf16[256,128]{1,0:T(8,128)(2,1)S(1)} %copy-done.8, bf16[256,256]{1,0:T(8,128)(2,1)S(1)} %copy-done.7), custom_call_target="tpu_custom_call" | custom-call | flops 1006632960 | bytes 1572864 | tf_op jit(solution)/shard_map/pick/pallas_call | solution.py:230
  17.3 4.5 %all-to-all-done.squares_ref = f32[32,1,128]{2,1,0:T(1,128)S(1)} async-done(((f32[32,1,128]{2,1,0:T(1,128)}), f32[32,1,128]{2,1,0:T(1,128)S(1)}, u32[]{:S(2)}, u32[]{:S(2)}) %all-to-all-start) | async-done | bytes 16416 | tf_op jit(solution)/shard_map/all_to_all | solution.py:227
  21.8 0.1 scale.1
  21.9 0.0 copy-start.5
  21.9 0.0 copy-start.6
  21.9 26.3 %all-gather = f32[768,128]{1,0:T(8,128)S(1)} all-gather(f32[48,128]{1,0:T(8,128)S(1)} %get-tuple-element.6.own_ref), channel_id=2, replica_groups=mesh['rep'=16,'fsdp'=32] {'rep'}, dimensions={0}, use_global_device_ids=true | all-gather | bytes 417792 | tf_op jit(solution)/shard_map/all_gather | solution.py:259
  48.2 0.0 copy-done.3
  48.2 0.0 copy-done.4
  48.2 0.0 copy-done.5
  48.2 0.0 copy-done.6
  48.2 7.1 %finish.1 = (bf16[128,3072]{1,0:T(8,128)(2,1)}, bf16[128,3072]{1,0:T(8,128)(2,1)}) custom-call(f32[48,128]{1,0:T(8,128)S(1)} %get-tuple-element.6.own_ref, f32[16,48,128]{2,1,0:T(8,128)S(1)} %bitcast.10, f32[1,128]{1,0:T(1,128)S(1)} %get-tuple-element.7.factor_ref, bf16[128,3072]{1,0:T(8,128)(2,1)S(1)} %bitcast.9, bf16[128,3072]{1,0:T(8,128)(2,1)S(1)} %bitcast.12, ...), custom_call_target="tpu_custom_call" | custom-call | tf_op jit(solution)/shard_map/finish/pallas_call | solution.py:261
  (1 shorter events, 0.0 us)
Async XLA Ops:
  0.6 1.1 %copy-start = (bf16[1,128,3072]{2,1,0:T(8,128)(2,1)S(1)}, bf16[1,128,3072]{2,1,0:T(8,128)(2,1)}, u32[]{:S(2)}) copy-start(bf16[1,128,3072]{2,1,0:T(8,128)(2,1)} %param.8) | copy-start | bytes 2359300
  1.8 11.5 %copy-start.9 = (s32[1,2,1536]{2,1,0:T(2,128)S(1)}, s32[1,2,1536]{2,1,0:T(2,128)}, u32[]{:S(2)}) copy-start(s32[1,2,1536]{2,1,0:T(2,128)} %param.10) | copy-start | bytes 36868
  1.8 11.8 %copy-start.1 = (bf16[1,128,3072]{2,1,0:T(8,128)(2,1)S(1)}, bf16[1,128,3072]{2,1,0:T(8,128)(2,1)}, u32[]{:S(2)}) copy-start(bf16[1,128,3072]{2,1,0:T(8,128)(2,1)} %param.8) | copy-start | bytes 2359300
  2.6 10.9 %copy-start.7 = (bf16[256,256]{1,0:T(8,128)(2,1)S(1)}, bf16[256,256]{1,0:T(8,128)(2,1)}, u32[]{:S(2)}) copy-start(bf16[256,256]{1,0:T(8,128)(2,1)} %constant.10.clone.pair_ref) | copy-start | bytes 393220
  2.6 19.1 %all-to-all-start = ((f32[32,1,128]{2,1,0:T(1,128)}), f32[32,1,128]{2,1,0:T(1,128)S(1)}, u32[]{:S(2)}, u32[]{:S(2)}) async-start(f32[32,1,128]{2,1,0:T(1,128)} %squares.1), calls=%async_computation | async-start | bytes 32768 | tf_op jit(solution)/shard_map/all_to_all | solution.py:227
  13.4 0.8 %copy-start.8 = (bf16[256,128]{1,0:T(8,128)(2,1)S(1)}, bf16[256,128]{1,0:T(8,128)(2,1)}, u32[]{:S(2)}) copy-start(bf16[256,128]{1,0:T(8,128)(2,1)} %constant.8.clone.forth_ref) | copy-start | bytes 196612
  14.2 1.1 %copy-start.2 = (bf16[1,128,3072]{2,1,0:T(8,128)(2,1)S(1)}, bf16[1,128,3072]{2,1,0:T(8,128)(2,1)}, u32[]{:S(2)}) copy-start(bf16[1,128,3072]{2,1,0:T(8,128)(2,1)} %param.9) | copy-start | bytes 2359300
  15.3 32.9 %copy-start.3 = (bf16[1,128,3072]{2,1,0:T(8,128)(2,1)S(1)}, bf16[1,128,3072]{2,1,0:T(8,128)(2,1)}, u32[]{:S(2)}) copy-start(bf16[1,128,3072]{2,1,0:T(8,128)(2,1)} %param.9) | copy-start | bytes 2359300
  15.4 32.9 %copy-start.4 = (bf16[128,3072]{1,0:T(8,128)(2,1)S(1)}, bf16[128,3072]{1,0:T(8,128)(2,1)}, u32[]{:S(2)}) copy-start(bf16[128,3072]{1,0:T(8,128)(2,1)} %weight_ref.1) | copy-start | bytes 2359300
  21.9 26.3 %copy-start.5 = (bf16[256,256]{1,0:T(8,128)(2,1)S(1)}, bf16[256,256]{1,0:T(8,128)(2,1)}, u32[]{:S(2)}) copy-start(bf16[256,256]{1,0:T(8,128)(2,1)} %constant.11.clone.pair_ref) | copy-start | bytes 393220
  21.9 26.3 %copy-start.6 = (bf16[256,256]{1,0:T(8,128)(2,1)S(1)}, bf16[256,256]{1,0:T(8,128)(2,1)}, u32[]{:S(2)}) copy-start(bf16[256,256]{1,0:T(8,128)(2,1)} %constant.9.clone.back_ref) | copy-start | bytes 393220

commit v3 on v2

v3 whole, which is shorter than its diff:
```python
import functools

import jax
import jax.numpy as jnp
import ml_dtypes
import numpy as np
from jax import lax
from jax.experimental import pallas as pl
from jax.experimental.pallas import tpu as pltpu
from jax.sharding import PartitionSpec as P

clip_rms = 0.5
momentum_decay = 0.9
step_rate = 0.5
VMEM = pltpu.VMEM
NN = (((1,), (0,)), ((), ()))
NT = (((1,), (1,)), ((), ()))


def split_table(table):
    high = table.astype(ml_dtypes.bfloat16)
    low = (table - high.astype(np.float64)).astype(ml_dtypes.bfloat16)
    return high, low


def tables():
    u = np.arange(64, dtype=np.float64)[:, None]
    x = np.arange(64, dtype=np.float64)[None, :]
    weight = np.where(u == 0, np.sqrt(1.0 / 64.0), np.sqrt(2.0 / 64.0))
    dct = weight * np.cos(np.pi * (2.0 * x + 1.0) * u / 128.0)
    pair = np.kron(np.eye(2), dct)
    rows = np.zeros((2, 64, 2, 2, 32))
    by_parity = dct.reshape(32, 2, 64)
    for i in range(2):
        rows[i, :, :, i, :] = by_parity.transpose(2, 1, 0)
    return pair, rows.reshape(128, 128)


def widen(table):
    high, low = split_table(table)
    return np.block([[high, high], [low, low]])


def split(value):
    high = value.astype(jnp.bfloat16)
    low = (value - high.astype(jnp.float32)).astype(jnp.bfloat16)
    return high, low


def dot(left, right, dims):
    return lax.dot_general(left, right, dims, preferred_element_type=jnp.float32)


def duplicate(packed):
    lane = lax.broadcasted_iota(jnp.int32, packed.shape, 1)
    other = pltpu.roll(packed, 64, 1)
    return jnp.where(lane < 64, packed, other), jnp.where(lane < 64, other, packed)


def block(k):
    return pl.ds(k * 128 if isinstance(k, int) else pl.multiple_of(k * 128, 128), 128)


def row(k):
    return pl.ds(k, 1)


def square_kernel(grad_ref, out_ref):
    def step(k, total):
        value = grad_ref[:, block(k)].astype(jnp.float32)
        return total + jnp.sum((value * value).reshape(-1, 8, 128), axis=0)

    total = lax.fori_loop(
        0, grad_ref.shape[1] // 128, step, jnp.zeros((8, 128), jnp.float32), unroll=8
    )
    out_ref[...] = jnp.broadcast_to(
        jnp.sum(total, axis=0, keepdims=True)[None], out_ref.shape
    )


def put_split(ref, index, value):
    high, low = split(value)
    for n in range(value.shape[1] // 128):
        ref[index, n * 128 : (n + 1) * 128, :128] = high[:, n * 128 : (n + 1) * 128]
        ref[index, n * 128 : (n + 1) * 128, 128:] = low[:, n * 128 : (n + 1) * 128]


def pick_kernel(
    grad_ref,
    moment_ref,
    where_ref,
    forth_ref,
    pair_ref,
    back_ref,
    pair_tall_ref,
    out_ref,
    rest_ref,
    at_ref,
    first_ref,
    sparse_ref,
    second_ref,
    kept_ref,
):
    groups = where_ref.shape[0]
    lane = lax.broadcasted_iota(jnp.int32, out_ref.shape[1:], 1)
    for h, offset in enumerate(duplicate((where_ref[...] & 127).astype(jnp.float32))):
        at_ref[h] = jnp.where(lane < 64, offset, offset - 64.0)
    level = lax.broadcasted_iota(jnp.int32, (64, 128), 0).astype(jnp.float32)

    def encode_rows(k):
        both = jnp.concatenate([grad_ref[:, block(k)], moment_ref[:, block(k)]], axis=1)
        first = dot(forth_ref[...], both, NN)
        put_split(first_ref, k, first[:128] + first[128:])

    def encode_columns(k):
        coeffs = dot(pair_ref[...], first_ref[k], NT)
        coeffs = coeffs[:128] + coeffs[128:]
        for h in range(2):
            hit = level == at_ref[h, row(k), :]
            for n in range(2):
                part = coeffs[h * 64 : (h + 1) * 64, n * 128 : (n + 1) * 128]
                part = jnp.where(hit, part, 0.0)
                kept_ref[n, h, row(k), :] = jnp.sum(part, axis=0, keepdims=True)
                high, low = split(part)
                at = slice(n * 128 + h * 64, n * 128 + h * 64 + 64)
                sparse_ref[k, at, :128] = high
                sparse_ref[k, at, 128:] = low

    def decode_rows(k):
        first = dot(back_ref[...], sparse_ref[k], NT)
        put_split(second_ref, k, first[:128] + first[128:])

    def decode_columns(k):
        decoded = dot(second_ref[k], pair_tall_ref[...], NN)
        decoded = decoded[:, :128] + decoded[:, 128:]
        rest_ref[0, :, block(k)] = grad_ref[:, block(k)].astype(jnp.float32) - decoded[:128]
        rest_ref[1, :, block(k)] = momentum_decay * (
            moment_ref[:, block(k)].astype(jnp.float32) - decoded[128:]
        )

    for step in (encode_rows, encode_columns, decode_rows, decode_columns):
        for k in range(groups):
            step(k)
    for n in range(2):
        front, back = kept_ref[n, 0], kept_ref[n, 1]
        front = front + pltpu.roll(front, 64, 1)
        back = back + pltpu.roll(back, 64, 1)
        out_ref[n] = jnp.where(lane < 64, front, back)


def scale_kernel(count, squares_ref, picked_ref, where_ref, factor_ref, out_ref):
    total = jnp.sum(jnp.sum(squares_ref[...], axis=0), axis=1, keepdims=True)
    mean_square = jnp.broadcast_to(total, (1, 128)) / count
    factor = jnp.minimum(1.0, clip_rms / jnp.sqrt(mean_square + 1e-06))
    factor_ref[...] = factor
    groups = where_ref.shape[0]
    out_ref[:groups] = momentum_decay * picked_ref[1] + factor * picked_ref[0]
    out_ref[groups:] = (where_ref[...] & 127).astype(jnp.float32)


def finish_kernel(
    all_ref,
    factor_ref,
    rest_ref,
    weight_ref,
    back_ref,
    pair_tall_ref,
    new_moment_ref,
    new_weight_ref,
    at_ref,
    value_ref,
    sparse_ref,
    second_ref,
    moment_out_ref,
    weight_out_ref,
    sems,
):
    replicas = all_ref.shape[0]
    groups = all_ref.shape[1] // 2
    factor = factor_ref[...]
    for k in range(groups):
        moment_out_ref[:, block(k)] = (
            rest_ref[1, :, block(k)] + factor * rest_ref[0, :, block(k)]
        ).astype(jnp.bfloat16)
    copies = [pltpu.make_async_copy(moment_out_ref, new_moment_ref, sems.at[0])]
    copies[0].start()

    lane = lax.broadcasted_iota(jnp.int32, (groups, 128), 1)
    offsets = [all_ref[r, groups:] for r in range(replicas)]
    for r in range(replicas):
        total = all_ref[r, :groups]
        for s in range(r):
            total = total + jnp.where(offsets[s] == offsets[r], all_ref[s, :groups], 0.0)
        values = duplicate(total)
        for h, offset in enumerate(duplicate(offsets[r])):
            value_ref[r, h] = values[h]
            at_ref[r, h] = jnp.where(lane < 64, offset, offset - 64.0)
    level = lax.broadcasted_iota(jnp.int32, (64, 128), 0).astype(jnp.float32)

    def scatter(t):
        for k in range(2):
            for h in range(2):
                part = jnp.zeros((64, 128), jnp.float32)
                for r in range(replicas):
                    hit = level == at_ref[r, h, row(2 * t + k), :]
                    part = jnp.where(hit, value_ref[r, h, row(2 * t + k), :], part)
                high, low = split(part)
                at = slice(k * 128 + h * 64, k * 128 + h * 64 + 64)
                sparse_ref[t, at, :128] = high
                sparse_ref[t, at, 128:] = low

    def decode_rows(t):
        first = dot(back_ref[...], sparse_ref[t], NT)
        put_split(second_ref, t, first[:128] + first[128:])

    def decode_columns(t):
        decoded = dot(second_ref[t], pair_tall_ref[...], NN)
        decoded = decoded[:, :128] + decoded[:, 128:]
        for k in range(2):
            at = block(2 * t + k)
            weight_out_ref[:, at] = (
                weight_ref[:, at].astype(jnp.float32) - step_rate * decoded[k * 128 : (k + 1) * 128]
            ).astype(jnp.bfloat16)

    pairs = groups // 2
    per_copy = max(1, pairs // 3)
    for t in range(pairs + 2):
        if t < pairs:
            scatter(t)
        if 1 <= t <= pairs:
            decode_rows(t - 1)
        if 2 <= t:
            decode_columns(t - 2)
            done = t - 1
            if done % per_copy == 0:
                at = pl.ds((done - per_copy) * 256, per_copy * 256)
                copies.append(
                    pltpu.make_async_copy(
                        weight_out_ref.at[:, at], new_weight_ref.at[:, at], sems.at[len(copies)]
                    )
                )
                copies[-1].start()
    for copy in copies:
        copy.wait()


def body(grad, momentum, kept_index, weights):
    grad, momentum = grad[0], momentum[0]
    rows, cols = grad.shape
    ring = lax.axis_size("fsdp")
    replicas = lax.axis_size("rep")
    groups = cols // 128
    pair, back = tables()
    forth = jnp.asarray(np.concatenate(split_table(back.T), axis=0))
    back_wide = jnp.asarray(widen(back))
    pair_wide = jnp.asarray(widen(pair))
    pair_tall = jnp.asarray(np.ascontiguousarray(widen(pair.T).T))
    whole = pl.BlockSpec(memory_space=VMEM)
    params = pltpu.CompilerParams(vmem_limit_bytes=32 * 1024 * 1024)

    squares = pl.pallas_call(
        square_kernel,
        out_shape=jax.ShapeDtypeStruct((ring, 1, 128), jnp.float32),
        in_specs=[whole],
        out_specs=whole,
        compiler_params=params,
        name="squares",
    )(grad)
    squares = lax.all_to_all(squares, "fsdp", 0, 0, tiled=True)

    where = kept_index[0].reshape(2, groups, 2, 32).transpose(1, 2, 0, 3).reshape(groups, 128)
    picked, rest = pl.pallas_call(
        pick_kernel,
        out_shape=(
            jax.ShapeDtypeStruct((2, groups, 128), jnp.float32),
            jax.ShapeDtypeStruct((2, rows, cols), jnp.float32),
        ),
        in_specs=[whole] * 7,
        out_specs=(whole, whole),
        scratch_shapes=[
            VMEM((2, groups, 128), jnp.float32),
            VMEM((groups, 256, 256), jnp.bfloat16),
            VMEM((groups, 256, 256), jnp.bfloat16),
            VMEM((groups, 256, 256), jnp.bfloat16),
            VMEM((2, 2, groups, 128), jnp.float32),
        ],
        compiler_params=params,
        cost_estimate=pl.CostEstimate(
            flops=2 * 2 * 20 * 128 * 128 * cols, bytes_accessed=4 * rows * cols, transcendentals=0
        ),
        name="pick",
    )(grad, momentum, where, forth, pair_wide, back_wide, pair_tall)

    factor, own = pl.pallas_call(
        functools.partial(scale_kernel, float(rows * ring * cols)),
        out_shape=(
            jax.ShapeDtypeStruct((1, 128), jnp.float32),
            jax.ShapeDtypeStruct((2 * groups, 128), jnp.float32),
        ),
        in_specs=[whole] * 3,
        out_specs=(whole, whole),
        compiler_params=params,
        name="scale",
    )(squares, picked, where)

    every = lax.all_gather(own, "rep", axis=0, tiled=False)

    hbm = pl.BlockSpec(memory_space=pl.ANY)
    new_momentum, new_weights = pl.pallas_call(
        finish_kernel,
        out_shape=(
            jax.ShapeDtypeStruct((rows, cols), jnp.bfloat16),
            jax.ShapeDtypeStruct((rows, cols), jnp.bfloat16),
        ),
        in_specs=[whole] * 6,
        out_specs=(hbm, hbm),
        scratch_shapes=[
            VMEM((replicas, 2, groups, 128), jnp.float32),
            VMEM((replicas, 2, groups, 128), jnp.float32),
            VMEM((groups // 2, 256, 256), jnp.bfloat16),
            VMEM((groups // 2, 256, 256), jnp.bfloat16),
            VMEM((rows, cols), jnp.bfloat16),
            VMEM((rows, cols), jnp.bfloat16),
            pltpu.SemaphoreType.DMA((groups // 2 + 1,)),
        ],
        compiler_params=params,
        name="finish",
    )(every, factor, rest, weights, back_wide, pair_tall)
    return (new_momentum[None], new_weights)


def solution(mesh):
    in_specs = (
        P("rep", "fsdp", None),
        P("rep", "fsdp", None),
        P("rep", "fsdp", None),
        P("fsdp", None),
    )
    out_specs = (P("rep", "fsdp", None), P("fsdp", None))
    return jax.shard_map(body, mesh=mesh, in_specs=in_specs, out_specs=out_specs, check_vma=False)
```

time: 55.6 us -> 54.9 us (0.987)
  local copies, waits for them, and re-layouts: 3.22 us -> 9.03 us
  waiting for transfers between devices: 4.49 us -> 0.01 us
  blocking collectives: 26.3 us -> 25 us
  Pallas kernels: 9.99 us -> 9.24 us
    unnamed x20, local copies, waits for them, and re-layouts: 2.98 us -> 8.09 us
    all_to_all x1, waiting for transfers between devices: 4.49 us -> 0.01 us  [body(): squares = lax.all_to_all(squares, 'fsdp', 0, 0, tiled=True)]
    pallas_call x1, Pallas kernels: 7.12 us -> 4.69 us  [body(): pl.pallas_call(finish_kernel, out_shape=(jax.ShapeDtypeStruct((rows, cols...]
    pallas_call x1, Pallas kernels: 1.91 us -> 3.58 us  [body(): pl.pallas_call(pick_kernel, out_shape=(jax.ShapeDtypeStruct((2, groups, 1...]
    all_gather x1, blocking collectives: 26.3 us -> 25 us  [body(): every = lax.all_gather(own, 'rep', axis=0, tiled=False)]
    another operation x2, local copies, waits for them, and re-layouts: 0.13 us -> 0.84 us  [body(): kept_index[0].reshape(2, groups, 2, 32).transpose(1, 2, 0, 3)]
  transfers between devices with their start and end apart: 1 -> 1, of which waited for: 1 -> 0; matrix products, arithmetic and copies ran while one was open for 0% -> 2% of each run, Pallas kernels for 3% -> 7%
where the time goes in v3:
time: 54.9 us; the launch traced here: 54.5 us
  blocking collectives  25 us (46%)
  starting transfers between devices  10.5 us (19%)
  Pallas kernels  9.24 us (17%)
  local copies, waits for them, and re-layouts  9.03 us (16%)
  between operations  0.69 us (1%)
    all_gather x1, blocking collectives, body(): every = lax.all_gather(own, 'rep', axis=0, tiled=False)  25 us
    all_to_all x1, starting transfers between devices, body(): squares = lax.all_to_all(squares, 'fsdp', 0, 0, tiled=True)  10.5 us
    unnamed x20, local copies, waits for them, and re-layouts  8.09 us
    pallas_call x1, Pallas kernels, body(): pl.pallas_call(finish_kernel, out_shape=(jax.ShapeDtypeStruct((rows, cols...  4.69 us
    pallas_call x1, Pallas kernels, body(): pl.pallas_call(pick_kernel, out_shape=(jax.ShapeDtypeStruct((2, groups, 1...  3.58 us
  transfers between devices with their start and end apart: 1, of which 0 were waited for; matrix products, arithmetic and copies ran while one was open for 2% of the time, Pallas kernels for 7%

profile of v3, /device:TPU:1, one launch (start us, length us, event | category | flops | bytes accessed | tf_op | source)
XLA Modules:
  0.0 54.5 jit_solution(16907866117187256516)
XLA Ops:
  0.6 0.0 copy-start.1
  0.6 1.1 %copy-done.1 = bf16[1,128,3072]{2,1,0:T(8,128)(2,1)S(1)} copy-done((bf16[1,128,3072]{2,1,0:T(8,128)(2,1)S(1)}, bf16[1,128,3072]{2,1,0:T(8,128)(2,1)}, u32[]{:S(2)}) %copy-start.1) | copy-done | bytes 786456
  1.8 0.8 %squares.1 = f32[32,1,128]{2,1,0:T(1,128)} custom-call(bf16[128,3072]{1,0:T(8,128)(2,1)S(1)} %bitcast.8), custom_call_target="tpu_custom_call" | custom-call | tf_op jit(solution)/shard_map/squares/pallas_call | solution.py:261
  2.6 10.5 %all-to-all-start = ((f32[32,1,128]{2,1,0:T(1,128)}), f32[32,1,128]{2,1,0:T(1,128)S(1)}, u32[]{:S(2)}, u32[]{:S(2)}) async-start(f32[32,1,128]{2,1,0:T(1,128)} %squares.1), calls=%async_computation | async-start | bytes 32768 | tf_op jit(solution)/shard_map/all_to_all | solution.py:269
  13.1 0.8 %reshape_squeeze.3 = s32[2,24,2,32]{3,2,1,0:T(2,128)S(1)} reshape(s32[1,2,1536]{2,1,0:T(2,128)} %param.10) | data formatting | bytes 24576 | tf_op jit(solution)/shard_map/reshape;squeeze | solution.py:271
  14.0 0.1 reshape.7.where_ref
  14.1 0.0 copy-start.2
  14.1 1.1 %copy-done.2 = bf16[1,128,3072]{2,1,0:T(8,128)(2,1)S(1)} copy-done((bf16[1,128,3072]{2,1,0:T(8,128)(2,1)S(1)}, bf16[1,128,3072]{2,1,0:T(8,128)(2,1)}, u32[]{:S(2)}) %copy-start.2) | copy-done | bytes 786456
  15.2 0.0 copy-start.3
  15.2 0.9 %copy-done.3 = bf16[256,256]{1,0:T(8,128)(2,1)S(1)} copy-done((bf16[256,256]{1,0:T(8,128)(2,1)S(1)}, bf16[256,256]{1,0:T(8,128)(2,1)}, u32[]{:S(2)}) %copy-start.3) | copy-done | bytes 131096
  16.1 0.0 copy-start.5
  16.1 0.9 %copy-done.5 = bf16[256,256]{1,0:T(8,128)(2,1)S(1)} copy-done((bf16[256,256]{1,0:T(8,128)(2,1)S(1)}, bf16[256,256]{1,0:T(8,128)(2,1)}, u32[]{:S(2)}) %copy-start.5) | copy-done | bytes 131096
  17.0 0.0 copy-start.7
  17.0 1.1 %copy-done.7 = bf16[1,128,3072]{2,1,0:T(8,128)(2,1)S(1)} copy-done((bf16[1,128,3072]{2,1,0:T(8,128)(2,1)S(1)}, bf16[1,128,3072]{2,1,0:T(8,128)(2,1)}, u32[]{:S(2)}) %copy-start.7) | copy-done | bytes 786456
  18.2 0.0 copy-start.8
  18.2 0.9 %copy-done.8 = bf16[256,256]{1,0:T(8,128)(2,1)S(1)} copy-done((bf16[256,256]{1,0:T(8,128)(2,1)S(1)}, bf16[256,256]{1,0:T(8,128)(2,1)}, u32[]{:S(2)}) %copy-start.8) | copy-done | bytes 131096
  19.1 0.0 copy-start.9
  19.1 0.8 %copy-done.9 = bf16[256,128]{1,0:T(8,128)(2,1)S(1)} copy-done((bf16[256,128]{1,0:T(8,128)(2,1)S(1)}, bf16[256,128]{1,0:T(8,128)(2,1)}, u32[]{:S(2)}) %copy-start.9) | copy-done | bytes 65560
  19.9 0.0 copy-start.4
  19.9 0.0 copy-start.6
  19.9 3.6 %pick.1 = (f32[2,24,128]{2,1,0:T(8,128)S(1)}, f32[2,128,3072]{2,1,0:T(8,128)S(1)}) custom-call(bf16[128,3072]{1,0:T(8,128)(2,1)S(1)} %bitcast.9, bf16[128,3072]{1,0:T(8,128)(2,1)S(1)} %bitcast.10, s32[24,128]{1,0:T(8,128)S(1)} %reshape.7.where_ref, bf16[256,128]{1,0:T(8,128)(2,1)S(1)} %copy-done.9, bf16[256,256]{1,0:T(8,128)(2,1)S(1)} %copy-done.8, ...), custom_call_target="tpu_custom_call" | custom-call | flops 4026531840 | bytes 1572864 | tf_op jit(solution)/shard_map/pick/pallas_call | solution.py:272
  23.5 0.0 all-to-all-done.squares_ref
  23.5 0.1 scale.1
  23.6 25.0 %all-gather = f32[768,128]{1,0:T(8,128)S(1)} all-gather(f32[48,128]{1,0:T(8,128)S(1)} %get-tuple-element.9), channel_id=2, replica_groups=mesh['rep'=16,'fsdp'=32] {'rep'}, dimensions={0}, use_global_device_ids=true | all-gather | bytes 417792 | tf_op jit(solution)/shard_map/all_gather | solution.py:306
  48.6 0.0 copy-done.4
  48.6 0.0 copy-done.6
  48.6 0.0 copy-start
  48.6 1.1 %copy-done = bf16[128,3072]{1,0:T(8,128)(2,1)S(1)} copy-done((bf16[128,3072]{1,0:T(8,128)(2,1)S(1)}, bf16[128,3072]{1,0:T(8,128)(2,1)}, u32[]{:S(2)}) %copy-start) | copy-done | bytes 786456
  49.8 4.7 %finish.1 = (bf16[128,3072]{1,0:T(8,128)(2,1)}, bf16[128,3072]{1,0:T(8,128)(2,1)}) custom-call(f32[16,48,128]{2,1,0:T(8,128)S(1)} %bitcast.7, f32[1,128]{1,0:T(1,128)S(1)} %get-tuple-element.10.factor_ref, f32[2,128,3072]{2,1,0:T(8,128)S(1)} %get-tuple-element.11.rest_ref, bf16[128,3072]{1,0:T(8,128)(2,1)S(1)} %copy-done, bf16[256,256]{1,0:T(8,128)(2,1)S(1)} %copy-done.6, ...), custom_call_target="tpu_custom_call" | custom-call | tf_op jit(solution)/shard_map/finish/pallas_call | solution.py:309
  (1 shorter events, 0.0 us)
Async XLA Ops:
  0.6 1.1 %copy-start.1 = (bf16[1,128,3072]{2,1,0:T(8,128)(2,1)S(1)}, bf16[1,128,3072]{2,1,0:T(8,128)(2,1)}, u32[]{:S(2)}) copy-start(bf16[1,128,3072]{2,1,0:T(8,128)(2,1)} %param.8) | copy-start | bytes 2359300
  2.6 20.9 %all-to-all-start = ((f32[32,1,128]{2,1,0:T(1,128)}), f32[32,1,128]{2,1,0:T(1,128)S(1)}, u32[]{:S(2)}, u32[]{:S(2)}) async-start(f32[32,1,128]{2,1,0:T(1,128)} %squares.1), calls=%async_computation | async-start | bytes 32768 | tf_op jit(solution)/shard_map/all_to_all | solution.py:269
  14.1 1.1 %copy-start.2 = (bf16[1,128,3072]{2,1,0:T(8,128)(2,1)S(1)}, bf16[1,128,3072]{2,1,0:T(8,128)(2,1)}, u32[]{:S(2)}) copy-start(bf16[1,128,3072]{2,1,0:T(8,128)(2,1)} %param.8) | copy-start | bytes 2359300
  15.2 0.9 %copy-start.3 = (bf16[256,256]{1,0:T(8,128)(2,1)S(1)}, bf16[256,256]{1,0:T(8,128)(2,1)}, u32[]{:S(2)}) copy-start(bf16[256,256]{1,0:T(8,128)(2,1)} %constant.11.clone.pair_tall_ref) | copy-start | bytes 393220
  16.1 0.9 %copy-start.5 = (bf16[256,256]{1,0:T(8,128)(2,1)S(1)}, bf16[256,256]{1,0:T(8,128)(2,1)}, u32[]{:S(2)}) copy-start(bf16[256,256]{1,0:T(8,128)(2,1)} %constant.9.clone.back_ref) | copy-start | bytes 393220
  17.0 1.1 %copy-start.7 = (bf16[1,128,3072]{2,1,0:T(8,128)(2,1)S(1)}, bf16[1,128,3072]{2,1,0:T(8,128)(2,1)}, u32[]{:S(2)}) copy-start(bf16[1,128,3072]{2,1,0:T(8,128)(2,1)} %param.9) | copy-start | bytes 2359300
  18.2 0.9 %copy-start.8 = (bf16[256,256]{1,0:T(8,128)(2,1)S(1)}, bf16[256,256]{1,0:T(8,128)(2,1)}, u32[]{:S(2)}) copy-start(bf16[256,256]{1,0:T(8,128)(2,1)} %constant.10.clone.pair_ref) | copy-start | bytes 393220
  19.1 0.8 %copy-start.9 = (bf16[256,128]{1,0:T(8,128)(2,1)S(1)}, bf16[256,128]{1,0:T(8,128)(2,1)}, u32[]{:S(2)}) copy-start(bf16[256,128]{1,0:T(8,128)(2,1)} %constant.8.clone.forth_ref) | copy-start | bytes 196612
  19.9 28.7 %copy-start.4 = (bf16[256,256]{1,0:T(8,128)(2,1)S(1)}, bf16[256,256]{1,0:T(8,128)(2,1)}, u32[]{:S(2)}) copy-start(bf16[256,256]{1,0:T(8,128)(2,1)} %constant.11.clone.pair_tall_ref) | copy-start | bytes 393220
  19.9 28.7 %copy-start.6 = (bf16[256,256]{1,0:T(8,128)(2,1)S(1)}, bf16[256,256]{1,0:T(8,128)(2,1)}, u32[]{:S(2)}) copy-start(bf16[256,256]{1,0:T(8,128)(2,1)} %constant.9.clone.back_ref) | copy-start | bytes 393220
  48.6 1.1 %copy-start = (bf16[128,3072]{1,0:T(8,128)(2,1)S(1)}, bf16[128,3072]{1,0:T(8,128)(2,1)}, u32[]{:S(2)}) copy-start(bf16[128,3072]{1,0:T(8,128)(2,1)} %weight_ref.1) | copy-start | bytes 2359300

commit v4 on v3

--- a/solution.py
+++ b/solution.py
@@ -86,21 +86,46 @@
 
 
 def pick_kernel(
+    where_ref,
+    grad_hbm,
+    moment_hbm,
+    forth_hbm,
+    pair_hbm,
+    back_hbm,
+    pair_tall_hbm,
+    weight_hbm,
+    out_ref,
+    rest_ref,
+    weight_ref,
+    back_ref,
+    pair_tall_ref,
     grad_ref,
     moment_ref,
-    where_ref,
     forth_ref,
     pair_ref,
-    back_ref,
-    pair_tall_ref,
-    out_ref,
-    rest_ref,
+    sems,
     at_ref,
     first_ref,
     sparse_ref,
     second_ref,
     kept_ref,
 ):
+    copies = [
+        pltpu.make_async_copy(source, target, sems.at[n])
+        for n, (source, target) in enumerate(
+            (
+                (forth_hbm, forth_ref),
+                (grad_hbm, grad_ref),
+                (moment_hbm, moment_ref),
+                (pair_hbm, pair_ref),
+                (back_hbm, back_ref),
+                (pair_tall_hbm, pair_tall_ref),
+                (weight_hbm, weight_ref),
+            )
+        )
+    ]
+    for copy in copies:
+        copy.start()
     groups = where_ref.shape[0]
     lane = lax.broadcasted_iota(jnp.int32, out_ref.shape[1:], 1)
     for h, offset in enumerate(duplicate((where_ref[...] & 127).astype(jnp.float32))):
@@ -138,7 +163,14 @@
             moment_ref[:, block(k)].astype(jnp.float32) - decoded[128:]
         )
 
-    for step in (encode_rows, encode_columns, decode_rows, decode_columns):
+    for needed, step in (
+        (copies[:3], encode_rows),
+        (copies[3:4], encode_columns),
+        (copies[4:5], decode_rows),
+        (copies[5:], decode_columns),
+    ):
+        for copy in needed:
+            copy.wait()
         for k in range(groups):
             step(k)
     for n in range(2):
@@ -269,15 +301,24 @@
     squares = lax.all_to_all(squares, "fsdp", 0, 0, tiled=True)
 
     where = kept_index[0].reshape(2, groups, 2, 32).transpose(1, 2, 0, 3).reshape(groups, 128)
-    picked, rest = pl.pallas_call(
+    hbm = pl.BlockSpec(memory_space=pltpu.HBM)
+    picked, rest, weights_near, back_near, tall_near = pl.pallas_call(
         pick_kernel,
         out_shape=(
             jax.ShapeDtypeStruct((2, groups, 128), jnp.float32),
             jax.ShapeDtypeStruct((2, rows, cols), jnp.float32),
+            jax.ShapeDtypeStruct((rows, cols), jnp.bfloat16),
+            jax.ShapeDtypeStruct((256, 256), jnp.bfloat16),
+            jax.ShapeDtypeStruct((256, 256), jnp.bfloat16),
         ),
-        in_specs=[whole] * 7,
-        out_specs=(whole, whole),
+        in_specs=[whole] + [hbm] * 7,
+        out_specs=(whole,) * 5,
         scratch_shapes=[
+            VMEM((rows, cols), jnp.bfloat16),
+            VMEM((rows, cols), jnp.bfloat16),
+            VMEM((256, 128), jnp.bfloat16),
+            VMEM((256, 256), jnp.bfloat16),
+            pltpu.SemaphoreType.DMA((7,)),
             VMEM((2, groups, 128), jnp.float32),
             VMEM((groups, 256, 256), jnp.bfloat16),
             VMEM((groups, 256, 256), jnp.bfloat16),
@@ -289,7 +330,7 @@
             flops=2 * 2 * 20 * 128 * 128 * cols, bytes_accessed=4 * rows * cols, transcendentals=0
         ),
         name="pick",
-    )(grad, momentum, where, forth, pair_wide, back_wide, pair_tall)
+    )(where, *(pltpu.with_memory_space_constraint(t, pltpu.HBM) for t in (grad, momentum, forth, pair_wide, back_wide, pair_tall, weights)))
 
     factor, own = pl.pallas_call(
         functools.partial(scale_kernel, float(rows * ring * cols)),
@@ -305,7 +346,6 @@
 
     every = lax.all_gather(own, "rep", axis=0, tiled=False)
 
-    hbm = pl.BlockSpec(memory_space=pl.ANY)
     new_momentum, new_weights = pl.pallas_call(
         finish_kernel,
         out_shape=(
@@ -325,7 +365,7 @@
         ],
         compiler_params=params,
         name="finish",
-    )(every, factor, rest, weights, back_wide, pair_tall)
+    )(every, factor, rest, weights_near, back_near, tall_near)
     return (new_momentum[None], new_weights)
 
 

time: 54.9 us -> 54 us (0.984)
  local copies, waits for them, and re-layouts: 9.03 us -> 4.08 us
  Pallas kernels: 9.24 us -> 11.2 us
  blocking collectives: 25 us -> 26.2 us
  waiting for transfers between devices: 0.01 us -> 1.09 us
    unnamed x20 -> x6, local copies, waits for them, and re-layouts: 8.09 us -> 3.14 us
    pallas_call x1, Pallas kernels: 3.58 us -> 5.57 us  [body(): pl.pallas_call(pick_kernel, out_shape=(jax.ShapeDtypeStruct((2, groups, 1...]
    all_gather x1, blocking collectives: 25 us -> 26.2 us  [body(): every = lax.all_gather(own, 'rep', axis=0, tiled=False)]
    all_to_all x1, waiting for transfers between devices: 0.01 us -> 1.09 us  [body(): squares = lax.all_to_all(squares, 'fsdp', 0, 0, tiled=True)]
  transfers between devices with their start and end apart: 1 -> 1, of which waited for: 0 -> 1; matrix products, arithmetic and copies ran while one was open for 2% -> 2% of each run, Pallas kernels for 7% -> 10%
where the time goes in v4:
time: 54 us; the launch traced here: 53.7 us
  blocking collectives  26.2 us (49%)
  Pallas kernels  11.2 us (21%)
  starting transfers between devices  10.5 us (19%)
  local copies, waits for them, and re-layouts  4.08 us (8%)
  waiting for transfers between devices  1.09 us (2%)
  between operations  0.68 us (1%)
    all_gather x1, blocking collectives, body(): every = lax.all_gather(own, 'rep', axis=0, tiled=False)  26.2 us
    all_to_all x1, starting transfers between devices, body(): squares = lax.all_to_all(squares, 'fsdp', 0, 0, tiled=True)  10.5 us
    pallas_call x1, Pallas kernels, body(): pl.pallas_call(pick_kernel, out_shape=(jax.ShapeDtypeStruct((2, groups, 1...  5.57 us
    pallas_call x1, Pallas kernels, body(): pl.pallas_call(finish_kernel, out_shape=(jax.ShapeDtypeStruct((rows, cols...  4.67 us
    unnamed x6, local copies, waits for them, and re-layouts  3.14 us
    all_to_all x1, waiting for transfers between devices, body(): squares = lax.all_to_all(squares, 'fsdp', 0, 0, tiled=True)  1.09 us
  transfers between devices with their start and end apart: 1, of which 1 were waited for; matrix products, arithmetic and copies ran while one was open for 2% of the time, Pallas kernels for 10%

profile of v4, /device:TPU:1, one launch (start us, length us, event | category | flops | bytes accessed | tf_op | source)
XLA Modules:
  0.0 53.7 jit_solution(2569012616201323954)
XLA Ops:
  0.6 0.0 copy-start.2
  0.6 1.1 %copy-done.2 = bf16[1,128,3072]{2,1,0:T(8,128)(2,1)S(1)} copy-done((bf16[1,128,3072]{2,1,0:T(8,128)(2,1)S(1)}, bf16[1,128,3072]{2,1,0:T(8,128)(2,1)}, u32[]{:S(2)}) %copy-start.2) | copy-done | bytes 786456
  1.8 0.8 %squares.1 = f32[32,1,128]{2,1,0:T(1,128)} custom-call(bf16[128,3072]{1,0:T(8,128)(2,1)S(1)} %bitcast.9), custom_call_target="tpu_custom_call" | custom-call | tf_op jit(solution)/shard_map/squares/pallas_call | solution.py:293
  2.6 10.5 %all-to-all-start = ((f32[32,1,128]{2,1,0:T(1,128)}), f32[32,1,128]{2,1,0:T(1,128)S(1)}, u32[]{:S(2)}, u32[]{:S(2)}) async-start(f32[32,1,128]{2,1,0:T(1,128)} %squares.1), calls=%async_computation | async-start | bytes 32768 | tf_op jit(solution)/shard_map/all_to_all | solution.py:301
  13.1 0.8 %reshape_squeeze.3 = s32[2,24,2,32]{3,2,1,0:T(2,128)S(1)} reshape(s32[1,2,1536]{2,1,0:T(2,128)} %param.10) | data formatting | bytes 24576 | tf_op jit(solution)/shard_map/reshape;squeeze | solution.py:303
  14.0 0.1 reshape.7.where_ref
  14.1 5.6 %pick.1 = (f32[2,24,128]{2,1,0:T(8,128)S(1)}, f32[2,128,3072]{2,1,0:T(8,128)S(1)}, bf16[128,3072]{1,0:T(8,128)(2,1)S(1)}, bf16[256,256]{1,0:T(8,128)(2,1)S(1)}, bf16[256,256]{1,0:T(8,128)(2,1)S(1)}) custom-call(s32[24,128]{1,0:T(8,128)S(1)} %reshape.7.where_ref, bf16[128,3072]{1,0:T(8,128)(2,1)} %bitcast.8, bf16[128,3072]{1,0:T(8,128)(2,1)} %bitcast.11, ...), custom_call_target="tpu_custom_call" | custom-call | flops 4026531840 | bytes 1572864 | tf_op jit(solution)/shard_map/pick/pallas_call | solution.py:305
  19.6 0.0 copy-start
  19.7 0.9 %copy-done = bf16[128,3072]{1,0:T(8,128)(2,1)} copy-done((bf16[128,3072]{1,0:T(8,128)(2,1)}, bf16[128,3072]{1,0:T(8,128)(2,1)S(1)}, u32[]{:S(2)}) %copy-start) | copy-done | bytes 786456
  20.5 1.1 %all-to-all-done.squares_ref = f32[32,1,128]{2,1,0:T(1,128)S(1)} async-done(((f32[32,1,128]{2,1,0:T(1,128)}), f32[32,1,128]{2,1,0:T(1,128)S(1)}, u32[]{:S(2)}, u32[]{:S(2)}) %all-to-all-start) | async-done | bytes 16416 | tf_op jit(solution)/shard_map/all_to_all | solution.py:301
  21.6 0.1 scale.1
  21.7 26.2 %all-gather = f32[768,128]{1,0:T(8,128)S(1)} all-gather(f32[48,128]{1,0:T(8,128)S(1)} %get-tuple-element.12), channel_id=2, replica_groups=mesh['rep'=16,'fsdp'=32] {'rep'}, dimensions={0}, use_global_device_ids=true | all-gather | bytes 417792 | tf_op jit(solution)/shard_map/all_gather | solution.py:347
  47.9 0.0 copy-start.1
  47.9 1.1 %copy-done.1 = bf16[128,3072]{1,0:T(8,128)(2,1)S(1)} copy-done((bf16[128,3072]{1,0:T(8,128)(2,1)S(1)}, bf16[128,3072]{1,0:T(8,128)(2,1)}, u32[]{:S(2)}) %copy-start.1) | copy-done | bytes 786456
  49.0 4.7 %finish.1 = (bf16[128,3072]{1,0:T(8,128)(2,1)}, bf16[128,3072]{1,0:T(8,128)(2,1)}) custom-call(f32[16,48,128]{2,1,0:T(8,128)S(1)} %bitcast.7, f32[1,128]{1,0:T(1,128)S(1)} %get-tuple-element.13.factor_ref, f32[2,128,3072]{2,1,0:T(8,128)S(1)} %get-tuple-element.14.rest_ref, bf16[128,3072]{1,0:T(8,128)(2,1)S(1)} %copy-done.1, ...), custom_call_target="tpu_custom_call" | custom-call | tf_op jit(solution)/shard_map/finish/pallas_call | solution.py:349
  (1 shorter events, 0.0 us)
Async XLA Ops:
  0.6 1.1 %copy-start.2 = (bf16[1,128,3072]{2,1,0:T(8,128)(2,1)S(1)}, bf16[1,128,3072]{2,1,0:T(8,128)(2,1)}, u32[]{:S(2)}) copy-start(bf16[1,128,3072]{2,1,0:T(8,128)(2,1)} %param.8) | copy-start | bytes 2359300
  2.6 19.0 %all-to-all-start = ((f32[32,1,128]{2,1,0:T(1,128)}), f32[32,1,128]{2,1,0:T(1,128)S(1)}, u32[]{:S(2)}, u32[]{:S(2)}) async-start(f32[32,1,128]{2,1,0:T(1,128)} %squares.1), calls=%async_computation | async-start | bytes 32768 | tf_op jit(solution)/shard_map/all_to_all | solution.py:301
  19.6 0.9 %copy-start = (bf16[128,3072]{1,0:T(8,128)(2,1)}, bf16[128,3072]{1,0:T(8,128)(2,1)S(1)}, u32[]{:S(2)}) copy-start(bf16[128,3072]{1,0:T(8,128)(2,1)S(1)} %get-tuple-element.15.weight_ref) | copy-start | bytes 2359300
  47.9 1.1 %copy-start.1 = (bf16[128,3072]{1,0:T(8,128)(2,1)S(1)}, bf16[128,3072]{1,0:T(8,128)(2,1)}, u32[]{:S(2)}) copy-start(bf16[128,3072]{1,0:T(8,128)(2,1)} %copy-done) | copy-start | bytes 2359300

commit v5 on v2

v5 whole, which is shorter than its diff:
```python
import functools

import jax
import jax.numpy as jnp
import ml_dtypes
import numpy as np
from jax import lax
from jax.experimental import pallas as pl
from jax.experimental.pallas import tpu as pltpu
from jax.sharding import PartitionSpec as P

clip_rms = 0.5
momentum_decay = 0.9
step_rate = 0.5
VMEM = pltpu.VMEM
PARTS = 6
NN = (((1,), (0,)), ((), ()))
NT = (((1,), (1,)), ((), ()))


def split_table(table):
    high = table.astype(ml_dtypes.bfloat16)
    low = (table - high.astype(np.float64)).astype(ml_dtypes.bfloat16)
    return high, low


def tables():
    u = np.arange(64, dtype=np.float64)[:, None]
    x = np.arange(64, dtype=np.float64)[None, :]
    weight = np.where(u == 0, np.sqrt(1.0 / 64.0), np.sqrt(2.0 / 64.0))
    dct = weight * np.cos(np.pi * (2.0 * x + 1.0) * u / 128.0)
    pair = np.kron(np.eye(2), dct)
    rows = np.zeros((2, 64, 2, 2, 32))
    by_parity = dct.reshape(32, 2, 64)
    for i in range(2):
        rows[i, :, :, i, :] = by_parity.transpose(2, 1, 0)
    return pair, rows.reshape(128, 128)


def widen(table):
    high, low = split_table(table)
    return np.block([[high, high], [low, low]])


def split(value):
    high = value.astype(jnp.bfloat16)
    low = (value - high.astype(jnp.float32)).astype(jnp.bfloat16)
    return high, low


def dot(left, right, dims):
    return lax.dot_general(left, right, dims, preferred_element_type=jnp.float32)


def duplicate(packed):
    lane = lax.broadcasted_iota(jnp.int32, packed.shape, 1)
    other = pltpu.roll(packed, 64, 1)
    return jnp.where(lane < 64, packed, other), jnp.where(lane < 64, other, packed)


def block(k):
    return pl.ds(k * 128 if isinstance(k, int) else pl.multiple_of(k * 128, 128), 128)


def row(k):
    return pl.ds(k, 1)


def in_hbm(*arrays):
    return [pltpu.with_memory_space_constraint(array, pltpu.HBM) for array in arrays]


def put_split(ref, value):
    high, low = split(value)
    for n in range(value.shape[1] // 128):
        ref[n * 128 : (n + 1) * 128, :128] = high[:, n * 128 : (n + 1) * 128]
        ref[n * 128 : (n + 1) * 128, 128:] = low[:, n * 128 : (n + 1) * 128]


def fetch_kernel(grad_hbm, *refs):
    count = (len(refs) - 3) // 2
    sources, (out_ref, grad_ref), (targets, sems) = refs[:count], refs[count : count + 2], (refs[count + 2 : -1], refs[-1])
    copies = [
        pltpu.make_async_copy(source, target, sems.at[n])
        for n, (source, target) in enumerate(zip((grad_hbm, *sources), (grad_ref, *targets)))
    ]
    for copy in copies:
        copy.start()
    copies[0].wait()

    def step(k, total):
        value = grad_ref[:, block(k)].astype(jnp.float32)
        return total + jnp.sum((value * value).reshape(-1, 8, 128), axis=0)

    total = lax.fori_loop(
        0, grad_ref.shape[1] // 128, step, jnp.zeros((8, 128), jnp.float32), unroll=8
    )
    out_ref[...] = jnp.broadcast_to(
        jnp.sum(total, axis=0, keepdims=True)[None], out_ref.shape
    )
    for copy in copies[1:]:
        copy.wait()


def pick_kernel(
    where_ref, grad_ref, moment_ref, forth_ref, pair_ref, out_ref, at_ref, first_ref, kept_ref
):
    groups = where_ref.shape[0]
    lane = lax.broadcasted_iota(jnp.int32, out_ref.shape[1:], 1)
    for h, offset in enumerate(duplicate((where_ref[...] & 127).astype(jnp.float32))):
        at_ref[h] = jnp.where(lane < 64, offset, offset - 64.0)
    level = lax.broadcasted_iota(jnp.int32, (64, 128), 0).astype(jnp.float32)

    def over_rows(k):
        both = jnp.concatenate([grad_ref[:, block(k)], moment_ref[:, block(k)]], axis=1)
        first = dot(forth_ref[...], both, NN)
        put_split(first_ref.at[k], first[:128] + first[128:])

    def over_columns(k):
        coeffs = dot(pair_ref[...], first_ref[k], NT)
        coeffs = coeffs[:128] + coeffs[128:]
        for h in range(2):
            hit = level == at_ref[h, row(k), :]
            for n in range(2):
                part = coeffs[h * 64 : (h + 1) * 64, n * 128 : (n + 1) * 128]
                kept_ref[n, h, row(k), :] = jnp.sum(
                    jnp.where(hit, part, 0.0), axis=0, keepdims=True
                )

    for step in (over_rows, over_columns):
        for k in range(groups):
            step(k)
    for n in range(2):
        front, back = kept_ref[n, 0], kept_ref[n, 1]
        front = front + pltpu.roll(front, 64, 1)
        back = back + pltpu.roll(back, 64, 1)
        out_ref[n] = jnp.where(lane < 64, front, back)


def scale_kernel(count, squares_ref, picked_ref, where_ref, factor_ref, own_ref, send_ref):
    total = jnp.sum(jnp.sum(squares_ref[...], axis=0), axis=1, keepdims=True)
    mean_square = jnp.broadcast_to(total, (1, 128)) / count
    factor = jnp.minimum(1.0, clip_rms / jnp.sqrt(mean_square + 1e-06))
    factor_ref[...] = factor
    values = momentum_decay * picked_ref[1] + factor * picked_ref[0]
    listing = jnp.concatenate([values, (where_ref[...] & 127).astype(jnp.float32)], axis=0)
    own_ref[...] = listing
    send_ref[...] = jnp.broadcast_to(listing[None], send_ref.shape)


def unpack(listings, at_ref, value_ref):
    groups = at_ref.shape[2]
    lane = lax.broadcasted_iota(jnp.int32, (groups, 128), 1)
    offsets = [listing[groups:] for listing in listings]
    for r in range(len(listings)):
        total = listings[r][:groups]
        for s in range(r):
            total = total + jnp.where(offsets[s] == offsets[r], listings[s][:groups], 0.0)
        values = duplicate(total)
        for h, offset in enumerate(duplicate(offsets[r])):
            value_ref[r, h] = values[h]
            at_ref[r, h] = jnp.where(lane < 64, offset, offset - 64.0)


def decode(at_ref, value_ref, sparse_ref, second_ref, back_ref, tall_ref, ready, emit):
    lists, _, groups, _ = at_ref.shape
    level = lax.broadcasted_iota(jnp.int32, (64, 128), 0).astype(jnp.float32)

    def scatter(t, carry):
        for k in range(2):
            for h in range(2):
                part = jnp.zeros((64, 128), jnp.float32)
                for r in range(lists):
                    hit = level == at_ref[r, h, row(2 * t + k), :]
                    part = jnp.where(hit, value_ref[r, h, row(2 * t + k), :], part)
                high, low = split(part)
                at = slice(k * 128 + h * 64, k * 128 + h * 64 + 64)
                sparse_ref[t, at, :128] = high
                sparse_ref[t, at, 128:] = low
        return carry

    lax.fori_loop(0, groups // 2, scatter, 0)
    for copy in ready:
        copy.wait()
    for t in range(groups // 2):
        first = dot(back_ref[...], sparse_ref[t], NT)
        put_split(second_ref.at[t], first[:128] + first[128:])
    for t in range(groups // 2):
        decoded = dot(second_ref[t], tall_ref[...], NN)
        decoded = decoded[:, :128] + decoded[:, 128:]
        for k in range(2):
            emit(2 * t + k, decoded[k * 128 : (k + 1) * 128])


def fetch(sems, *pairs):
    copies = [pltpu.make_async_copy(source, target, sems.at[n]) for n, (source, target) in enumerate(pairs)]
    for copy in copies:
        copy.start()
    return copies


class Outlet:
    def __init__(self, source, target, sems, first_sem):
        self.source, self.target, self.sems, self.first_sem = source, target, sems, first_sem
        self.per = max(2, source.shape[1] // 128 // PARTS)
        self.copies = []

    def put(self, k, value):
        self.source[:, block(k)] = value.astype(self.source.dtype)
        if (k + 1) % self.per == 0:
            at = pl.ds((k + 1 - self.per) * 128, self.per * 128)
            copy = pltpu.make_async_copy(
                self.source.at[:, at],
                self.target.at[:, at],
                self.sems.at[self.first_sem + len(self.copies)],
            )
            copy.start()
            self.copies.append(copy)

    def wait(self):
        for copy in self.copies:
            copy.wait()


def own_kernel(
    own_ref, factor_ref, grad_ref, moment_ref, back_hbm, tall_hbm, new_moment_hbm,
    back_ref, tall_ref, at_ref, value_ref, sparse_ref, second_ref, out_ref, sems,
):
    ready = fetch(sems, (back_hbm, back_ref), (tall_hbm, tall_ref))
    factor = factor_ref[...]
    unpack([own_ref[...]], at_ref, value_ref)
    outlet = Outlet(out_ref, new_moment_hbm, sems, 2)

    def emit(k, decoded):
        blended = momentum_decay * moment_ref[:, block(k)].astype(jnp.float32)
        blended = blended + factor * grad_ref[:, block(k)].astype(jnp.float32)
        outlet.put(k, blended - decoded)

    decode(at_ref, value_ref, sparse_ref, second_ref, back_ref, tall_ref, ready, emit)
    outlet.wait()


def finish_kernel(
    all_ref, back_hbm, tall_hbm, weight_hbm, new_weight_hbm,
    back_ref, tall_ref, weight_ref, at_ref, value_ref, sparse_ref, second_ref, out_ref, sems,
):
    ready = fetch(sems, (back_hbm, back_ref), (tall_hbm, tall_ref), (weight_hbm, weight_ref))
    unpack([all_ref[r] for r in range(all_ref.shape[0])], at_ref, value_ref)
    outlet = Outlet(out_ref, new_weight_hbm, sems, 3)

    def emit(k, decoded):
        outlet.put(k, weight_ref[:, block(k)].astype(jnp.float32) - step_rate * decoded)

    decode(at_ref, value_ref, sparse_ref, second_ref, back_ref, tall_ref, ready, emit)
    outlet.wait()


def ring_order(size):
    head = size // 2 + 2 if size == 32 else 0
    return [head] + [member for member in range(size) if member != head]


def replica_order(size):
    return [chip * 2 + core for chip in range(size // 2 - 1, -1, -1) for core in range(2)]


def body(grad, momentum, kept_index, weights):
    grad, momentum = grad[0], momentum[0]
    rows, cols = grad.shape
    ring = lax.axis_size("fsdp")
    replicas = lax.axis_size("rep")
    groups = cols // 128
    bf16, f32 = jnp.bfloat16, jnp.float32
    pair, back = tables()
    forth = jnp.asarray(np.concatenate(split_table(back.T), axis=0))
    back_wide = jnp.asarray(widen(back))
    pair_wide = jnp.asarray(widen(pair))
    pair_tall = jnp.asarray(np.ascontiguousarray(widen(pair.T).T))
    whole = pl.BlockSpec(memory_space=VMEM)
    hbm = pl.BlockSpec(memory_space=pl.ANY)
    params = pltpu.CompilerParams(vmem_limit_bytes=32 * 1024 * 1024)
    full = jax.ShapeDtypeStruct((rows, cols), bf16)
    square = jax.ShapeDtypeStruct((256, 256), bf16)

    squares, grad_near, moment_near, kept_near, forth_near, pair_near = pl.pallas_call(
        fetch_kernel,
        out_shape=(
            jax.ShapeDtypeStruct((ring, 1, 128), f32),
            full,
            full,
            jax.ShapeDtypeStruct(kept_index.shape[1:], jnp.int32),
            jax.ShapeDtypeStruct((256, 128), bf16),
            square,
        ),
        in_specs=[hbm] * 5,
        out_specs=(whole,) * 6,
        scratch_shapes=[pltpu.SemaphoreType.DMA((5,))],
        compiler_params=params,
        name="fetch",
    )(*in_hbm(grad, momentum, kept_index[0], forth, pair_wide))
    squares = lax.all_to_all(
        squares, "fsdp", 0, 0, tiled=True, axis_index_groups=[ring_order(ring)]
    )

    where = kept_near.reshape(2, groups, 2, 32).transpose(1, 2, 0, 3).reshape(groups, 128)
    picked = pl.pallas_call(
        pick_kernel,
        out_shape=jax.ShapeDtypeStruct((2, groups, 128), f32),
        in_specs=[whole] * 5,
        out_specs=whole,
        scratch_shapes=[
            VMEM((2, groups, 128), f32),
            VMEM((groups, 256, 256), bf16),
            VMEM((2, 2, groups, 128), f32),
        ],
        compiler_params=params,
        cost_estimate=pl.CostEstimate(
            flops=2 * 2 * 10 * 128 * 128 * cols, bytes_accessed=4 * rows * cols, transcendentals=0
        ),
        name="pick",
    )(where, grad_near, moment_near, forth_near, pair_near)

    factor, own, send = pl.pallas_call(
        functools.partial(scale_kernel, float(rows * ring * cols)),
        out_shape=(
            jax.ShapeDtypeStruct((1, 128), f32),
            jax.ShapeDtypeStruct((2 * groups, 128), f32),
            jax.ShapeDtypeStruct((replicas, 2 * groups, 128), f32),
        ),
        in_specs=[whole] * 3,
        out_specs=(whole,) * 3,
        compiler_params=params,
        name="scale",
    )(squares, picked, where)

    every = lax.all_to_all(
        send, "rep", 0, 0, tiled=True, axis_index_groups=[replica_order(replicas)]
    )

    def work(lists):
        return [
            VMEM((lists, 2, groups, 128), f32),
            VMEM((lists, 2, groups, 128), f32),
            VMEM((groups // 2, 256, 256), bf16),
            VMEM((groups // 2, 256, 256), bf16),
            VMEM((rows, cols), bf16),
            pltpu.SemaphoreType.DMA((3 + groups // 2,)),
        ]

    new_momentum = pl.pallas_call(
        own_kernel,
        out_shape=full,
        in_specs=[whole] * 4 + [hbm] * 2,
        out_specs=hbm,
        scratch_shapes=[VMEM((256, 256), bf16)] * 2 + work(1),
        compiler_params=params,
        cost_estimate=pl.CostEstimate(
            flops=2 * 2 * 10 * 128 * 128 * cols, bytes_accessed=4 * rows * cols, transcendentals=0
        ),
        name="own",
    )(own, factor, grad_near, moment_near, *in_hbm(back_wide, pair_tall))

    new_weights = pl.pallas_call(
        finish_kernel,
        out_shape=full,
        in_specs=[whole] + [hbm] * 3,
        out_specs=hbm,
        scratch_shapes=[VMEM((256, 256), bf16)] * 2 + [VMEM((rows, cols), bf16)] + work(replicas),
        compiler_params=params,
        name="finish",
    )(every, *in_hbm(back_wide, pair_tall, weights))
    return (new_momentum[None], new_weights)


def solution(mesh):
    in_specs = (
        P("rep", "fsdp", None),
        P("rep", "fsdp", None),
        P("rep", "fsdp", None),
        P("fsdp", None),
    )
    out_specs = (P("rep", "fsdp", None), P("fsdp", None))
    return jax.shard_map(body, mesh=mesh, in_specs=in_specs, out_specs=out_specs, check_vma=False)
```

time: 55.6 us -> 46.3 us (0.83)
  blocking collectives: 26.3 us -> 0 us
  starting transfers between devices: 10.6 us -> 25.6 us
  waiting for transfers between devices: 4.49 us -> 7.83 us
  local copies, waits for them, and re-layouts: 3.22 us -> 0.24 us
  Pallas kernels: 9.99 us -> 11.6 us
    all_gather x1 -> x0, blocking collectives: 26.3 us -> none  [body(): every = lax.all_gather(own, 'rep', axis=0, tiled=False)]
    all_to_all x1 -> x2, starting transfers between devices: 10.6 us -> 25.6 us  [the longest x1 13.3 us: body(): lax.all_to_all(send, 'rep', 0, 0, tiled=True, axis_index_groups=[replica_...]
    all_to_all x1 -> x2, waiting for transfers between devices: 4.49 us -> 7.83 us  [the longest x1 7.83 us: body(): lax.all_to_all(send, 'rep', 0, 0, tiled=True, axis_index_groups=[replica_...]
    unnamed x20 -> x0, local copies, waits for them, and re-layouts: 2.98 us -> none
    pallas_call x2 -> x3, Pallas kernels: 7.96 us -> 8.84 us  [the longest x1 3.99 us: body(): pl.pallas_call(finish_kernel, out_shape=full, in_specs=[whole] + [hbm] *...]
    pallas_call x1, Pallas kernels: 0.12 us -> 0.9 us  [body(): pl.pallas_call(functools.partial(scale_kernel, float(rows * ring * cols))...]
  transfers between devices with their start and end apart: 1 -> 2, of which waited for: 1 -> 1; matrix products, arithmetic and copies ran while one was open for 0% -> 1% of each run, Pallas kernels for 3% -> 10%
where the time goes in v5:
time: 46.3 us; the launch traced here: 46 us
  starting transfers between devices  25.6 us (55%)
  Pallas kernels  11.6 us (25%)
  waiting for transfers between devices  7.83 us (17%)
  between operations  0.67 us (1%)
    all_to_all x1, starting transfers between devices, body(): lax.all_to_all(send, 'rep', 0, 0, tiled=True, axis_index_groups=[replica_...  13.3 us
    all_to_all x1, starting transfers between devices, body(): lax.all_to_all(squares, 'fsdp', 0, 0, tiled=True, axis_index_groups=[ring...  12.3 us
    all_to_all x1, waiting for transfers between devices, body(): lax.all_to_all(send, 'rep', 0, 0, tiled=True, axis_index_groups=[replica_...  7.83 us
    pallas_call x1, Pallas kernels, body(): pl.pallas_call(finish_kernel, out_shape=full, in_specs=[whole] + [hbm] *...  3.99 us
    pallas_call x1, Pallas kernels, body(): pl.pallas_call(own_kernel, out_shape=full, in_specs=[whole] * 4 + [hbm] *...  2.79 us
    pallas_call x1, Pallas kernels, body(): pl.pallas_call(fetch_kernel, out_shape=(jax.ShapeDtypeStruct((ring, 1, 12...  2.06 us
    pallas_call x1, Pallas kernels, body(): pl.pallas_call(pick_kernel, out_shape=jax.ShapeDtypeStruct((2, groups, 12...  1.91 us
  transfers between devices with their start and end apart: 2, of which 1 were waited for; matrix products, arithmetic and copies ran while one was open for 1% of the time, Pallas kernels for 10%

profile of v5, /device:TPU:1, one launch (start us, length us, event | category | flops | bytes accessed | tf_op | source)
XLA Modules:
  0.0 46.0 jit_solution(16305277661651616164)
XLA Ops:
  0.6 2.1 %fetch.1 = (f32[32,1,128]{2,1,0:T(1,128)}, bf16[128,3072]{1,0:T(8,128)(2,1)S(1)}, bf16[128,3072]{1,0:T(8,128)(2,1)S(1)}, s32[2,1536]{1,0:T(2,128)S(1)}, bf16[256...) custom-call(bf16[128,3072]{1,0:T(8,128)(2,1)} %bitcast.7, bf16[128,3072]{1,0:T(8,128)(2,1)} %bitcast.8, ...), custom_call_target="tpu_custom_call" | custom-call | tf_op jit(solution)/shard_map/fetch/pallas_call | solution.py:285
  2.7 12.3 %all-to-all-start = ((f32[32,1,128]{2,1,0:T(1,128)}), f32[32,1,128]{2,1,0:T(1,128)S(1)}, u32[]{:S(2)}, u32[]{:S(2)}) async-start(f32[32,1,128]{2,1,0:T(1,128)} %get-tuple-element.11), calls=%async_computation | async-start | bytes 32768 | tf_op jit(solution)/shard_map/all_to_all | solution.py:301
  15.0 0.1 reshape.10
  15.2 0.1 reshape.11.where_ref
  15.3 1.9 %pick.1.picked_ref = f32[2,24,128]{2,1,0:T(8,128)S(1)} custom-call(s32[24,128]{1,0:T(8,128)S(1)} %reshape.11.where_ref, bf16[128,3072]{1,0:T(8,128)(2,1)S(1)} %get-tuple-element.13.grad_ref, bf16[128,3072]{1,0:T(8,128)(2,1)S(1)} %get-tuple-element.14.moment_ref, bf16[256,128]{1,0:T(8,128)(2,1)S(1)} %get-tuple-element.15.forth_ref, ...), custom_call_target="tpu_custom_call" | custom-call | flops 2013265920 | bytes 1572864 | tf_op jit(solution)/shard_map/pick/pallas_call | solution.py:306
  17.2 0.0 all-to-all-done.squares_ref
  17.2 0.9 %scale.1 = (f32[1,128]{1,0:T(1,128)S(1)}, f32[48,128]{1,0:T(8,128)S(1)}, f32[16,48,128]{2,1,0:T(8,128)}) custom-call(f32[32,1,128]{2,1,0:T(1,128)S(1)} %all-to-all-done.squares_ref, f32[2,24,128]{2,1,0:T(8,128)S(1)} %pick.1.picked_ref, s32[24,128]{1,0:T(8,128)S(1)} %reshape.11.where_ref), custom_call_target="tpu_custom_call" | custom-call | tf_op jit(solution)/shard_map/scale/pallas_call | solution.py:323
  18.1 13.3 %all-to-all-start.1 = ((f32[16,48,128]{2,1,0:T(8,128)}), f32[16,48,128]{2,1,0:T(8,128)S(1)}, u32[]{:S(2)}, u32[]{:S(2)}) async-start(f32[16,48,128]{2,1,0:T(8,128)} %get-tuple-element.19), calls=%async_computation.1 | async-start | bytes 786432 | tf_op jit(solution)/shard_map/all_to_all | solution.py:336
  31.4 2.8 %own.1 = bf16[128,3072]{1,0:T(8,128)(2,1)} custom-call(f32[48,128]{1,0:T(8,128)S(1)} %get-tuple-element.17.own_ref, f32[1,128]{1,0:T(1,128)S(1)} %get-tuple-element.18.factor_ref, bf16[128,3072]{1,0:T(8,128)(2,1)S(1)} %get-tuple-element.13.grad_ref, bf16[128,3072]{1,0:T(8,128)(2,1)S(1)} %get-tuple-element.14.moment_ref, ...), custom_call_target="tpu_custom_call" | custom-call | flops 2013265920 | bytes 1572864 | tf_op jit(solution)/shard_map/own/pallas_call | solution.py:350
  34.2 7.8 %all-to-all-done.1.all_ref = f32[16,48,128]{2,1,0:T(8,128)S(1)} async-done(((f32[16,48,128]{2,1,0:T(8,128)}), f32[16,48,128]{2,1,0:T(8,128)S(1)}, u32[]{:S(2)}, u32[]{:S(2)}) %all-to-all-start.1) | async-done | bytes 393248 | tf_op jit(solution)/shard_map/all_to_all | solution.py:336
  42.0 4.0 %finish.1 = bf16[128,3072]{1,0:T(8,128)(2,1)} custom-call(f32[16,48,128]{2,1,0:T(8,128)S(1)} %all-to-all-done.1.all_ref, bf16[256,256]{1,0:T(8,128)(2,1)} %constant.9.clone.back_hbm, bf16[256,256]{1,0:T(8,128)(2,1)} %constant.11.clone.tall_hbm, bf16[128,3072]{1,0:T(8,128)(2,1)} %weight_hbm.1), custom_call_target="tpu_custom_call" | custom-call | tf_op jit(solution)/shard_map/finish/pallas_call | solution.py:363
  (1 shorter events, 0.0 us)
Async XLA Ops:
  2.7 14.5 %all-to-all-start = ((f32[32,1,128]{2,1,0:T(1,128)}), f32[32,1,128]{2,1,0:T(1,128)S(1)}, u32[]{:S(2)}, u32[]{:S(2)}) async-start(f32[32,1,128]{2,1,0:T(1,128)} %get-tuple-element.11), calls=%async_computation | async-start | bytes 32768 | tf_op jit(solution)/shard_map/all_to_all | solution.py:301
  18.1 23.9 %all-to-all-start.1 = ((f32[16,48,128]{2,1,0:T(8,128)}), f32[16,48,128]{2,1,0:T(8,128)S(1)}, u32[]{:S(2)}, u32[]{:S(2)}) async-start(f32[16,48,128]{2,1,0:T(8,128)} %get-tuple-element.19), calls=%async_computation.1 | async-start | bytes 786432 | tf_op jit(solution)/shard_map/all_to_all | solution.py:336

commit v6 on v5

--- a/solution.py
+++ b/solution.py
@@ -14,6 +14,7 @@
 step_rate = 0.5
 VMEM = pltpu.VMEM
 PARTS = 6
+ZHEAD = 5
 NN = (((1,), (0,)), ((), ()))
 NT = (((1,), (1,)), ((), ()))
 
@@ -260,8 +261,9 @@
     return [head] + [member for member in range(size) if member != head]
 
 
-def replica_order(size):
-    return [chip * 2 + core for chip in range(size // 2 - 1, -1, -1) for core in range(2)]
+def chip_order(size):
+    head = ZHEAD % size
+    return [(head - n) % size for n in range(size)]
 
 
 def body(grad, momentum, kept_index, weights):
@@ -325,7 +327,7 @@
         out_shape=(
             jax.ShapeDtypeStruct((1, 128), f32),
             jax.ShapeDtypeStruct((2 * groups, 128), f32),
-            jax.ShapeDtypeStruct((replicas, 2 * groups, 128), f32),
+            jax.ShapeDtypeStruct((replicas // 2, 2 * groups, 128), f32),
         ),
         in_specs=[whole] * 3,
         out_specs=(whole,) * 3,
@@ -333,9 +335,10 @@
         name="scale",
     )(squares, picked, where)
 
-    every = lax.all_to_all(
-        send, "rep", 0, 0, tiled=True, axis_index_groups=[replica_order(replicas)]
-    )
+    by_core = [[chip * 2 + core for chip in chip_order(replicas // 2)] for core in range(2)]
+    every = lax.all_to_all(send, "rep", 0, 0, tiled=True, axis_index_groups=by_core)
+    cores = [[chip * 2 + core for core in range(2)] for chip in range(replicas // 2)]
+    every = lax.all_gather(every, "rep", axis=0, tiled=True, axis_index_groups=cores)
 
     def work(lists):
         return [

time: 46.3 us -> 42.8 us (0.924)
  waiting for transfers between devices: 7.83 us -> 1.4 us
  blocking collectives: 0 us -> 4.21 us
  starting transfers between devices: 25.6 us -> 24.4 us
    all_to_all x1, waiting for transfers between devices: 7.83 us -> 1.4 us  [body(): lax.all_to_all(send, 'rep', 0, 0, tiled=True, axis_index_groups=by_core)]
    all_gather x0 -> x1, blocking collectives: none -> 4.21 us  [body(): lax.all_gather(every, 'rep', axis=0, tiled=True, axis_index_groups=cores)]
    all_to_all x1, starting transfers between devices: 13.3 us -> 12.1 us  [body(): lax.all_to_all(send, 'rep', 0, 0, tiled=True, axis_index_groups=by_core)]
  transfers between devices with their start and end apart: 2 -> 2, of which waited for: 1 -> 1; matrix products, arithmetic and copies ran while one was open for 1% -> 1% of each run, Pallas kernels for 10% -> 11%
where the time goes in v6:
time: 42.8 us; the launch traced here: 42.5 us
  starting transfers between devices  24.4 us (57%)
  Pallas kernels  11.6 us (27%)
  blocking collectives  4.21 us (10%)
  waiting for transfers between devices  1.4 us (3%)
  between operations  0.67 us (2%)
    all_to_all x1, starting transfers between devices, body(): lax.all_to_all(squares, 'fsdp', 0, 0, tiled=True, axis_index_groups=[ring...  12.3 us
    all_to_all x1, starting transfers between devices, body(): lax.all_to_all(send, 'rep', 0, 0, tiled=True, axis_index_groups=by_core)  12.1 us
    all_gather x1, blocking collectives, body(): lax.all_gather(every, 'rep', axis=0, tiled=True, axis_index_groups=cores)  4.21 us
    pallas_call x1, Pallas kernels, body(): pl.pallas_call(finish_kernel, out_shape=full, in_specs=[whole] + [hbm] *...  3.99 us
    pallas_call x1, Pallas kernels, body(): pl.pallas_call(own_kernel, out_shape=full, in_specs=[whole] * 4 + [hbm] *...  2.8 us
    pallas_call x1, Pallas kernels, body(): pl.pallas_call(fetch_kernel, out_shape=(jax.ShapeDtypeStruct((ring, 1, 12...  2.06 us
    pallas_call x1, Pallas kernels, body(): pl.pallas_call(pick_kernel, out_shape=jax.ShapeDtypeStruct((2, groups, 12...  1.9 us
    all_to_all x1, waiting for transfers between devices, body(): lax.all_to_all(send, 'rep', 0, 0, tiled=True, axis_index_groups=by_core)  1.4 us
  transfers between devices with their start and end apart: 2, of which 1 were waited for; matrix products, arithmetic and copies ran while one was open for 1% of the time, Pallas kernels for 11%

profile of v6, /device:TPU:1, one launch (start us, length us, event | category | flops | bytes accessed | tf_op | source)
XLA Modules:
  0.0 42.5 jit_solution(18362132448642708658)
XLA Ops:
  0.6 2.1 %fetch.1 = (f32[32,1,128]{2,1,0:T(1,128)}, bf16[128,3072]{1,0:T(8,128)(2,1)S(1)}, bf16[128,3072]{1,0:T(8,128)(2,1)S(1)}, s32[2,1536]{1,0:T(2,128)S(1)}, bf16[256...) custom-call(bf16[128,3072]{1,0:T(8,128)(2,1)} %bitcast.7, bf16[128,3072]{1,0:T(8,128)(2,1)} %bitcast.8, ...), custom_call_target="tpu_custom_call" | custom-call | tf_op jit(solution)/shard_map/fetch/pallas_call | solution.py:287
  2.7 12.3 %all-to-all-start = ((f32[32,1,128]{2,1,0:T(1,128)}), f32[32,1,128]{2,1,0:T(1,128)S(1)}, u32[]{:S(2)}, u32[]{:S(2)}) async-start(f32[32,1,128]{2,1,0:T(1,128)} %get-tuple-element.11), calls=%async_computation | async-start | bytes 32768 | tf_op jit(solution)/shard_map/all_to_all | solution.py:303
  15.0 0.1 reshape.10
  15.2 0.1 reshape.11.where_ref
  15.3 1.9 %pick.1.picked_ref = f32[2,24,128]{2,1,0:T(8,128)S(1)} custom-call(s32[24,128]{1,0:T(8,128)S(1)} %reshape.11.where_ref, bf16[128,3072]{1,0:T(8,128)(2,1)S(1)} %get-tuple-element.13.grad_ref, bf16[128,3072]{1,0:T(8,128)(2,1)S(1)} %get-tuple-element.14.moment_ref, bf16[256,128]{1,0:T(8,128)(2,1)S(1)} %get-tuple-element.15.forth_ref, ...), custom_call_target="tpu_custom_call" | custom-call | flops 2013265920 | bytes 1572864 | tf_op jit(solution)/shard_map/pick/pallas_call | solution.py:308
  17.2 0.0 all-to-all-done.squares_ref
  17.2 0.8 %scale.1 = (f32[1,128]{1,0:T(1,128)S(1)}, f32[48,128]{1,0:T(8,128)S(1)}, f32[8,48,128]{2,1,0:T(8,128)}) custom-call(f32[32,1,128]{2,1,0:T(1,128)S(1)} %all-to-all-done.squares_ref, f32[2,24,128]{2,1,0:T(8,128)S(1)} %pick.1.picked_ref, s32[24,128]{1,0:T(8,128)S(1)} %reshape.11.where_ref), custom_call_target="tpu_custom_call" | custom-call | tf_op jit(solution)/shard_map/scale/pallas_call | solution.py:325
  18.0 12.1 %all-to-all-start.1 = ((f32[8,48,128]{2,1,0:T(8,128)}), f32[8,48,128]{2,1,0:T(8,128)S(1)}, u32[]{:S(2)}, u32[]{:S(2)}) async-start(f32[8,48,128]{2,1,0:T(8,128)} %get-tuple-element.19), calls=%async_computation.1 | async-start | bytes 393216 | tf_op jit(solution)/shard_map/all_to_all | solution.py:339
  30.1 2.8 %own.1 = bf16[128,3072]{1,0:T(8,128)(2,1)} custom-call(f32[48,128]{1,0:T(8,128)S(1)} %get-tuple-element.17.own_ref, f32[1,128]{1,0:T(1,128)S(1)} %get-tuple-element.18.factor_ref, bf16[128,3072]{1,0:T(8,128)(2,1)S(1)} %get-tuple-element.13.grad_ref, bf16[128,3072]{1,0:T(8,128)(2,1)S(1)} %get-tuple-element.14.moment_ref, ...), custom_call_target="tpu_custom_call" | custom-call | flops 2013265920 | bytes 1572864 | tf_op jit(solution)/shard_map/own/pallas_call | solution.py:353
  32.9 1.4 %all-to-all-done.1 = f32[8,48,128]{2,1,0:T(8,128)S(1)} async-done(((f32[8,48,128]{2,1,0:T(8,128)}), f32[8,48,128]{2,1,0:T(8,128)S(1)}, u32[]{:S(2)}, u32[]{:S(2)}) %all-to-all-start.1) | async-done | bytes 196640 | tf_op jit(solution)/shard_map/all_to_all | solution.py:339
  34.3 4.2 %all_gather.3.all_ref = f32[16,48,128]{2,1,0:T(8,128)S(1)} all-gather(f32[8,48,128]{2,1,0:T(8,128)S(1)} %all-to-all-done.1), channel_id=1, replica_groups={{0,32},{64,96},{128,160},{192,224},{256,288},{320,352},{384,416},{448,4..., dimensions={0}, use_global_device_ids=true | all-gather | bytes 589824 | tf_op jit(solution)/shard_map/all_gather | solution.py:341
  38.5 4.0 %finish.1 = bf16[128,3072]{1,0:T(8,128)(2,1)} custom-call(f32[16,48,128]{2,1,0:T(8,128)S(1)} %all_gather.3.all_ref, bf16[256,256]{1,0:T(8,128)(2,1)} %constant.9.clone.back_hbm, bf16[256,256]{1,0:T(8,128)(2,1)} %constant.11.clone.tall_hbm, bf16[128,3072]{1,0:T(8,128)(2,1)} %weight_hbm.1), custom_call_target="tpu_custom_call" | custom-call | tf_op jit(solution)/shard_map/finish/pallas_call | solution.py:366
  (1 shorter events, 0.0 us)
Async XLA Ops:
  2.7 14.5 %all-to-all-start = ((f32[32,1,128]{2,1,0:T(1,128)}), f32[32,1,128]{2,1,0:T(1,128)S(1)}, u32[]{:S(2)}, u32[]{:S(2)}) async-start(f32[32,1,128]{2,1,0:T(1,128)} %get-tuple-element.11), calls=%async_computation | async-start | bytes 32768 | tf_op jit(solution)/shard_map/all_to_all | solution.py:303
  18.0 16.3 %all-to-all-start.1 = ((f32[8,48,128]{2,1,0:T(8,128)}), f32[8,48,128]{2,1,0:T(8,128)S(1)}, u32[]{:S(2)}, u32[]{:S(2)}) async-start(f32[8,48,128]{2,1,0:T(8,128)} %get-tuple-element.19), calls=%async_computation.1 | async-start | bytes 393216 | tf_op jit(solution)/shard_map/all_to_all | solution.py:339

commit v7 on v6

--- a/solution.py
+++ b/solution.py
@@ -14,6 +14,7 @@
 step_rate = 0.5
 VMEM = pltpu.VMEM
 PARTS = 6
+CHUNKS = 2
 ZHEAD = 5
 NN = (((1,), (0,)), ((), ()))
 NT = (((1,), (1,)), ((), ()))
@@ -63,8 +64,8 @@
     return pl.ds(k * 128 if isinstance(k, int) else pl.multiple_of(k * 128, 128), 128)
 
 
-def row(k):
-    return pl.ds(k, 1)
+def row(k, groups):
+    return pl.ds((k % 2) * (groups // 2) + k // 2, 1)
 
 
 def in_hbm(*arrays):
@@ -79,72 +80,97 @@
 
 
 def fetch_kernel(grad_hbm, *refs):
-    count = (len(refs) - 3) // 2
-    sources, (out_ref, grad_ref), (targets, sems) = refs[:count], refs[count : count + 2], (refs[count + 2 : -1], refs[-1])
+    count = (len(refs) - 4) // 2
+    sources, out_hbm, grad_ref = refs[:count], refs[count], refs[count + 1]
+    targets, out_ref, sems = refs[count + 2 : -2], refs[-2], refs[-1]
+    width = grad_ref.shape[1] // CHUNKS
     copies = [
-        pltpu.make_async_copy(source, target, sems.at[n])
-        for n, (source, target) in enumerate(zip((grad_hbm, *sources), (grad_ref, *targets)))
+        pltpu.make_async_copy(
+            grad_hbm.at[:, pl.ds(n * width, width)],
+            grad_ref.at[:, pl.ds(n * width, width)],
+            sems.at[n],
+        )
+        for n in range(CHUNKS)
+    ]
+    copies += [
+        pltpu.make_async_copy(source, target, sems.at[CHUNKS + n])
+        for n, (source, target) in enumerate(zip(sources, targets))
     ]
     for copy in copies:
         copy.start()
-    copies[0].wait()
-
-    def step(k, total):
-        value = grad_ref[:, block(k)].astype(jnp.float32)
-        return total + jnp.sum((value * value).reshape(-1, 8, 128), axis=0)
-
-    total = lax.fori_loop(
-        0, grad_ref.shape[1] // 128, step, jnp.zeros((8, 128), jnp.float32), unroll=8
-    )
+    total = jnp.zeros((8, 128), jnp.float32)
+    for n in range(CHUNKS):
+        copies[n].wait()
+        for k in range(n * width // 128, (n + 1) * width // 128):
+            value = grad_ref[:, block(k)].astype(jnp.float32)
+            total = total + jnp.sum((value * value).reshape(-1, 8, 128), axis=0)
     out_ref[...] = jnp.broadcast_to(
         jnp.sum(total, axis=0, keepdims=True)[None], out_ref.shape
     )
-    for copy in copies[1:]:
+    copies.append(pltpu.make_async_copy(out_ref, out_hbm, sems.at[len(copies)]))
+    copies[-1].start()
+    for copy in copies[CHUNKS:]:
         copy.wait()
 
 
 def pick_kernel(
-    where_ref, grad_ref, moment_ref, forth_ref, pair_ref, out_ref, at_ref, first_ref, kept_ref
+    kept_ref, grad_ref, moment_ref, forth_ref, pair_ref, out_ref, listed_ref, at_ref, first_ref, picked_ref
 ):
-    groups = where_ref.shape[0]
-    lane = lax.broadcasted_iota(jnp.int32, out_ref.shape[1:], 1)
-    for h, offset in enumerate(duplicate((where_ref[...] & 127).astype(jnp.float32))):
-        at_ref[h] = jnp.where(lane < 64, offset, offset - 64.0)
+    groups = out_ref.shape[1]
+    half = groups // 2
+    lane = lax.broadcasted_iota(jnp.int32, (half, 128), 1)
+    for i in range(2):
+        for n in range(half):
+            listed_ref[i, n : n + 1] = kept_ref[i : i + 1, n * 128 : (n + 1) * 128]
+    offsets = [(listed_ref[i] & 127).astype(jnp.float32) for i in range(2)]
+    for q in range(2):
+        placed = []
+        for h in range(2):
+            here = (2 * q + h) * 32
+            front = pltpu.roll(offsets[0], (128 - here) % 128, 1)
+            back = pltpu.roll(offsets[1], (160 - here) % 128, 1)
+            placed.append(jnp.where(lane < 32, front, back))
+            there = pltpu.roll(placed[h], 64, 1)
+            at_ref[h, q * half : (q + 1) * half] = jnp.where(lane < 64, placed[h], there - 64.0)
+        out_ref[2, q * half : (q + 1) * half] = jnp.where(
+            lane < 64, placed[0], pltpu.roll(placed[1], 64, 1)
+        )
     level = lax.broadcasted_iota(jnp.int32, (64, 128), 0).astype(jnp.float32)
 
     def over_rows(k):
         both = jnp.concatenate([grad_ref[:, block(k)], moment_ref[:, block(k)]], axis=1)
-        first = dot(forth_ref[...], both, NN)
-        put_split(first_ref.at[k], first[:128] + first[128:])
+        twice = jnp.concatenate([both, both], axis=0)
+        put_split(first_ref.at[k], dot(forth_ref[...], twice, NN))
 
     def over_columns(k):
         coeffs = dot(pair_ref[...], first_ref[k], NT)
         coeffs = coeffs[:128] + coeffs[128:]
         for h in range(2):
-            hit = level == at_ref[h, row(k), :]
+            hit = level == at_ref[h, row(k, groups), :]
             for n in range(2):
                 part = coeffs[h * 64 : (h + 1) * 64, n * 128 : (n + 1) * 128]
-                kept_ref[n, h, row(k), :] = jnp.sum(
+                picked_ref[n, h, row(k, groups), :] = jnp.sum(
                     jnp.where(hit, part, 0.0), axis=0, keepdims=True
                 )
 
     for step in (over_rows, over_columns):
         for k in range(groups):
             step(k)
+    lane = lax.broadcasted_iota(jnp.int32, (groups, 128), 1)
     for n in range(2):
-        front, back = kept_ref[n, 0], kept_ref[n, 1]
+        front, back = picked_ref[n, 0], picked_ref[n, 1]
         front = front + pltpu.roll(front, 64, 1)
         back = back + pltpu.roll(back, 64, 1)
         out_ref[n] = jnp.where(lane < 64, front, back)
 
 
-def scale_kernel(count, squares_ref, picked_ref, where_ref, factor_ref, own_ref, send_ref):
+def scale_kernel(count, squares_ref, picked_ref, factor_ref, own_ref, send_ref):
     total = jnp.sum(jnp.sum(squares_ref[...], axis=0), axis=1, keepdims=True)
     mean_square = jnp.broadcast_to(total, (1, 128)) / count
     factor = jnp.minimum(1.0, clip_rms / jnp.sqrt(mean_square + 1e-06))
     factor_ref[...] = factor
     values = momentum_decay * picked_ref[1] + factor * picked_ref[0]
-    listing = jnp.concatenate([values, (where_ref[...] & 127).astype(jnp.float32)], axis=0)
+    listing = jnp.concatenate([values, picked_ref[2]], axis=0)
     own_ref[...] = listing
     send_ref[...] = jnp.broadcast_to(listing[None], send_ref.shape)
 
@@ -172,15 +198,15 @@
             for h in range(2):
                 part = jnp.zeros((64, 128), jnp.float32)
                 for r in range(lists):
-                    hit = level == at_ref[r, h, row(2 * t + k), :]
-                    part = jnp.where(hit, value_ref[r, h, row(2 * t + k), :], part)
+                    hit = level == at_ref[r, h, row(2 * t + k, groups), :]
+                    part = jnp.where(hit, value_ref[r, h, row(2 * t + k, groups), :], part)
                 high, low = split(part)
                 at = slice(k * 128 + h * 64, k * 128 + h * 64 + 64)
                 sparse_ref[t, at, :128] = high
                 sparse_ref[t, at, 128:] = low
         return carry
 
-    lax.fori_loop(0, groups // 2, scatter, 0)
+    lax.fori_loop(0, groups // 2, scatter, 0, unroll=3 if groups % 6 == 0 else 1)
     for copy in ready:
         copy.wait()
     for t in range(groups // 2):
@@ -274,7 +300,7 @@
     groups = cols // 128
     bf16, f32 = jnp.bfloat16, jnp.float32
     pair, back = tables()
-    forth = jnp.asarray(np.concatenate(split_table(back.T), axis=0))
+    forth = jnp.asarray(np.concatenate(split_table(back.T), axis=1))
     back_wide = jnp.asarray(widen(back))
     pair_wide = jnp.asarray(widen(pair))
     pair_tall = jnp.asarray(np.ascontiguousarray(widen(pair.T).T))
@@ -291,12 +317,12 @@
             full,
             full,
             jax.ShapeDtypeStruct(kept_index.shape[1:], jnp.int32),
-            jax.ShapeDtypeStruct((256, 128), bf16),
+            jax.ShapeDtypeStruct((128, 256), bf16),
             square,
         ),
         in_specs=[hbm] * 5,
-        out_specs=(whole,) * 6,
-        scratch_shapes=[pltpu.SemaphoreType.DMA((5,))],
+        out_specs=(hbm,) + (whole,) * 5,
+        scratch_shapes=[VMEM((ring, 1, 128), f32), pltpu.SemaphoreType.DMA((CHUNKS + 5,))],
         compiler_params=params,
         name="fetch",
     )(*in_hbm(grad, momentum, kept_index[0], forth, pair_wide))
@@ -304,13 +330,13 @@
         squares, "fsdp", 0, 0, tiled=True, axis_index_groups=[ring_order(ring)]
     )
 
-    where = kept_near.reshape(2, groups, 2, 32).transpose(1, 2, 0, 3).reshape(groups, 128)
     picked = pl.pallas_call(
         pick_kernel,
-        out_shape=jax.ShapeDtypeStruct((2, groups, 128), f32),
+        out_shape=jax.ShapeDtypeStruct((3, groups, 128), f32),
         in_specs=[whole] * 5,
         out_specs=whole,
         scratch_shapes=[
+            VMEM((2, groups // 2, 128), jnp.int32),
             VMEM((2, groups, 128), f32),
             VMEM((groups, 256, 256), bf16),
             VMEM((2, 2, groups, 128), f32),
@@ -320,7 +346,7 @@
             flops=2 * 2 * 10 * 128 * 128 * cols, bytes_accessed=4 * rows * cols, transcendentals=0
         ),
         name="pick",
-    )(where, grad_near, moment_near, forth_near, pair_near)
+    )(kept_near, grad_near, moment_near, forth_near, pair_near)
 
     factor, own, send = pl.pallas_call(
         functools.partial(scale_kernel, float(rows * ring * cols)),
@@ -329,11 +355,11 @@
             jax.ShapeDtypeStruct((2 * groups, 128), f32),
             jax.ShapeDtypeStruct((replicas // 2, 2 * groups, 128), f32),
         ),
-        in_specs=[whole] * 3,
+        in_specs=[whole] * 2,
         out_specs=(whole,) * 3,
         compiler_params=params,
         name="scale",
-    )(squares, picked, where)
+    )(squares, picked)
 
     by_core = [[chip * 2 + core for chip in chip_order(replicas // 2)] for core in range(2)]
     every = lax.all_to_all(send, "rep", 0, 0, tiled=True, axis_index_groups=by_core)

time: 42.8 us -> 43 us (level)
  blocking collectives: 4.21 us -> 4.95 us
    all_gather x1, blocking collectives: 4.21 us -> 4.95 us  [body(): lax.all_gather(every, 'rep', axis=0, tiled=True, axis_index_groups=cores)]
  transfers between devices with their start and end apart: 2 -> 2, of which waited for: 1 -> 1; matrix products, arithmetic and copies ran while one was open for 1% -> 0% of each run, Pallas kernels for 11% -> 11%
where the time goes in v7:
time: 43 us; the launch traced here: 42.7 us
  starting transfers between devices  24.4 us (57%)
  Pallas kernels  11.2 us (26%)
  blocking collectives  4.95 us (12%)
  waiting for transfers between devices  1.4 us (3%)
  between operations  0.66 us (2%)
    all_to_all x1, starting transfers between devices, body(): lax.all_to_all(squares, 'fsdp', 0, 0, tiled=True, axis_index_groups=[ring...  12.3 us
    all_to_all x1, starting transfers between devices, body(): lax.all_to_all(send, 'rep', 0, 0, tiled=True, axis_index_groups=by_core)  12.1 us
    all_gather x1, blocking collectives, body(): lax.all_gather(every, 'rep', axis=0, tiled=True, axis_index_groups=cores)  4.95 us
    pallas_call x1, Pallas kernels, body(): pl.pallas_call(finish_kernel, out_shape=full, in_specs=[whole] + [hbm] *...  3.96 us
    pallas_call x1, Pallas kernels, body(): pl.pallas_call(own_kernel, out_shape=full, in_specs=[whole] * 4 + [hbm] *...  2.81 us
    pallas_call x1, Pallas kernels, body(): pl.pallas_call(fetch_kernel, out_shape=(jax.ShapeDtypeStruct((ring, 1, 12...  1.88 us
    pallas_call x1, Pallas kernels, body(): pl.pallas_call(pick_kernel, out_shape=jax.ShapeDtypeStruct((3, groups, 12...  1.77 us
    all_to_all x1, waiting for transfers between devices, body(): lax.all_to_all(send, 'rep', 0, 0, tiled=True, axis_index_groups=by_core)  1.4 us
  transfers between devices with their start and end apart: 2, of which 1 were waited for; matrix products, arithmetic and copies ran while one was open for 0% of the time, Pallas kernels for 11%

profile of v7, /device:TPU:1, one launch (start us, length us, event | category | flops | bytes accessed | tf_op | source)
XLA Modules:
  0.0 42.7 jit_solution(6378728730808839909)
XLA Ops:
  0.6 1.9 %fetch.1 = (f32[32,1,128]{2,1,0:T(1,128)}, bf16[128,3072]{1,0:T(8,128)(2,1)S(1)}, bf16[128,3072]{1,0:T(8,128)(2,1)S(1)}, s32[2,1536]{1,0:T(2,128)S(1)}, bf16[128...) custom-call(bf16[128,3072]{1,0:T(8,128)(2,1)} %bitcast.4, bf16[128,3072]{1,0:T(8,128)(2,1)} %bitcast.5, ...), custom_call_target="tpu_custom_call" | custom-call | tf_op jit(solution)/shard_map/fetch/pallas_call | solution.py:313
  2.5 12.3 %all-to-all-start = ((f32[32,1,128]{2,1,0:T(1,128)}), f32[32,1,128]{2,1,0:T(1,128)S(1)}, u32[]{:S(2)}, u32[]{:S(2)}) async-start(f32[32,1,128]{2,1,0:T(1,128)} %get-tuple-element.11), calls=%async_computation | async-start | bytes 32768 | tf_op jit(solution)/shard_map/all_to_all | solution.py:329
  14.9 1.8 %pick.1.picked_ref = f32[3,24,128]{2,1,0:T(8,128)S(1)} custom-call(s32[2,1536]{1,0:T(2,128)S(1)} %get-tuple-element.12.kept_ref, bf16[128,3072]{1,0:T(8,128)(2,1)S(1)} %get-tuple-element.13.grad_ref, bf16[128,3072]{1,0:T(8,128)(2,1)S(1)} %get-tuple-element.14.moment_ref, bf16[128,256]{1,0:T(8,128)(2,1)S(1)} %get-tuple-element.15.forth_ref, ...), custom_call_target="tpu_custom_call" | custom-call | flops 2013265920 | bytes 1572864 | tf_op jit(solution)/shard_map/pick/pallas_call | solution.py:333
  16.6 0.0 all-to-all-done.squares_ref
  16.6 0.8 %scale.1 = (f32[1,128]{1,0:T(1,128)S(1)}, f32[48,128]{1,0:T(8,128)S(1)}, f32[8,48,128]{2,1,0:T(8,128)}) custom-call(f32[32,1,128]{2,1,0:T(1,128)S(1)} %all-to-all-done.squares_ref, f32[3,24,128]{2,1,0:T(8,128)S(1)} %pick.1.picked_ref), custom_call_target="tpu_custom_call" | custom-call | tf_op jit(solution)/shard_map/scale/pallas_call | solution.py:351
  17.4 12.1 %all-to-all-start.1 = ((f32[8,48,128]{2,1,0:T(8,128)}), f32[8,48,128]{2,1,0:T(8,128)S(1)}, u32[]{:S(2)}, u32[]{:S(2)}) async-start(f32[8,48,128]{2,1,0:T(8,128)} %get-tuple-element.19), calls=%async_computation.1 | async-start | bytes 393216 | tf_op jit(solution)/shard_map/all_to_all | solution.py:365
  29.6 2.8 %own.1 = bf16[128,3072]{1,0:T(8,128)(2,1)} custom-call(f32[48,128]{1,0:T(8,128)S(1)} %get-tuple-element.17.own_ref, f32[1,128]{1,0:T(1,128)S(1)} %get-tuple-element.18.factor_ref, bf16[128,3072]{1,0:T(8,128)(2,1)S(1)} %get-tuple-element.13.grad_ref, bf16[128,3072]{1,0:T(8,128)(2,1)S(1)} %get-tuple-element.14.moment_ref, ...), custom_call_target="tpu_custom_call" | custom-call | flops 2013265920 | bytes 1572864 | tf_op jit(solution)/shard_map/own/pallas_call | solution.py:379
  32.4 1.4 %all-to-all-done.1 = f32[8,48,128]{2,1,0:T(8,128)S(1)} async-done(((f32[8,48,128]{2,1,0:T(8,128)}), f32[8,48,128]{2,1,0:T(8,128)S(1)}, u32[]{:S(2)}, u32[]{:S(2)}) %all-to-all-start.1) | async-done | bytes 196640 | tf_op jit(solution)/shard_map/all_to_all | solution.py:365
  33.8 5.0 %all_gather.3.all_ref = f32[16,48,128]{2,1,0:T(8,128)S(1)} all-gather(f32[8,48,128]{2,1,0:T(8,128)S(1)} %all-to-all-done.1), channel_id=1, replica_groups={{0,32},{64,96},{128,160},{192,224},{256,288},{320,352},{384,416},{448,4..., dimensions={0}, use_global_device_ids=true | all-gather | bytes 589824 | tf_op jit(solution)/shard_map/all_gather | solution.py:367
  38.7 4.0 %finish.1 = bf16[128,3072]{1,0:T(8,128)(2,1)} custom-call(f32[16,48,128]{2,1,0:T(8,128)S(1)} %all_gather.3.all_ref, bf16[256,256]{1,0:T(8,128)(2,1)} %constant.9.clone.back_hbm, bf16[256,256]{1,0:T(8,128)(2,1)} %constant.11.clone.tall_hbm, bf16[128,3072]{1,0:T(8,128)(2,1)} %weight_hbm.1), custom_call_target="tpu_custom_call" | custom-call | tf_op jit(solution)/shard_map/finish/pallas_call | solution.py:392
Async XLA Ops:
  2.5 14.1 %all-to-all-start = ((f32[32,1,128]{2,1,0:T(1,128)}), f32[32,1,128]{2,1,0:T(1,128)S(1)}, u32[]{:S(2)}, u32[]{:S(2)}) async-start(f32[32,1,128]{2,1,0:T(1,128)} %get-tuple-element.11), calls=%async_computation | async-start | bytes 32768 | tf_op jit(solution)/shard_map/all_to_all | solution.py:329
  17.4 16.3 %all-to-all-start.1 = ((f32[8,48,128]{2,1,0:T(8,128)}), f32[8,48,128]{2,1,0:T(8,128)S(1)}, u32[]{:S(2)}, u32[]{:S(2)}) async-start(f32[8,48,128]{2,1,0:T(8,128)} %get-tuple-element.19), calls=%async_computation.1 | async-start | bytes 393216 | tf_op jit(solution)/shard_map/all_to_all | solution.py:365

commit v8 on v7

--- a/solution.py
+++ b/solution.py
@@ -15,7 +15,6 @@
 VMEM = pltpu.VMEM
 PARTS = 6
 CHUNKS = 2
-ZHEAD = 5
 NN = (((1,), (0,)), ((), ()))
 NT = (((1,), (1,)), ((), ()))
 
@@ -282,14 +281,22 @@
     outlet.wait()
 
 
-def ring_order(size):
-    head = size // 2 + 2 if size == 32 else 0
-    return [head] + [member for member in range(size) if member != head]
-
-
-def chip_order(size):
-    head = ZHEAD % size
-    return [(head - n) % size for n in range(size)]
+def led_by(head, members):
+    return [head] + [member for member in members if member != head]
+
+
+def ring_groups(replicas, size):
+    heads = (18, 22) if size == 32 else (0, 0)
+    return [
+        [r * size + member for member in led_by(heads[r % 2], range(size))] for r in range(replicas)
+    ]
+
+
+def chip_groups(replicas):
+    chips = replicas // 2
+    return [
+        [(head - n) % chips * 2 + core for n in range(chips)] for core, head in enumerate((5, 6))
+    ]
 
 
 def body(grad, momentum, kept_index, weights):
@@ -327,7 +334,12 @@
         name="fetch",
     )(*in_hbm(grad, momentum, kept_index[0], forth, pair_wide))
     squares = lax.all_to_all(
-        squares, "fsdp", 0, 0, tiled=True, axis_index_groups=[ring_order(ring)]
+        squares,
+        ("rep", "fsdp"),
+        0,
+        0,
+        tiled=True,
+        axis_index_groups=ring_groups(replicas, ring),
     )
 
     picked = pl.pallas_call(
@@ -361,8 +373,9 @@
         name="scale",
     )(squares, picked)
 
-    by_core = [[chip * 2 + core for chip in chip_order(replicas // 2)] for core in range(2)]
-    every = lax.all_to_all(send, "rep", 0, 0, tiled=True, axis_index_groups=by_core)
+    every = lax.all_to_all(
+        send, "rep", 0, 0, tiled=True, axis_index_groups=chip_groups(replicas)
+    )
     cores = [[chip * 2 + core for core in range(2)] for chip in range(replicas // 2)]
     every = lax.all_gather(every, "rep", axis=0, tiled=True, axis_index_groups=cores)
 

time: 43 us -> 42.7 us (level)
  waiting for transfers between devices: 1.4 us -> 2.36 us
  starting transfers between devices: 24.4 us -> 23.6 us
    all_to_all x2, waiting for transfers between devices: 1.4 us -> 2.36 us  [the longest x1 1.78 us: body(): lax.all_to_all(send, 'rep', 0, 0, tiled=True, axis_index_groups=chip_grou...]
    all_to_all x2, starting transfers between devices: 24.4 us -> 23.6 us  [the longest x1 12.1 us: body(): lax.all_to_all(send, 'rep', 0, 0, tiled=True, axis_index_groups=chip_grou...]
  transfers between devices with their start and end apart: 2 -> 2, of which waited for: 1 -> 2; matrix products, arithmetic and copies ran while one was open for 0% -> 0% of each run, Pallas kernels for 11% -> 11%
where the time goes in v8:
time: 42.7 us; the launch traced here: 42.4 us
  starting transfers between devices  23.6 us (55%)
  Pallas kernels  11.2 us (26%)
  blocking collectives  4.54 us (11%)
  waiting for transfers between devices  2.36 us (6%)
  between operations  0.66 us (2%)
    all_to_all x1, starting transfers between devices, body(): lax.all_to_all(send, 'rep', 0, 0, tiled=True, axis_index_groups=chip_grou...  12.1 us
    all_to_all x1, starting transfers between devices, body(): lax.all_to_all(squares, ('rep', 'fsdp'), 0, 0, tiled=True, axis_index_gro...  11.5 us
    all_gather x1, blocking collectives, body(): lax.all_gather(every, 'rep', axis=0, tiled=True, axis_index_groups=cores)  4.54 us
    pallas_call x1, Pallas kernels, body(): pl.pallas_call(finish_kernel, out_shape=full, in_specs=[whole] + [hbm] *...  3.96 us
    pallas_call x1, Pallas kernels, body(): pl.pallas_call(own_kernel, out_shape=full, in_specs=[whole] * 4 + [hbm] *...  2.8 us
    pallas_call x1, Pallas kernels, body(): pl.pallas_call(fetch_kernel, out_shape=(jax.ShapeDtypeStruct((ring, 1, 12...  1.88 us
    all_to_all x1, waiting for transfers between devices, body(): lax.all_to_all(send, 'rep', 0, 0, tiled=True, axis_index_groups=chip_grou...  1.78 us
    pallas_call x1, Pallas kernels, body(): pl.pallas_call(pick_kernel, out_shape=jax.ShapeDtypeStruct((3, groups, 12...  1.77 us
  transfers between devices with their start and end apart: 2, of which 2 were waited for; matrix products, arithmetic and copies ran while one was open for 0% of the time, Pallas kernels for 11%

profile of v8, /device:TPU:1, one launch (start us, length us, event | category | flops | bytes accessed | tf_op | source)
XLA Modules:
  0.0 42.4 jit_solution(6024083465818452022)
XLA Ops:
  0.6 1.9 %fetch.1 = (f32[32,1,128]{2,1,0:T(1,128)}, bf16[128,3072]{1,0:T(8,128)(2,1)S(1)}, bf16[128,3072]{1,0:T(8,128)(2,1)S(1)}, s32[2,1536]{1,0:T(2,128)S(1)}, bf16[128...) custom-call(bf16[128,3072]{1,0:T(8,128)(2,1)} %bitcast.4, bf16[128,3072]{1,0:T(8,128)(2,1)} %bitcast.5, ...), custom_call_target="tpu_custom_call" | custom-call | tf_op jit(solution)/shard_map/fetch/pallas_call | solution.py:320
  2.5 11.5 %all-to-all-start = ((f32[32,1,128]{2,1,0:T(1,128)}), f32[32,1,128]{2,1,0:T(1,128)S(1)}, u32[]{:S(2)}, u32[]{:S(2)}) async-start(f32[32,1,128]{2,1,0:T(1,128)} %get-tuple-element.11), calls=%async_computation | async-start | bytes 32768 | tf_op jit(solution)/shard_map/all_to_all | solution.py:336
  14.1 1.8 %pick.1.picked_ref = f32[3,24,128]{2,1,0:T(8,128)S(1)} custom-call(s32[2,1536]{1,0:T(2,128)S(1)} %get-tuple-element.12.kept_ref, bf16[128,3072]{1,0:T(8,128)(2,1)S(1)} %get-tuple-element.13.grad_ref, bf16[128,3072]{1,0:T(8,128)(2,1)S(1)} %get-tuple-element.14.moment_ref, bf16[128,256]{1,0:T(8,128)(2,1)S(1)} %get-tuple-element.15.forth_ref, ...), custom_call_target="tpu_custom_call" | custom-call | flops 2013265920 | bytes 1572864 | tf_op jit(solution)/shard_map/pick/pallas_call | solution.py:345
  15.8 0.6 %all-to-all-done.squares_ref = f32[32,1,128]{2,1,0:T(1,128)S(1)} async-done(((f32[32,1,128]{2,1,0:T(1,128)}), f32[32,1,128]{2,1,0:T(1,128)S(1)}, u32[]{:S(2)}, u32[]{:S(2)}) %all-to-all-start) | async-done | bytes 16416 | tf_op jit(solution)/shard_map/all_to_all | solution.py:336
  16.4 0.8 %scale.1 = (f32[1,128]{1,0:T(1,128)S(1)}, f32[48,128]{1,0:T(8,128)S(1)}, f32[8,48,128]{2,1,0:T(8,128)}) custom-call(f32[32,1,128]{2,1,0:T(1,128)S(1)} %all-to-all-done.squares_ref, f32[3,24,128]{2,1,0:T(8,128)S(1)} %pick.1.picked_ref), custom_call_target="tpu_custom_call" | custom-call | tf_op jit(solution)/shard_map/scale/pallas_call | solution.py:363
  17.2 12.1 %all-to-all-start.1 = ((f32[8,48,128]{2,1,0:T(8,128)}), f32[8,48,128]{2,1,0:T(8,128)S(1)}, u32[]{:S(2)}, u32[]{:S(2)}) async-start(f32[8,48,128]{2,1,0:T(8,128)} %get-tuple-element.19), calls=%async_computation.1 | async-start | bytes 393216 | tf_op jit(solution)/shard_map/all_to_all | solution.py:376
  29.3 2.8 %own.1 = bf16[128,3072]{1,0:T(8,128)(2,1)} custom-call(f32[48,128]{1,0:T(8,128)S(1)} %get-tuple-element.17.own_ref, f32[1,128]{1,0:T(1,128)S(1)} %get-tuple-element.18.factor_ref, bf16[128,3072]{1,0:T(8,128)(2,1)S(1)} %get-tuple-element.13.grad_ref, bf16[128,3072]{1,0:T(8,128)(2,1)S(1)} %get-tuple-element.14.moment_ref, ...), custom_call_target="tpu_custom_call" | custom-call | flops 2013265920 | bytes 1572864 | tf_op jit(solution)/shard_map/own/pallas_call | solution.py:392
  32.1 1.8 %all-to-all-done.1 = f32[8,48,128]{2,1,0:T(8,128)S(1)} async-done(((f32[8,48,128]{2,1,0:T(8,128)}), f32[8,48,128]{2,1,0:T(8,128)S(1)}, u32[]{:S(2)}, u32[]{:S(2)}) %all-to-all-start.1) | async-done | bytes 196640 | tf_op jit(solution)/shard_map/all_to_all | solution.py:376
  33.9 4.5 %all_gather.3.all_ref = f32[16,48,128]{2,1,0:T(8,128)S(1)} all-gather(f32[8,48,128]{2,1,0:T(8,128)S(1)} %all-to-all-done.1), channel_id=1, replica_groups={{0,32},{64,96},{128,160},{192,224},{256,288},{320,352},{384,416},{448,4..., dimensions={0}, use_global_device_ids=true | all-gather | bytes 589824 | tf_op jit(solution)/shard_map/all_gather | solution.py:380
  38.4 4.0 %finish.1 = bf16[128,3072]{1,0:T(8,128)(2,1)} custom-call(f32[16,48,128]{2,1,0:T(8,128)S(1)} %all_gather.3.all_ref, bf16[256,256]{1,0:T(8,128)(2,1)} %constant.9.clone.back_hbm, bf16[256,256]{1,0:T(8,128)(2,1)} %constant.11.clone.tall_hbm, bf16[128,3072]{1,0:T(8,128)(2,1)} %weight_hbm.1), custom_call_target="tpu_custom_call" | custom-call | tf_op jit(solution)/shard_map/finish/pallas_call | solution.py:405
Async XLA Ops:
  2.5 13.9 %all-to-all-start = ((f32[32,1,128]{2,1,0:T(1,128)}), f32[32,1,128]{2,1,0:T(1,128)S(1)}, u32[]{:S(2)}, u32[]{:S(2)}) async-start(f32[32,1,128]{2,1,0:T(1,128)} %get-tuple-element.11), calls=%async_computation | async-start | bytes 32768 | tf_op jit(solution)/shard_map/all_to_all | solution.py:336
  17.2 16.7 %all-to-all-start.1 = ((f32[8,48,128]{2,1,0:T(8,128)}), f32[8,48,128]{2,1,0:T(8,128)S(1)}, u32[]{:S(2)}, u32[]{:S(2)}) async-start(f32[8,48,128]{2,1,0:T(8,128)} %get-tuple-element.19), calls=%async_computation.1 | async-start | bytes 393216 | tf_op jit(solution)/shard_map/all_to_all | solution.py:376

commit v9 on v8

--- a/solution.py
+++ b/solution.py
@@ -13,6 +13,7 @@
 momentum_decay = 0.9
 step_rate = 0.5
 VMEM = pltpu.VMEM
+SPARE = 8
 PARTS = 6
 CHUNKS = 2
 NN = (((1,), (0,)), ((), ()))
@@ -113,15 +114,16 @@
 
 
 def pick_kernel(
-    kept_ref, grad_ref, moment_ref, forth_ref, pair_ref, out_ref, listed_ref, at_ref, first_ref, picked_ref
+    kept_ref, grad_ref, moment_ref, forth_ref, pair_ref, out_ref, listed_ref, at_ref, placed_ref, first_ref, picked_ref
 ):
     groups = out_ref.shape[1]
     half = groups // 2
     lane = lax.broadcasted_iota(jnp.int32, (half, 128), 1)
+    kept = kept_ref[...]
     for i in range(2):
         for n in range(half):
-            listed_ref[i, n : n + 1] = kept_ref[i : i + 1, n * 128 : (n + 1) * 128]
-    offsets = [(listed_ref[i] & 127).astype(jnp.float32) for i in range(2)]
+            listed_ref[i, n : n + 1] = kept[i : i + 1, n * 128 : (n + 1) * 128]
+    offsets = [(listed_ref[i, :half] & 127).astype(jnp.float32) for i in range(2)]
     for q in range(2):
         placed = []
         for h in range(2):
@@ -131,9 +133,10 @@
             placed.append(jnp.where(lane < 32, front, back))
             there = pltpu.roll(placed[h], 64, 1)
             at_ref[h, q * half : (q + 1) * half] = jnp.where(lane < 64, placed[h], there - 64.0)
-        out_ref[2, q * half : (q + 1) * half] = jnp.where(
+        placed_ref[q * half : (q + 1) * half] = jnp.where(
             lane < 64, placed[0], pltpu.roll(placed[1], 64, 1)
         )
+    out_ref[2] = placed_ref[:groups]
     level = lax.broadcasted_iota(jnp.int32, (64, 128), 0).astype(jnp.float32)
 
     def over_rows(k):
@@ -157,7 +160,7 @@
             step(k)
     lane = lax.broadcasted_iota(jnp.int32, (groups, 128), 1)
     for n in range(2):
-        front, back = picked_ref[n, 0], picked_ref[n, 1]
+        front, back = picked_ref[n, 0, :groups], picked_ref[n, 1, :groups]
         front = front + pltpu.roll(front, 64, 1)
         back = back + pltpu.roll(back, 64, 1)
         out_ref[n] = jnp.where(lane < 64, front, back)
@@ -175,7 +178,7 @@
 
 
 def unpack(listings, at_ref, value_ref):
-    groups = at_ref.shape[2]
+    groups = listings[0].shape[0] // 2
     lane = lax.broadcasted_iota(jnp.int32, (groups, 128), 1)
     offsets = [listing[groups:] for listing in listings]
     for r in range(len(listings)):
@@ -184,12 +187,13 @@
             total = total + jnp.where(offsets[s] == offsets[r], listings[s][:groups], 0.0)
         values = duplicate(total)
         for h, offset in enumerate(duplicate(offsets[r])):
-            value_ref[r, h] = values[h]
-            at_ref[r, h] = jnp.where(lane < 64, offset, offset - 64.0)
+            value_ref[r, h, :groups] = values[h]
+            at_ref[r, h, :groups] = jnp.where(lane < 64, offset, offset - 64.0)
 
 
 def decode(at_ref, value_ref, sparse_ref, second_ref, back_ref, tall_ref, ready, emit):
-    lists, _, groups, _ = at_ref.shape
+    lists = at_ref.shape[0]
+    groups = 2 * sparse_ref.shape[0]
     level = lax.broadcasted_iota(jnp.int32, (64, 128), 0).astype(jnp.float32)
 
     def scatter(t, carry):
@@ -348,10 +352,11 @@
         in_specs=[whole] * 5,
         out_specs=whole,
         scratch_shapes=[
-            VMEM((2, groups // 2, 128), jnp.int32),
-            VMEM((2, groups, 128), f32),
+            VMEM((2, groups // 2 + SPARE, 128), jnp.int32),
+            VMEM((2, groups + SPARE, 128), f32),
+            VMEM((groups + SPARE, 128), f32),
             VMEM((groups, 256, 256), bf16),
-            VMEM((2, 2, groups, 128), f32),
+            VMEM((2, 2, groups + SPARE, 128), f32),
         ],
         compiler_params=params,
         cost_estimate=pl.CostEstimate(
@@ -381,8 +386,8 @@
 
     def work(lists):
         return [
-            VMEM((lists, 2, groups, 128), f32),
-            VMEM((lists, 2, groups, 128), f32),
+            VMEM((lists, 2, groups + SPARE, 128), f32),
+            VMEM((lists, 2, groups + SPARE, 128), f32),
             VMEM((groups // 2, 256, 256), bf16),
             VMEM((groups // 2, 256, 256), bf16),
             VMEM((rows, cols), bf16),

time: 42.7 us -> 42.7 us (level)
  no operation moved by 1% of the time
where the time goes in v9:
time: 42.7 us; the launch traced here: 42.4 us
  starting transfers between devices  23.6 us (55%)
  Pallas kernels  11.3 us (26%)
  blocking collectives  4.54 us (11%)
  waiting for transfers between devices  2.35 us (6%)
  between operations  0.66 us (2%)
    all_to_all x1, starting transfers between devices, body(): lax.all_to_all(send, 'rep', 0, 0, tiled=True, axis_index_groups=chip_grou...  12.1 us
    all_to_all x1, starting transfers between devices, body(): lax.all_to_all(squares, ('rep', 'fsdp'), 0, 0, tiled=True, axis_index_gro...  11.5 us
    all_gather x1, blocking collectives, body(): lax.all_gather(every, 'rep', axis=0, tiled=True, axis_index_groups=cores)  4.54 us
    pallas_call x1, Pallas kernels, body(): pl.pallas_call(finish_kernel, out_shape=full, in_specs=[whole] + [hbm] *...  3.98 us
    pallas_call x1, Pallas kernels, body(): pl.pallas_call(own_kernel, out_shape=full, in_specs=[whole] * 4 + [hbm] *...  2.8 us
    pallas_call x1, Pallas kernels, body(): pl.pallas_call(fetch_kernel, out_shape=(jax.ShapeDtypeStruct((ring, 1, 12...  1.88 us
    all_to_all x1, waiting for transfers between devices, body(): lax.all_to_all(send, 'rep', 0, 0, tiled=True, axis_index_groups=chip_grou...  1.78 us
    pallas_call x1, Pallas kernels, body(): pl.pallas_call(pick_kernel, out_shape=jax.ShapeDtypeStruct((3, groups, 12...  1.78 us
  transfers between devices with their start and end apart: 2, of which 2 were waited for; matrix products, arithmetic and copies ran while one was open for 0% of the time, Pallas kernels for 11%

profile of v9, /device:TPU:1, one launch (start us, length us, event | category | flops | bytes accessed | tf_op | source)
XLA Modules:
  0.0 42.4 jit_solution(11229831972432235071)
XLA Ops:
  0.6 1.9 %fetch.1 = (f32[32,1,128]{2,1,0:T(1,128)}, bf16[128,3072]{1,0:T(8,128)(2,1)S(1)}, bf16[128,3072]{1,0:T(8,128)(2,1)S(1)}, s32[2,1536]{1,0:T(2,128)S(1)}, bf16[128...) custom-call(bf16[128,3072]{1,0:T(8,128)(2,1)} %bitcast.4, bf16[128,3072]{1,0:T(8,128)(2,1)} %bitcast.5, ...), custom_call_target="tpu_custom_call" | custom-call | tf_op jit(solution)/shard_map/fetch/pallas_call | solution.py:324
  2.5 11.5 %all-to-all-start = ((f32[32,1,128]{2,1,0:T(1,128)}), f32[32,1,128]{2,1,0:T(1,128)S(1)}, u32[]{:S(2)}, u32[]{:S(2)}) async-start(f32[32,1,128]{2,1,0:T(1,128)} %get-tuple-element.11), calls=%async_computation | async-start | bytes 32768 | tf_op jit(solution)/shard_map/all_to_all | solution.py:340
  14.1 1.8 %pick.1.picked_ref = f32[3,24,128]{2,1,0:T(8,128)S(1)} custom-call(s32[2,1536]{1,0:T(2,128)S(1)} %get-tuple-element.12.kept_ref, bf16[128,3072]{1,0:T(8,128)(2,1)S(1)} %get-tuple-element.13.grad_ref, bf16[128,3072]{1,0:T(8,128)(2,1)S(1)} %get-tuple-element.14.moment_ref, bf16[128,256]{1,0:T(8,128)(2,1)S(1)} %get-tuple-element.15.forth_ref, ...), custom_call_target="tpu_custom_call" | custom-call | flops 2013265920 | bytes 1572864 | tf_op jit(solution)/shard_map/pick/pallas_call | solution.py:349
  15.8 0.6 %all-to-all-done.squares_ref = f32[32,1,128]{2,1,0:T(1,128)S(1)} async-done(((f32[32,1,128]{2,1,0:T(1,128)}), f32[32,1,128]{2,1,0:T(1,128)S(1)}, u32[]{:S(2)}, u32[]{:S(2)}) %all-to-all-start) | async-done | bytes 16416 | tf_op jit(solution)/shard_map/all_to_all | solution.py:340
  16.4 0.8 %scale.1 = (f32[1,128]{1,0:T(1,128)S(1)}, f32[48,128]{1,0:T(8,128)S(1)}, f32[8,48,128]{2,1,0:T(8,128)}) custom-call(f32[32,1,128]{2,1,0:T(1,128)S(1)} %all-to-all-done.squares_ref, f32[3,24,128]{2,1,0:T(8,128)S(1)} %pick.1.picked_ref), custom_call_target="tpu_custom_call" | custom-call | tf_op jit(solution)/shard_map/scale/pallas_call | solution.py:368
  17.2 12.1 %all-to-all-start.1 = ((f32[8,48,128]{2,1,0:T(8,128)}), f32[8,48,128]{2,1,0:T(8,128)S(1)}, u32[]{:S(2)}, u32[]{:S(2)}) async-start(f32[8,48,128]{2,1,0:T(8,128)} %get-tuple-element.19), calls=%async_computation.1 | async-start | bytes 393216 | tf_op jit(solution)/shard_map/all_to_all | solution.py:381
  29.3 2.8 %own.1 = bf16[128,3072]{1,0:T(8,128)(2,1)} custom-call(f32[48,128]{1,0:T(8,128)S(1)} %get-tuple-element.17.own_ref, f32[1,128]{1,0:T(1,128)S(1)} %get-tuple-element.18.factor_ref, bf16[128,3072]{1,0:T(8,128)(2,1)S(1)} %get-tuple-element.13.grad_ref, bf16[128,3072]{1,0:T(8,128)(2,1)S(1)} %get-tuple-element.14.moment_ref, ...), custom_call_target="tpu_custom_call" | custom-call | flops 2013265920 | bytes 1572864 | tf_op jit(solution)/shard_map/own/pallas_call | solution.py:397
  32.1 1.8 %all-to-all-done.1 = f32[8,48,128]{2,1,0:T(8,128)S(1)} async-done(((f32[8,48,128]{2,1,0:T(8,128)}), f32[8,48,128]{2,1,0:T(8,128)S(1)}, u32[]{:S(2)}, u32[]{:S(2)}) %all-to-all-start.1) | async-done | bytes 196640 | tf_op jit(solution)/shard_map/all_to_all | solution.py:381
  33.9 4.5 %all_gather.3.all_ref = f32[16,48,128]{2,1,0:T(8,128)S(1)} all-gather(f32[8,48,128]{2,1,0:T(8,128)S(1)} %all-to-all-done.1), channel_id=1, replica_groups={{0,32},{64,96},{128,160},{192,224},{256,288},{320,352},{384,416},{448,4..., dimensions={0}, use_global_device_ids=true | all-gather | bytes 589824 | tf_op jit(solution)/shard_map/all_gather | solution.py:385
  38.4 4.0 %finish.1 = bf16[128,3072]{1,0:T(8,128)(2,1)} custom-call(f32[16,48,128]{2,1,0:T(8,128)S(1)} %all_gather.3.all_ref, bf16[256,256]{1,0:T(8,128)(2,1)} %constant.9.clone.back_hbm, bf16[256,256]{1,0:T(8,128)(2,1)} %constant.11.clone.tall_hbm, bf16[128,3072]{1,0:T(8,128)(2,1)} %weight_hbm.1), custom_call_target="tpu_custom_call" | custom-call | tf_op jit(solution)/shard_map/finish/pallas_call | solution.py:410
Async XLA Ops:
  2.5 13.9 %all-to-all-start = ((f32[32,1,128]{2,1,0:T(1,128)}), f32[32,1,128]{2,1,0:T(1,128)S(1)}, u32[]{:S(2)}, u32[]{:S(2)}) async-start(f32[32,1,128]{2,1,0:T(1,128)} %get-tuple-element.11), calls=%async_computation | async-start | bytes 32768 | tf_op jit(solution)/shard_map/all_to_all | solution.py:340
  17.2 16.7 %all-to-all-start.1 = ((f32[8,48,128]{2,1,0:T(8,128)}), f32[8,48,128]{2,1,0:T(8,128)S(1)}, u32[]{:S(2)}, u32[]{:S(2)}) async-start(f32[8,48,128]{2,1,0:T(8,128)} %get-tuple-element.19), calls=%async_computation.1 | async-start | bytes 393216 | tf_op jit(solution)/shard_map/all_to_all | solution.py:381

commit v10 on v9

--- a/solution.py
+++ b/solution.py
@@ -299,7 +299,7 @@
 def chip_groups(replicas):
     chips = replicas // 2
     return [
-        [(head - n) % chips * 2 + core for n in range(chips)] for core, head in enumerate((5, 6))
+        [(head - n) % chips * 2 + core for n in range(chips)] for core, head in enumerate((4, 6))
     ]
 
 

time: 42.7 us -> 42.7 us (level)
  no operation moved by 1% of the time
where the time goes in v10:
time: 42.7 us; the launch traced here: 42.4 us
  starting transfers between devices  23.6 us (55%)
  Pallas kernels  11.3 us (26%)
  blocking collectives  4.56 us (11%)
  waiting for transfers between devices  2.35 us (6%)
  between operations  0.66 us (2%)
    all_to_all x1, starting transfers between devices, body(): lax.all_to_all(send, 'rep', 0, 0, tiled=True, axis_index_groups=chip_grou...  12.1 us
    all_to_all x1, starting transfers between devices, body(): lax.all_to_all(squares, ('rep', 'fsdp'), 0, 0, tiled=True, axis_index_gro...  11.5 us
    all_gather x1, blocking collectives, body(): lax.all_gather(every, 'rep', axis=0, tiled=True, axis_index_groups=cores)  4.56 us
    pallas_call x1, Pallas kernels, body(): pl.pallas_call(finish_kernel, out_shape=full, in_specs=[whole] + [hbm] *...  3.98 us
    pallas_call x1, Pallas kernels, body(): pl.pallas_call(own_kernel, out_shape=full, in_specs=[whole] * 4 + [hbm] *...  2.8 us
    pallas_call x1, Pallas kernels, body(): pl.pallas_call(fetch_kernel, out_shape=(jax.ShapeDtypeStruct((ring, 1, 12...  1.88 us
    all_to_all x1, waiting for transfers between devices, body(): lax.all_to_all(send, 'rep', 0, 0, tiled=True, axis_index_groups=chip_grou...  1.78 us
    pallas_call x1, Pallas kernels, body(): pl.pallas_call(pick_kernel, out_shape=jax.ShapeDtypeStruct((3, groups, 12...  1.78 us
  transfers between devices with their start and end apart: 2, of which 2 were waited for; matrix products, arithmetic and copies ran while one was open for 0% of the time, Pallas kernels for 11%

profile of v10, /device:TPU:1, one launch (start us, length us, event | category | flops | bytes accessed | tf_op | source)
XLA Modules:
  0.0 42.4 jit_solution(13095650559390100663)
XLA Ops:
  0.6 1.9 %fetch.1 = (f32[32,1,128]{2,1,0:T(1,128)}, bf16[128,3072]{1,0:T(8,128)(2,1)S(1)}, bf16[128,3072]{1,0:T(8,128)(2,1)S(1)}, s32[2,1536]{1,0:T(2,128)S(1)}, bf16[128...) custom-call(bf16[128,3072]{1,0:T(8,128)(2,1)} %bitcast.4, bf16[128,3072]{1,0:T(8,128)(2,1)} %bitcast.5, ...), custom_call_target="tpu_custom_call" | custom-call | tf_op jit(solution)/shard_map/fetch/pallas_call | solution.py:324
  2.5 11.5 %all-to-all-start = ((f32[32,1,128]{2,1,0:T(1,128)}), f32[32,1,128]{2,1,0:T(1,128)S(1)}, u32[]{:S(2)}, u32[]{:S(2)}) async-start(f32[32,1,128]{2,1,0:T(1,128)} %get-tuple-element.11), calls=%async_computation | async-start | bytes 32768 | tf_op jit(solution)/shard_map/all_to_all | solution.py:340
  14.1 1.8 %pick.1.picked_ref = f32[3,24,128]{2,1,0:T(8,128)S(1)} custom-call(s32[2,1536]{1,0:T(2,128)S(1)} %get-tuple-element.12.kept_ref, bf16[128,3072]{1,0:T(8,128)(2,1)S(1)} %get-tuple-element.13.grad_ref, bf16[128,3072]{1,0:T(8,128)(2,1)S(1)} %get-tuple-element.14.moment_ref, bf16[128,256]{1,0:T(8,128)(2,1)S(1)} %get-tuple-element.15.forth_ref, ...), custom_call_target="tpu_custom_call" | custom-call | flops 2013265920 | bytes 1572864 | tf_op jit(solution)/shard_map/pick/pallas_call | solution.py:349
  15.8 0.6 %all-to-all-done.squares_ref = f32[32,1,128]{2,1,0:T(1,128)S(1)} async-done(((f32[32,1,128]{2,1,0:T(1,128)}), f32[32,1,128]{2,1,0:T(1,128)S(1)}, u32[]{:S(2)}, u32[]{:S(2)}) %all-to-all-start) | async-done | bytes 16416 | tf_op jit(solution)/shard_map/all_to_all | solution.py:340
  16.4 0.8 %scale.1 = (f32[1,128]{1,0:T(1,128)S(1)}, f32[48,128]{1,0:T(8,128)S(1)}, f32[8,48,128]{2,1,0:T(8,128)}) custom-call(f32[32,1,128]{2,1,0:T(1,128)S(1)} %all-to-all-done.squares_ref, f32[3,24,128]{2,1,0:T(8,128)S(1)} %pick.1.picked_ref), custom_call_target="tpu_custom_call" | custom-call | tf_op jit(solution)/shard_map/scale/pallas_call | solution.py:368
  17.2 12.1 %all-to-all-start.1 = ((f32[8,48,128]{2,1,0:T(8,128)}), f32[8,48,128]{2,1,0:T(8,128)S(1)}, u32[]{:S(2)}, u32[]{:S(2)}) async-start(f32[8,48,128]{2,1,0:T(8,128)} %get-tuple-element.19), calls=%async_computation.1 | async-start | bytes 393216 | tf_op jit(solution)/shard_map/all_to_all | solution.py:381
  29.3 2.8 %own.1 = bf16[128,3072]{1,0:T(8,128)(2,1)} custom-call(f32[48,128]{1,0:T(8,128)S(1)} %get-tuple-element.17.own_ref, f32[1,128]{1,0:T(1,128)S(1)} %get-tuple-element.18.factor_ref, bf16[128,3072]{1,0:T(8,128)(2,1)S(1)} %get-tuple-element.13.grad_ref, bf16[128,3072]{1,0:T(8,128)(2,1)S(1)} %get-tuple-element.14.moment_ref, ...), custom_call_target="tpu_custom_call" | custom-call | flops 2013265920 | bytes 1572864 | tf_op jit(solution)/shard_map/own/pallas_call | solution.py:397
  32.1 1.8 %all-to-all-done.1 = f32[8,48,128]{2,1,0:T(8,128)S(1)} async-done(((f32[8,48,128]{2,1,0:T(8,128)}), f32[8,48,128]{2,1,0:T(8,128)S(1)}, u32[]{:S(2)}, u32[]{:S(2)}) %all-to-all-start.1) | async-done | bytes 196640 | tf_op jit(solution)/shard_map/all_to_all | solution.py:381
  33.9 4.6 %all_gather.3.all_ref = f32[16,48,128]{2,1,0:T(8,128)S(1)} all-gather(f32[8,48,128]{2,1,0:T(8,128)S(1)} %all-to-all-done.1), channel_id=1, replica_groups={{0,32},{64,96},{128,160},{192,224},{256,288},{320,352},{384,416},{448,4..., dimensions={0}, use_global_device_ids=true | all-gather | bytes 589824 | tf_op jit(solution)/shard_map/all_gather | solution.py:385
  38.5 4.0 %finish.1 = bf16[128,3072]{1,0:T(8,128)(2,1)} custom-call(f32[16,48,128]{2,1,0:T(8,128)S(1)} %all_gather.3.all_ref, bf16[256,256]{1,0:T(8,128)(2,1)} %constant.9.clone.back_hbm, bf16[256,256]{1,0:T(8,128)(2,1)} %constant.11.clone.tall_hbm, bf16[128,3072]{1,0:T(8,128)(2,1)} %weight_hbm.1), custom_call_target="tpu_custom_call" | custom-call | tf_op jit(solution)/shard_map/finish/pallas_call | solution.py:410
Async XLA Ops:
  2.5 13.9 %all-to-all-start = ((f32[32,1,128]{2,1,0:T(1,128)}), f32[32,1,128]{2,1,0:T(1,128)S(1)}, u32[]{:S(2)}, u32[]{:S(2)}) async-start(f32[32,1,128]{2,1,0:T(1,128)} %get-tuple-element.11), calls=%async_computation | async-start | bytes 32768 | tf_op jit(solution)/shard_map/all_to_all | solution.py:340
  17.2 16.7 %all-to-all-start.1 = ((f32[8,48,128]{2,1,0:T(8,128)}), f32[8,48,128]{2,1,0:T(8,128)S(1)}, u32[]{:S(2)}, u32[]{:S(2)}) async-start(f32[8,48,128]{2,1,0:T(8,128)} %get-tuple-element.19), calls=%async_computation.1 | async-start | bytes 393216 | tf_op jit(solution)/shard_map/all_to_all | solution.py:381

commit v11 on v9

--- a/solution.py
+++ b/solution.py
@@ -209,7 +209,7 @@
                 sparse_ref[t, at, 128:] = low
         return carry
 
-    lax.fori_loop(0, groups // 2, scatter, 0, unroll=3 if groups % 6 == 0 else 1)
+    lax.fori_loop(0, groups // 2, scatter, 0, unroll=4 if groups % 8 == 0 else 1)
     for copy in ready:
         copy.wait()
     for t in range(groups // 2):

time: 42.7 us -> 42.7 us (level)
  no operation moved by 1% of the time
where the time goes in v11:
time: 42.7 us; the launch traced here: 42.4 us
  starting transfers between devices  23.6 us (55%)
  Pallas kernels  11.2 us (26%)
  blocking collectives  4.54 us (11%)
  waiting for transfers between devices  2.35 us (6%)
  between operations  0.66 us (2%)
    all_to_all x1, starting transfers between devices, body(): lax.all_to_all(send, 'rep', 0, 0, tiled=True, axis_index_groups=chip_grou...  12.1 us
    all_to_all x1, starting transfers between devices, body(): lax.all_to_all(squares, ('rep', 'fsdp'), 0, 0, tiled=True, axis_index_gro...  11.5 us
    all_gather x1, blocking collectives, body(): lax.all_gather(every, 'rep', axis=0, tiled=True, axis_index_groups=cores)  4.54 us
    pallas_call x1, Pallas kernels, body(): pl.pallas_call(finish_kernel, out_shape=full, in_specs=[whole] + [hbm] *...  3.96 us
    pallas_call x1, Pallas kernels, body(): pl.pallas_call(own_kernel, out_shape=full, in_specs=[whole] * 4 + [hbm] *...  2.8 us
    pallas_call x1, Pallas kernels, body(): pl.pallas_call(fetch_kernel, out_shape=(jax.ShapeDtypeStruct((ring, 1, 12...  1.88 us
    all_to_all x1, waiting for transfers between devices, body(): lax.all_to_all(send, 'rep', 0, 0, tiled=True, axis_index_groups=chip_grou...  1.78 us
    pallas_call x1, Pallas kernels, body(): pl.pallas_call(pick_kernel, out_shape=jax.ShapeDtypeStruct((3, groups, 12...  1.78 us
  transfers between devices with their start and end apart: 2, of which 2 were waited for; matrix products, arithmetic and copies ran while one was open for 0% of the time, Pallas kernels for 11%

profile of v11, /device:TPU:1, one launch (start us, length us, event | category | flops | bytes accessed | tf_op | source)
XLA Modules:
  0.0 42.4 jit_solution(2328896425647736648)
XLA Ops:
  0.6 1.9 %fetch.1 = (f32[32,1,128]{2,1,0:T(1,128)}, bf16[128,3072]{1,0:T(8,128)(2,1)S(1)}, bf16[128,3072]{1,0:T(8,128)(2,1)S(1)}, s32[2,1536]{1,0:T(2,128)S(1)}, bf16[128...) custom-call(bf16[128,3072]{1,0:T(8,128)(2,1)} %bitcast.4, bf16[128,3072]{1,0:T(8,128)(2,1)} %bitcast.5, ...), custom_call_target="tpu_custom_call" | custom-call | tf_op jit(solution)/shard_map/fetch/pallas_call | solution.py:324
  2.5 11.5 %all-to-all-start = ((f32[32,1,128]{2,1,0:T(1,128)}), f32[32,1,128]{2,1,0:T(1,128)S(1)}, u32[]{:S(2)}, u32[]{:S(2)}) async-start(f32[32,1,128]{2,1,0:T(1,128)} %get-tuple-element.11), calls=%async_computation | async-start | bytes 32768 | tf_op jit(solution)/shard_map/all_to_all | solution.py:340
  14.1 1.8 %pick.1.picked_ref = f32[3,24,128]{2,1,0:T(8,128)S(1)} custom-call(s32[2,1536]{1,0:T(2,128)S(1)} %get-tuple-element.12.kept_ref, bf16[128,3072]{1,0:T(8,128)(2,1)S(1)} %get-tuple-element.13.grad_ref, bf16[128,3072]{1,0:T(8,128)(2,1)S(1)} %get-tuple-element.14.moment_ref, bf16[128,256]{1,0:T(8,128)(2,1)S(1)} %get-tuple-element.15.forth_ref, ...), custom_call_target="tpu_custom_call" | custom-call | flops 2013265920 | bytes 1572864 | tf_op jit(solution)/shard_map/pick/pallas_call | solution.py:349
  15.8 0.6 %all-to-all-done.squares_ref = f32[32,1,128]{2,1,0:T(1,128)S(1)} async-done(((f32[32,1,128]{2,1,0:T(1,128)}), f32[32,1,128]{2,1,0:T(1,128)S(1)}, u32[]{:S(2)}, u32[]{:S(2)}) %all-to-all-start) | async-done | bytes 16416 | tf_op jit(solution)/shard_map/all_to_all | solution.py:340
  16.4 0.8 %scale.1 = (f32[1,128]{1,0:T(1,128)S(1)}, f32[48,128]{1,0:T(8,128)S(1)}, f32[8,48,128]{2,1,0:T(8,128)}) custom-call(f32[32,1,128]{2,1,0:T(1,128)S(1)} %all-to-all-done.squares_ref, f32[3,24,128]{2,1,0:T(8,128)S(1)} %pick.1.picked_ref), custom_call_target="tpu_custom_call" | custom-call | tf_op jit(solution)/shard_map/scale/pallas_call | solution.py:368
  17.2 12.1 %all-to-all-start.1 = ((f32[8,48,128]{2,1,0:T(8,128)}), f32[8,48,128]{2,1,0:T(8,128)S(1)}, u32[]{:S(2)}, u32[]{:S(2)}) async-start(f32[8,48,128]{2,1,0:T(8,128)} %get-tuple-element.19), calls=%async_computation.1 | async-start | bytes 393216 | tf_op jit(solution)/shard_map/all_to_all | solution.py:381
  29.3 2.8 %own.1 = bf16[128,3072]{1,0:T(8,128)(2,1)} custom-call(f32[48,128]{1,0:T(8,128)S(1)} %get-tuple-element.17.own_ref, f32[1,128]{1,0:T(1,128)S(1)} %get-tuple-element.18.factor_ref, bf16[128,3072]{1,0:T(8,128)(2,1)S(1)} %get-tuple-element.13.grad_ref, bf16[128,3072]{1,0:T(8,128)(2,1)S(1)} %get-tuple-element.14.moment_ref, ...), custom_call_target="tpu_custom_call" | custom-call | flops 2013265920 | bytes 1572864 | tf_op jit(solution)/shard_map/own/pallas_call | solution.py:397
  32.1 1.8 %all-to-all-done.1 = f32[8,48,128]{2,1,0:T(8,128)S(1)} async-done(((f32[8,48,128]{2,1,0:T(8,128)}), f32[8,48,128]{2,1,0:T(8,128)S(1)}, u32[]{:S(2)}, u32[]{:S(2)}) %all-to-all-start.1) | async-done | bytes 196640 | tf_op jit(solution)/shard_map/all_to_all | solution.py:381
  33.9 4.5 %all_gather.3.all_ref = f32[16,48,128]{2,1,0:T(8,128)S(1)} all-gather(f32[8,48,128]{2,1,0:T(8,128)S(1)} %all-to-all-done.1), channel_id=1, replica_groups={{0,32},{64,96},{128,160},{192,224},{256,288},{320,352},{384,416},{448,4..., dimensions={0}, use_global_device_ids=true | all-gather | bytes 589824 | tf_op jit(solution)/shard_map/all_gather | solution.py:385
  38.4 4.0 %finish.1 = bf16[128,3072]{1,0:T(8,128)(2,1)} custom-call(f32[16,48,128]{2,1,0:T(8,128)S(1)} %all_gather.3.all_ref, bf16[256,256]{1,0:T(8,128)(2,1)} %constant.9.clone.back_hbm, bf16[256,256]{1,0:T(8,128)(2,1)} %constant.11.clone.tall_hbm, bf16[128,3072]{1,0:T(8,128)(2,1)} %weight_hbm.1), custom_call_target="tpu_custom_call" | custom-call | tf_op jit(solution)/shard_map/finish/pallas_call | solution.py:410
Async XLA Ops:
  2.5 13.9 %all-to-all-start = ((f32[32,1,128]{2,1,0:T(1,128)}), f32[32,1,128]{2,1,0:T(1,128)S(1)}, u32[]{:S(2)}, u32[]{:S(2)}) async-start(f32[32,1,128]{2,1,0:T(1,128)} %get-tuple-element.11), calls=%async_computation | async-start | bytes 32768 | tf_op jit(solution)/shard_map/all_to_all | solution.py:340
  17.2 16.7 %all-to-all-start.1 = ((f32[8,48,128]{2,1,0:T(8,128)}), f32[8,48,128]{2,1,0:T(8,128)S(1)}, u32[]{:S(2)}, u32[]{:S(2)}) async-start(f32[8,48,128]{2,1,0:T(8,128)} %get-tuple-element.19), calls=%async_computation.1 | async-start | bytes 393216 | tf_op jit(solution)/shard_map/all_to_all | solution.py:381
